TPU v7x, 32 devices: a whole 2x2x4 slice. The times are simulated.
32 devices in a mesh: batch: 8 (over y, x, core), blk: 4 (over z).
Axes of the slice: x: 2, y: 2, z: 4, core: 2. Of those that a mesh axis runs over, the one named last changes fastest.
Arguments:
- decoder_input: bfloat16 [16, 1024, 512], P('batch', 'blk'), may hold values from -6 to 6
- encoder_output: bfloat16 [16, 1024, 512], P('batch', 'blk'), may hold values from -6 to 6
- sequence_lengths: int32 [16], P('batch'), may hold values from 256 to 1024, as said below
- chain_breaks: int32 [16, 4], P('batch'), may hold values from 1 to 1022, as said below
- self_inward: bfloat16 [512, 1536], replicated, may hold values from -0.25 to 0.25
- self_outward: bfloat16 [512, 512], replicated, may hold values from -2 to 2
- cross_query: bfloat16 [512, 512], replicated, may hold values from -0.25 to 0.25
- cross_memory: bfloat16 [512, 1024], replicated, may hold values from -0.25 to 0.25
- cross_outward: bfloat16 [512, 512], replicated, may hold values from -4 to 4
- feed_up: bfloat16 [512, 2048], replicated, may hold values from -0.25 to 0.25
- feed_up_bias: bfloat16 [2048], replicated, may hold values from -4 to 4
- feed_down: bfloat16 [2048, 512], replicated, may hold values from -0.125 to 0.125
- feed_down_bias: bfloat16 [512], replicated, may hold values from -4 to 4
- norm_gains: float32 [3, 512], replicated, may hold values from 0.5 to 1.5
- norm_shifts: float32 [3, 512], replicated, may hold values from -3 to 3
- output_cotangent: bfloat16 [16, 1024, 512], P('batch', 'blk'), may hold values from -6 to 6
Outputs:
- layer_output: bfloat16 [16, 1024, 512], P('batch', 'blk')
- input_gradient: float32 [16, 1024, 512], P('batch', 'blk')
- encoder_gradient: float32 [16, 1024, 512], P('batch', 'blk')
- self_inward_gradient: float32 [512, 1536], replicated
- self_outward_gradient: float32 [512, 512], replicated
- cross_query_gradient: float32 [512, 512], replicated
- cross_memory_gradient: float32 [512, 1024], replicated
- cross_outward_gradient: float32 [512, 512], replicated
- feed_up_gradient: float32 [512, 2048], replicated
- feed_up_bias_gradient: float32 [2048], replicated
- feed_down_gradient: float32 [2048, 512], replicated
- feed_down_bias_gradient: float32 [512], replicated
- norm_gains_gradient: float32 [3, 512], replicated
- norm_shifts_gradient: float32 [3, 512], replicated
Inputs may be any that keep to these rules, and one draw needn't show every extreme that they name: `sequence_lengths`: in each group of 2 sequences that share an index of batch, one has length 1024; the others have a quarter of 1024 or more, and one of them exactly that. `chain_breaks`: each position lies from 1 to its sequence's length minus 2; positions may repeat.
All inputs are finite; a program needn't handle non-finite values.
Results may differ from a plain program's by a relative error of at most 0.019.
Values may be sent and summed in bfloat16 or wider, within the bound.
No kernel may reach another device: no remote copies, remote signals or barrier semaphores. Data moves between devices by JAX's collectives and lax.ppermute only.
A program may use at most 384 MiB of HBM per device.

v0:
```python
import functools

import jax
import jax.numpy as jnp
from jax import lax
from jax.experimental import pallas as pl
from jax.experimental.pallas import tpu as pltpu
from jax.sharding import PartitionSpec as P

HEAD = 64
PAIR = 2 * HEAD
EPSILON = 1e-05
FAR = 1e30
LOW = jnp.bfloat16
WIDE = jnp.float32


def contract(left, right, a, b):
    return lax.dot_general(left, right, (((a,), (b,)), ((), ())), preferred_element_type=WIDE)


def nn(left, right):
    return contract(left, right, 1, 0)


def nt(left, right):
    return contract(left, right, 1, 1)


def tn(left, right):
    return contract(left, right, 0, 0)


def standard(values):
    center = values - jnp.mean(values, axis=-1, keepdims=True)
    spread = jnp.mean(center * center, axis=-1, keepdims=True)
    inverse = lax.rsqrt(spread + EPSILON)
    return center * inverse, inverse


def norm_back(values, gain, upstream):
    unit, inverse = standard(values)
    m = upstream * gain
    grad = inverse * (
        m
        - jnp.mean(m, axis=-1, keepdims=True)
        - unit * jnp.mean(m * unit, axis=-1, keepdims=True)
    )
    return grad, jnp.sum(upstream * unit, axis=0), jnp.sum(upstream, axis=0)


def gelu_pair(x):
    z = jnp.abs(x) * 0.7071067811865476
    t = 1.0 / (1.0 + 0.5 * z)
    poly = 0.17087277
    for c in (
        -0.82215223,
        1.48851587,
        -1.13520398,
        0.27886807,
        -0.18628806,
        0.09678418,
        0.37409196,
        1.00002368,
        -1.26551223,
    ):
        poly = poly * t + c
    bell = jnp.exp(-z * z)
    tail = 0.5 * t * jnp.exp(poly) * bell
    share = jnp.where(x >= 0, 1.0 - tail, tail)
    return x * share, share + x * bell * 0.3989422804014327


def by_head(pair_rows):
    lane = lax.broadcasted_iota(jnp.int32, pair_rows.shape, 1)
    zero = jnp.zeros_like(pair_rows)
    return jnp.concatenate(
        [jnp.where(lane < HEAD, pair_rows, zero), jnp.where(lane >= HEAD, pair_rows, zero)], axis=0
    )


def own_parts(both):
    rows = both.shape[1] // 2
    return jnp.concatenate([both[:HEAD, :rows], both[HEAD:, rows:]], axis=0)


def columns(place, wide):
    return pl.ds(pl.multiple_of(place * wide, wide), wide)


def attend(q_ref, kv_ref, p_ref, low_ref, inverse_ref, plan, mask, done):
    rows = q_ref.shape[0] // 2
    width = q_ref.shape[1]

    @pl.loop(0, width // PAIR)
    def _(pair):
        lanes = columns(pair, PAIR)
        values = columns(width // PAIR + pair, PAIR)
        spot = columns(pair, 2 * rows)
        for seq, blocks in enumerate(plan):
            mine = slice(seq * rows, (seq + 1) * rows)
            queries = by_head(q_ref[mine, lanes])
            scores, tops = [], []
            for block in blocks:
                s = nt(kv_ref[block * rows : (block + 1) * rows, lanes], queries)
                s, far = mask(block, s)
                scores.append((s, far))
                tops.append(jnp.max(s, axis=0, keepdims=True) - far)
            top = functools.reduce(jnp.maximum, tops)
            total = jnp.zeros_like(top)
            mixed = jnp.zeros((PAIR, 2 * rows), WIDE)
            for block, (s, far) in zip(blocks, scores):
                at = slice(block * rows, (block + 1) * rows)
                p = jnp.exp(s - (top + far))
                total = total + jnp.sum(p, axis=0, keepdims=True)
                p = p.astype(LOW)
                p_ref[at, spot] = p
                mixed = mixed + tn(kv_ref[at, values], p)
            inverse = 1.0 / total
            low_ref[mine, lanes] = own_parts(mixed * inverse).T.astype(LOW)
            inverse_ref[pl.ds(2 * pair + seq, 1), :] = inverse
        done(pair)


def attend_back(up, low_ref, inverse_ref, q_ref, kv_ref, p_ref, dq_ref, dkv_ref, plan, ready, done):
    rows = q_ref.shape[0] // 2
    width = q_ref.shape[1]
    scale = HEAD ** (-0.5)

    @pl.loop(0, width // PAIR)
    def _(pair):
        lanes = columns(pair, PAIR)
        values = columns(width // PAIR + pair, PAIR)
        slot = lax.rem(pair, 2)
        ready(pair)
        for seq, blocks in enumerate(plan):
            mine = slice(seq * rows, (seq + 1) * rows)
            queries = by_head(q_ref[mine, lanes])
            inverse = inverse_ref[pl.ds(2 * pair + seq, 1), :]
            scaled = up[mine, lanes].astype(WIDE) * own_parts(jnp.broadcast_to(inverse, (PAIR, 2 * rows))).T
            inner = (scaled * low_ref[mine, lanes].astype(WIDE)).T
            offset = jnp.concatenate(
                [
                    jnp.sum(inner[:HEAD], axis=0, keepdims=True),
                    jnp.sum(inner[HEAD:], axis=0, keepdims=True),
                ],
                axis=1,
            )
            upper = by_head(scaled.astype(LOW))
            dq = jnp.zeros((PAIR, 2 * rows), WIDE)
            for block in blocks:
                at = slice(block * rows, (block + 1) * rows)
                p = p_ref[slot, at, :]
                dp = nt(kv_ref[at, values], upper)
                ds = (p.astype(WIDE) * (dp - offset)).astype(LOW)
                dkv_ref[at, values] = nn(p, upper).astype(LOW)
                dkv_ref[at, lanes] = nn(ds, queries).astype(LOW)
                dq = dq + tn(kv_ref[at, lanes], ds)
            dq_ref[mine, lanes] = (own_parts(dq).T * scale).astype(LOW)
        done(pair)


def columns_copy(source, target, sem, place, wide):
    at = columns(place, wide)
    return pltpu.make_async_copy(source.at[:, at], target.at[:, at], sem)


def plan_of(n):
    return (tuple(range(n)), tuple(range(n, n + n // 4)))


def add_terms(out, refs, terms):
    for j in range(out.shape[0]):
        total = refs[j * terms][...]
        for ref in refs[j * terms + 1 : (j + 1) * terms]:
            total = total + ref[...]
        out[j] = total


def self_kernel(n, terms, order, rank, x, *refs):
    xl, refs = refs[: n - 1], refs[n - 1 :]
    shorts, refs = refs[: terms * (n // 4)], refs[terms * (n // 4) :]
    (
        w_in, w_out, w_cq, gains, shifts,
        q, kv_far, p_far, mixed, inverse, after, cq, n1, xs, kv, p, sems,
    ) = refs
    pairs = q.shape[1] // PAIR
    kv_save = pltpu.make_async_copy(kv, kv_far, sems.at[pairs])

    def p_save(pair):
        return columns_copy(p, p_far, sems.at[pair], pair, p.shape[1] // pairs)
    add_terms(xs, shorts, terms)
    rows, width = x.shape[1:]
    r = rank[0]

    def first_norm(v):
        return (standard(v.astype(WIDE))[0] * gains[0:1] + shifts[0:1]).astype(LOW)

    def keys(v, block):
        kv[block * rows : (block + 1) * rows, :] = nn(first_norm(v), w_in[:, width:]).astype(LOW)

    mine = jnp.concatenate([x[order[0]], x[order[1]]], axis=0)
    normed = first_norm(mine)
    kv[0:rows, :] = nn(normed[:rows], w_in[:, width:]).astype(LOW)
    for d in range(1, n):
        keys(xl[d - 1][...], d)
    for j in range(n // 4):
        keys(xs[j], n + j)
    kv_save.start()
    q[...] = nn(normed, w_in[:, :width]).astype(LOW) * HEAD ** (-0.5)

    def mask(block, s):
        if 0 < block < n:
            return s, jnp.where(r >= block, 0.0, FAR)
        key = lax.broadcasted_iota(jnp.int32, s.shape, 0)
        query = lax.broadcasted_iota(jnp.int32, s.shape, 1)
        query = jnp.where(query >= rows, query - rows, query)
        if block >= n:
            query = query + (r - (block - n)) * rows
        return jnp.where(key <= query, s, -FAR), 0.0

    attend(q, kv, p, mixed, inverse, plan_of(n), mask, lambda pair: p_save(pair).start())
    total = mine.astype(WIDE) + nn(mixed[...], w_out[...])
    after[...] = total
    second = (standard(total)[0] * gains[1:2] + shifts[1:2]).astype(LOW)
    n1[...] = second
    cq[...] = nn(second, w_cq[...]).astype(LOW) * HEAD ** (-0.5)
    kv_save.wait()
    for pair in range(pairs):
        p_save(pair).wait()


def cross_kernel(n, terms, order, rank, breaks, enc, *refs):
    el, refs = refs[: n - 1], refs[n - 1 :]
    shorts, refs = refs[: terms * (n // 4)], refs[terms * (n // 4) :]
    cq, after, w_cm, w_out, kv_far, p_far, mixed, inverse, crossed, es, kv, p, sems = refs
    pairs = cq.shape[1] // PAIR
    kv_save = pltpu.make_async_copy(kv, kv_far, sems.at[pairs])

    def p_save(pair):
        return columns_copy(p, p_far, sems.at[pair], pair, p.shape[1] // pairs)
    add_terms(es, shorts, terms)
    rows, width = enc.shape[1:]
    r = rank[0]
    kv[0:rows, :] = nn(enc[order[0]], w_cm[...]).astype(LOW)
    for d in range(1, n):
        kv[d * rows : (d + 1) * rows, :] = nn(el[d - 1][...], w_cm[...]).astype(LOW)
    for j in range(n // 4):
        kv[(n + j) * rows : (n + j + 1) * rows, :] = nn(es[j], w_cm[...]).astype(LOW)

    kv_save.start()

    def mask(block, s):
        key = lax.broadcasted_iota(jnp.int32, s.shape, 0)
        if block < n:
            first = lax.rem(r - block + n, n) * rows
            which = order[0]
        else:
            first = (block - n) * rows
            which = order[1]
        shut = key == breaks[which, 0] - first
        for i in range(1, breaks.shape[1]):
            shut = shut | (key == breaks[which, i] - first)
        return jnp.where(shut, -FAR, s), 0.0

    attend(cq, kv, p, mixed, inverse, plan_of(n), mask, lambda pair: p_save(pair).start())
    crossed[...] = after[...] + nn(mixed[...], w_out[...])
    kv_save.wait()
    for pair in range(pairs):
        p_save(pair).wait()


def spread(sums, code, value, lane):
    tall = sums.shape[1]
    for k in range(sums.shape[0]):
        part = value[k * tall : (k + 1) * tall, :]
        sums[k ^ code, :, lane : lane + value.shape[1]] = part


def feed_kernel(
    order, codes, crossed, cot, w_up, b_up, w_down, b_down, gains, shifts,
    out, grad, near, far, g_bias, g_small, third, total, back, sums, sems,
):
    rows, width = cot.shape[1:]
    hidden = w_up.shape[1]
    half, tall = near.shape[:2]
    deep = hidden // (2 * half)
    third[...] = (standard(crossed[...])[0] * gains[2:3] + shifts[2:3]).astype(LOW)
    up_low = jnp.concatenate([cot[order[0]], cot[order[1]]], axis=0)
    total[...] = crossed[...] + b_down[...].astype(WIDE)
    back[...] = jnp.zeros_like(back)

    @pl.loop(0, hidden // width)
    def _(c):
        at = columns(c, width)
        rising = nn(third[...], w_up[:, at]) + b_up[:, at].astype(WIDE)
        active, slope = gelu_pair(rising)
        active = active.astype(LOW)
        total[...] += nn(active, w_down[at, :])
        rising_grad = nt(up_low, w_down[at, :]) * slope
        g_bias[:, at] = jnp.sum(rising_grad, axis=0, keepdims=True)
        rising_grad = rising_grad.astype(LOW)
        back[...] += nt(rising_grad, w_up[:, at])
        g_up = tn(third[...], rising_grad).astype(LOW)
        for k in range(2 * half):
            sums[k ^ codes[0], :, at] = g_up[k * tall : (k + 1) * tall]
        g_down = tn(active, up_low).astype(LOW)
        for k in range(width // deep):
            for i in range(deep // tall):
                first = k * deep + i * tall
                lanes = slice(hidden + i * width, hidden + (i + 1) * width)
                sums[(c * (width // deep) + k) ^ codes[1], :, lanes] = g_down[first : first + tall]

    saves = [
        pltpu.make_async_copy(sums.at[:half], near, sems.at[0]),
        pltpu.make_async_copy(sums.at[half:], far, sems.at[1]),
    ]
    for save in saves:
        save.start()
    low = total[...].astype(LOW)
    out[order[0]] = low[:rows]
    out[order[1]] = low[rows:]
    upward = up_low.astype(WIDE)
    inner, gain, shift = norm_back(crossed[...], gains[2:3], back[...])
    grad[...] = upward + inner
    g_small[0, :] = jnp.sum(upward, axis=0)
    g_small[1, :] = gain
    g_small[2, :] = shift
    for save in saves:
        save.wait()


def loads(kv_far, p_far, kv, p, sems):
    pairs = kv.shape[1] // (2 * PAIR)

    def p_copy(pair):
        at = columns(pair, p.shape[2])
        return pltpu.make_async_copy(p_far.at[:, at], p.at[lax.rem(pair, 2)], sems.at[pair])

    def kv_copies(pair):
        return (
            columns_copy(kv_far, kv, sems.at[pairs + pair], pair, PAIR),
            columns_copy(kv_far, kv, sems.at[2 * pairs + pair], pairs + pair, PAIR),
        )

    for pair in range(pairs):
        if pair < 2:
            p_copy(pair).start()
        for copy in kv_copies(pair):
            copy.start()

    def ready(pair):
        for copy in (p_copy(pair), *kv_copies(pair)):
            copy.wait()

    def done(pair):
        @pl.when(pair + 2 < pairs)
        def _():
            p_copy(pair + 2).start()

    return ready, done


def put_part(parts, n, b, value):
    rows = value.shape[0]
    if b < len(parts):
        parts[b][:rows, :] = value
    else:
        parts[1][(b - n + 1) * rows : (b - n + 2) * rows, :] = value


def cross_back_kernel(n, order, enc, *refs):
    el, es, refs = refs[: n - 1], refs[n - 1], refs[n:]
    (grad, mixed, inverse, cq, kv_far, p_far, after, n1, w_cm, w_cout, w_cq, gains) = refs[:12]
    parts, (self_grad, g_cross, g_small, dq, up, dkv, kv, p, sems) = refs[12:-9], refs[-9:]
    ready, done = loads(kv_far, p_far, kv, p, sems)
    rows, width = enc.shape[1:]
    low = grad[...].astype(LOW)
    g_cross[:, 3 * width :] = tn(mixed[...], low).astype(LOW)
    up[...] = nt(low, w_cout[...]).astype(LOW)
    attend_back(up, mixed, inverse, cq, kv, p, dq, dkv, plan_of(n), ready, done)
    dq_low = dq[...]
    g_cross[:, 2 * width : 3 * width] = tn(n1[...], dq_low).astype(LOW)
    total = tn(enc[order[0]], dkv[0:rows, :])
    for d in range(1, n):
        total = total + tn(el[d - 1][...], dkv[d * rows : (d + 1) * rows, :])
    for j in range(n // 4):
        total = total + tn(es[j], dkv[(n + j) * rows : (n + j + 1) * rows, :])
    g_cross[:, : 2 * width] = total.astype(LOW)
    for b in range(n + n // 4):
        put_part(parts, n, b, nt(dkv[b * rows : (b + 1) * rows, :], w_cm[...]).astype(LOW))
    inner, gain, shift = norm_back(after[...], gains[1:2], nt(dq_low, w_cq[...]))
    self_grad[...] = grad[...] + inner
    g_small[0, :] = gain
    g_small[1, :] = shift


def self_back_kernel(n, order, codes, x, *refs):
    xl, refs = refs[: n - 1], refs[n - 1 :]
    (
        xs, self_grad, mixed, inverse, q, kv_far, p_far, w_in, w_out, gains, shifts, small_feed, g_bias,
        small_cross, g_cross, _,
    ) = refs[:16]
    parts, (own, near, far, sums, dq, up, dkv, kv, p, sems) = refs[16:-10], refs[-10:]
    ready, done = loads(kv_far, p_far, kv, p, sems)
    rows, width = x.shape[1:]
    low = self_grad[...].astype(LOW)
    up[...] = nt(low, w_out[...]).astype(LOW)
    attend_back(up, mixed, inverse, q, kv, p, dq, dkv, plan_of(n), ready, done)
    mine = jnp.concatenate([x[order[0]], x[order[1]]], axis=0).astype(WIDE)
    unit = standard(mine)[0]
    normed = (unit * gains[0:1] + shifts[0:1]).astype(LOW)
    g_out = tn(mixed[...], low).astype(LOW)
    g_query = tn(normed, dq[...]).astype(LOW)
    mine = nt(dq[...], w_in[:, :width])
    own[...] = mine
    gain = jnp.sum(mine * unit, axis=0)
    shift = jnp.sum(mine, axis=0)
    total = None
    for b in range(n + n // 4):
        if b == 0:
            key_unit, key_low = unit[:rows], normed[:rows]
        else:
            v = xl[b - 1][...] if b < n else xs[b - n]
            key_unit = standard(v.astype(WIDE))[0]
            key_low = (key_unit * gains[0:1] + shifts[0:1]).astype(LOW)
        pairs = dkv[b * rows : (b + 1) * rows, :]
        term = tn(key_low, pairs)
        total = term if total is None else total + term
        back = nt(pairs, w_in[:, width:])
        put_part(parts, n, b, back.astype(LOW))
        gain = gain + jnp.sum(back * key_unit, axis=0)
        shift = shift + jnp.sum(back, axis=0)
    small = [gain[None], small_cross[0:1], small_feed[1:2], shift[None], small_cross[1:2],
             small_feed[2:3], small_feed[0:1], g_bias[...]]
    small = [v[:, i : i + 128] for v in small for i in range(0, v.shape[1], 128)]
    small.append(jnp.zeros((width - len(small), 128), WIDE))
    small = jnp.concatenate(small, axis=0).astype(LOW)
    spread(sums, codes[0], g_cross, 0)
    spread(sums, codes[1], g_query, 4 * width)
    spread(sums, codes[1], total.astype(LOW), 5 * width)
    spread(sums, codes[1], g_out, 7 * width)
    spread(sums, codes[1], small, 8 * width)
    half = sums.shape[0] // 2
    saves = [
        pltpu.make_async_copy(sums.at[:half], near, sems.at[0]),
        pltpu.make_async_copy(sums.at[half:], far, sems.at[1]),
    ]
    for save in saves:
        save.start()
    for save in saves:
        save.wait()


def unpack(plan, codes, pieces, outs):
    for out, (at, count, which, lane, side) in zip(outs, plan):
        wide = out.shape[1]
        depth, tall = pieces[at].shape[:2]
        for k in range(count * depth):
            first = (codes[which] ^ k) * (tall * side)
            for i in range(side):
                start = pl.multiple_of(first + i * tall, tall)
                lanes = slice(lane + i * wide, lane + (i + 1) * wide)
                out[pl.ds(start, tall), :] = pieces[at + k // depth][k % depth, :, lanes].astype(WIDE)


def unpack_feed_kernel(plan, codes, *refs):
    unpack(plan, codes, refs[: -len(plan)], refs[-len(plan) :])


def unpack_rest_kernel(plan, codes, *refs):
    *refs, up_bias, down_bias, gains, shifts, small = refs
    count = len(plan) - 1
    unpack(plan, codes, refs[:-count], refs[-count:] + [small])
    at = 0
    for out, count in ((gains, 3), (shifts, 3), (down_bias, 1), (up_bias, 1)):
        for i in range(count):
            across = out.shape[1] // 128
            row = [small[at + j : at + j + 1, :] for j in range(across)]
            out[i : i + 1, :] = jnp.concatenate(row, axis=1)
            at += across


def last_kernel(n, order, rank, x, self_grad, own, gains, part, part_got, e_long, *refs):
    shorts, e_shorts, (grad, e_grad) = refs[: n // 4], refs[n // 4 : n // 2], refs[-2:]
    rows = x.shape[1]

    def mine(helds):
        total = jnp.zeros(part.shape, WIDE)
        for root, held in enumerate(helds):
            total = jnp.where(rank[0] == root, held[...].astype(WIDE), total)
        return total

    long_up = own[:rows] + part[...].astype(WIDE) + part_got[...].astype(WIDE)
    short_up = own[rows:] + mine(shorts)
    for which, up, at in ((order[0], long_up, 0), (order[1], short_up, rows)):
        inner, _, _ = norm_back(x[which].astype(WIDE), gains[0:1], up)
        grad[which] = self_grad[at : at + rows] + inner
    e_grad[order[0]] = e_long[...]
    e_grad[order[1]] = mine(e_shorts)


def add_core(near, got, *outs):
    at = 0
    half = near.shape[0] // 2
    for keep, send in zip(outs[::2], outs[1::2]):
        lanes = slice(at, at + keep.shape[2])
        keep[...] = near[:half, :, lanes] + got[:half, :, lanes]
        send[...] = near[half:, :, lanes] + got[half:, :, lanes]
        at = lanes.stop


def add_returns(own, near, near_got, *refs):
    rows = own.shape[0]
    count = near.shape[0] // rows
    total = own[...].astype(WIDE) + near_got[:rows, :].astype(WIDE)
    for ref in refs[:-count]:
        total = total + ref[...].astype(WIDE)
    refs[-count][...] = total
    for k in range(1, count):
        at = slice(k * rows, (k + 1) * rows)
        refs[k - count][...] = near[at, :] + near_got[at, :]


def add_halves(keep, got, *outs):
    half = keep.shape[0] // 2
    outs[-2][...] = keep[:half] + got[:half]
    outs[-1][...] = keep[half:] + got[half:]


def add_to_pieces(a, got_a, b, got_b, *outs):
    wide = a.shape[2]
    for k, out in enumerate(outs[-a.shape[0] :]):
        out[:, :, :wide] = a[k : k + 1] + got_a[k : k + 1]
        out[:, :, wide:] = b[k : k + 1] + got_b[k : k + 1]


def note(*refs):
    pass


def add_all(_, *refs):
    *parts, out = refs
    total = parts[0][...].astype(WIDE)
    for part in parts[1:]:
        total = total + part[...].astype(WIDE)
    out[...] = total.astype(out.dtype)


def lay_whole(_, *refs):
    for k, ref in enumerate(refs[:-1]):
        refs[-1][k : k + 1] = ref[...]


def lay(*refs):
    *parts, a, b = refs
    wide = a.shape[2]
    for k, part in enumerate(parts):
        a[k : k + 1] = part[:, :, :wide]
        b[k : k + 1] = part[:, :, wide:]


def join(a, b, out):
    out[: a.shape[0]] = a[...]
    out[a.shape[0] :] = b[...]


def beside(a, got_a, b, got_b, out):
    half, _, wide = a.shape
    out[:half, :, :wide] = a[...]
    out[half:, :, :wide] = got_a[...]
    out[:half, :, wide:] = b[...]
    out[half:, :, wide:] = got_b[...]


def steps_kernel(steps, *refs):
    refs = list(refs)
    at_in, at_out = 0, sum(count for _, count, _ in steps)
    for kernel, ins, outs in steps:
        kernel(*refs[at_in : at_in + ins], *refs[at_out : at_out + outs])
        at_in += ins
        at_out += outs


def call(kernel, ins, outs, us, scratch=(), smem=0, room=62, far_ins=(), far_outs=(), sems=0):
    vmem = pl.BlockSpec(memory_space=pltpu.VMEM)
    far = pl.BlockSpec(memory_space=pltpu.HBM)
    in_specs = [vmem] * len(ins)
    in_specs[:smem] = [pl.BlockSpec(memory_space=pltpu.SMEM)] * smem
    for i in far_ins:
        in_specs[i] = far
    scratch_shapes = [pltpu.VMEM(s, t) for s, t in scratch]
    if sems:
        scratch_shapes.append(pltpu.SemaphoreType.DMA((sems,)))
    return pl.pallas_call(
        kernel,
        out_shape=[jax.ShapeDtypeStruct(s, t) for s, t in outs],
        in_specs=in_specs,
        out_specs=[far if i in far_outs else vmem for i in range(len(outs))],
        scratch_shapes=scratch_shapes,
        compiler_params=pltpu.CompilerParams(vmem_limit_bytes=room << 20),
        cost_estimate=pl.CostEstimate(flops=us * 10**9, bytes_accessed=0, transcendentals=0),
    )(*ins)


def small_steps(steps):
    outs = call(
        functools.partial(steps_kernel, [(k, len(i), len(o)) for k, i, o in steps]),
        [v for _, ins, _ in steps for v in ins],
        [o if isinstance(o[0], tuple) else (o, LOW) for _, _, outs in steps for o in outs],
        2,
        room=20,
    )
    got = []
    for _, _, shapes in steps:
        got.append(outs[: len(shapes)])
        outs = outs[len(shapes) :]
    return got


def send_long(block, n, wrap):
    got = []
    for d in range(1, n):
        pairs = [(i, (i + d) % n) for i in range(n) if wrap or i + d < n]
        got.append(lax.ppermute(block, "blk", pairs))
    return got


def return_long(block, n, distance, wrap):
    pairs = [(i, (i - distance) % n) for i in range(n) if wrap or i >= distance]
    return lax.ppermute(block, "blk", pairs)


def return_short(held, n, root, distance):
    pairs = [((root + k + distance) % n, (root + k) % n) for k in range(0, n, 2 * distance)]
    return lax.ppermute(held, "blk", pairs)


def return_short_rest(helds, n):
    got = []
    for root, held in enumerate(helds):
        d = 4
        while d < n:
            held = held + return_short(held, n, root, d)
            d *= 2
        got.append(held)
    return got


def send_short_first(block, n, rank):
    got = []
    for root in range(n // 4):
        held = jnp.where(rank == root, block, jnp.zeros_like(block))
        got.append([held, lax.ppermute(held, "blk", [(root, (root + n // 2) % n)])])
    return got


def send_short_rest(terms, n):
    for root in range(n // 4):
        d = n // 4
        while d:
            pairs = [((root + k) % n, (root + k + d) % n) for k in range(0, n, 2 * d)]
            held = functools.reduce(jnp.add, terms[root])
            terms[root].append(lax.ppermute(held, "blk", pairs))
            d //= 2
    return [v for several in terms for v in several]


def tied(value, *others):
    return lax.optimization_barrier((value, others))[0]


def trade(v, axis, distance):
    return lax.ppermute(v, axis, [(i, i ^ distance) for i in range(lax.axis_size(axis))])


class Sharing:
    def __init__(self, batch, n):
        self.rest = [("batch", d) for d in (8, 16, 32) if d < batch]
        self.rest += [("blk", d) for d in (4, 8, 16, 32) if d < n]
        self.chunks = 32

    def codes(self):
        codes = []
        for first, second in ((2, 4), (4, 2)):
            code = jnp.int32(0)
            for axis, distance in (("batch", 1), ("batch", first), ("batch", second), ("blk", 2),
                                   ("blk", 1)):
                code = 2 * code + (lax.axis_index(axis) // distance) % 2
            codes.append(code.astype(jnp.int32))
        return jnp.stack(codes)

    def doubled(self, v):
        for axis, distance in self.rest:
            v = v + trade(v, axis, distance)
        return v


def to_tall(pieces):
    return [trade(v, "blk", j) for j, v in enumerate(pieces) if j]


def on_device(
    decoder_input, encoder_output, sequence_lengths, chain_breaks,
    self_inward, self_outward, cross_query, cross_memory, cross_outward,
    feed_up, feed_up_bias, feed_down, feed_down_bias, norm_gains, norm_shifts,
    output_cotangent,
):
    sequences, rows, width = decoder_input.shape
    hidden = feed_up.shape[1]
    n = lax.axis_size("blk")
    rank = lax.axis_index("blk")
    ranks = rank.astype(jnp.int32)[None]
    longest = (sequence_lengths[1] > sequence_lengths[0]).astype(jnp.int32)
    order = jnp.stack([longest, 1 - longest])
    both = 2 * rows
    nk = (n + n // 4) * rows
    pairs = width // PAIR

    def pick(v, i):
        return jnp.where(order[i] == 0, v[0], v[1])

    sharing = Sharing(lax.axis_size("batch"), n)
    codes = sharing.codes()
    chunks = sharing.chunks
    tall = width // chunks
    blocks = nk // rows

    room = 62 if n > 4 else 40
    x_long, x_short = pick(decoder_input, 0), pick(decoder_input, 1)
    e_long, e_short = pick(encoder_output, 0), pick(encoder_output, 1)
    firsts = send_short_first(jnp.concatenate([x_short, e_short]), n, rank)
    xl = send_long(x_long, n, False)
    xs = send_short_rest([[v[:rows] for v in terms] for terms in firsts], n)
    shorts = len(xs) // (n // 4)
    e_long = tied(e_long, *xl)
    es = send_short_rest([[tied(v[rows:], *xl) for v in terms] for terms in firsts], n)
    el = send_long(e_long, n, True)

    kept = [((nk, 2 * width), LOW), ((nk, pairs * both), LOW)]
    loaded = [kept[0], ((2, nk, both), LOW)]
    inverses = ((2 * pairs, both), WIDE)
    low_rows, wide_rows = ((both, width), LOW), ((both, width), WIDE)
    q, kv, p, mixed, inverse, after, cq, n1, xs = call(
        functools.partial(self_kernel, n, shorts),
        (order, ranks, decoder_input, *xl, *xs, self_inward, self_outward, cross_query,
         norm_gains, norm_shifts),
        [low_rows, *kept, low_rows, inverses, wide_rows, low_rows, low_rows,
         ((n // 4, rows, width), LOW)],
        12,
        scratch=kept,
        smem=2,
        room=room,
        far_outs=(1, 2),
        sems=pairs + 1,
    )
    ckv, cp, cmixed, cinverse, crossed, es = call(
        functools.partial(cross_kernel, n, shorts),
        (order, ranks, chain_breaks, encoder_output, *el, *es, cq, after, cross_memory,
         cross_outward),
        [*kept, low_rows, inverses, wide_rows, ((n // 4, rows, width), LOW)],
        11,
        scratch=kept,
        smem=3,
        room=room,
        far_outs=(0, 1),
        sems=pairs + 1,
    )
    half = chunks // 2
    layer_output, cross_grad, near, far, g_bias, small_feed = call(
        feed_kernel,
        (order, codes, crossed, output_cotangent, feed_up, feed_up_bias[None], feed_down,
         feed_down_bias[None], norm_gains, norm_shifts),
        [(decoder_input.shape, LOW), ((both, width), WIDE), ((half, tall, 2 * hidden), LOW),
         ((half, tall, 2 * hidden), LOW), ((1, hidden), WIDE), ((3, width), WIDE)],
        14,
        scratch=[low_rows, wide_rows, wide_rows, ((chunks, tall, 2 * hidden), LOW)],
        smem=2,
        room=room,
        far_outs=(2, 3),
        sems=2,
    )
    wide = [hidden, hidden]
    wide_rest = [hidden, hidden + 128]

    def shape(count, lanes):
        return (count, tall, lanes)

    roots = range(n // 4)
    part_shapes = [((rows, width), LOW)] * n
    part_shapes[1] = (((n // 4 + 1) * rows, width), LOW)
    feed_core = trade(far, "batch", 1)
    feed_near = near
    *e_parts, self_grad, g_cross, small_cross = call(
        functools.partial(cross_back_kernel, n),
        (order, encoder_output, *el, es, cross_grad, cmixed, cinverse,
         cq, ckv, cp, after, n1, cross_memory, cross_outward, cross_query, norm_gains),
        part_shapes + [((both, width), WIDE), ((width, 4 * width), LOW), ((2, width), WIDE)],
        14,
        scratch=[low_rows, low_rows, kept[0], *loaded],
        smem=1,
        room=room,
        far_ins=(n + 6, n + 7),
        sems=3 * pairs,
    )
    (a, a_send, b, b_send), _ = small_steps(
        [(add_core, (feed_near, feed_core), [shape(8, w) for w in wide for _ in "ks"]),
         (note, (small_cross,), [])]
    )
    a_got, b_got = trade(a_send, "batch", 2), trade(b_send, "batch", 4)
    e_got = [return_long(e_parts[d], n, d, True) for d in range(1, n)]
    *parts, own, near, far = call(
        functools.partial(self_back_kernel, n),
        (order, codes, decoder_input, *xl, xs, self_grad, mixed, inverse, q, kv, p, self_inward,
         self_outward, norm_gains, norm_shifts, small_feed, g_bias, small_cross, g_cross, a),
        [((rows, width), LOW)] * blocks
        + [((both, width), WIDE), (shape(half, sum(wide_rest)), LOW),
           (shape(half, sum(wide_rest)), LOW)],
        16,
        scratch=[(shape(chunks, sum(wide_rest)), LOW), low_rows, low_rows, kept[0], *loaded],
        smem=2,
        room=room,
        far_ins=(n + 7, n + 8),
        far_outs=(blocks + 1, blocks + 2),
        sems=3 * pairs,
    )
    (a, a_send), (b, b_send), (e_long, *e_short) = small_steps(
        [(add_halves, (a, a_got, own), [shape(4, wide[0])] * 2),
         (add_halves, (b, b_got), [shape(4, wide[1])] * 2),
         (add_returns, (e_parts[0], e_parts[1], *e_got),
          [((rows, width), WIDE)] + [(rows, width)] * (n // 4))]
    )
    a_got, b_got = trade(a_send, "batch", 4), trade(b_send, "batch", 2)
    e_got = [return_short(e_short[k], n, k, 2) for k in roots]
    feed, (a, a_send, b, b_send), *e_short = small_steps(
        [(add_to_pieces, (a, a_got, b, b_got), [shape(1, sum(wide))] * 4),
         (add_core, (near, trade(tied(far, a_send), "batch", 1)),
          [shape(8, w) for w in wide_rest for _ in "ks"])]
        + [(add_all, (own, e_short[k], e_got[k]), [(rows, width)]) for k in roots]
    )
    e_short = return_short_rest([v for v, in e_short], n)
    a_got, b_got = trade(a_send, "batch", 2), trade(b_send, "batch", 4)
    (a, a_send), (b, b_send), (feed,) = small_steps(
        [(add_halves, (a, a_got), [shape(4, wide_rest[0])] * 2),
         (add_halves, (b, b_got), [shape(4, wide_rest[1])] * 2),
         (add_all, (own, feed[0], *to_tall(feed)), [shape(1, sum(wide))])]
    )
    feed = sharing.doubled(feed)
    a_got, b_got = trade(a_send, "batch", 4), trade(b_send, "batch", 2)
    rest, (fa, fb) = small_steps(
        [(add_to_pieces, (a, a_got, b, b_got), [shape(1, sum(wide_rest))] * 4),
         (lay, (feed, *to_tall([feed] * 4)), [shape(4, w) for w in wide])]
    )
    (rest,), (fa,), (fb,) = small_steps(
        [(add_all, (own, rest[0], *to_tall(rest)), [shape(1, sum(wide_rest))]),
         (join, (fa, trade(fa, "batch", 4)), [shape(8, wide[0])]),
         (join, (fb, trade(fb, "batch", 2)), [shape(8, wide[1])])]
    )
    rest = sharing.doubled(rest)
    (ra, rb), (feed,) = small_steps(
        [(lay, (rest, *to_tall([rest] * 4)), [shape(4, w) for w in wide_rest]),
         (beside, (fa, trade(fa, "batch", 2), fb, trade(fb, "batch", 4)),
          [shape(16, sum(wide))])]
    )
    ra_got, rb_got = trade(ra, "batch", 4), trade(rb, "batch", 2)
    feed_got = trade(feed, "batch", 1)
    held, *shorts = tied((parts[n - 1], *parts[n:]), ra)
    for d in range(n - 2, 2, -1):
        held = parts[d] + return_long(held, n, 1, False)
    long_got = return_long(held, n, 1, False)
    got = [return_short(shorts[k], n, k, 1) for k in roots]
    (ra,), (rb,), _, (held,), *shorts = small_steps(
        [(join, (ra, ra_got), [shape(8, wide_rest[0])]),
         (join, (rb, rb_got), [shape(8, wide_rest[1])]),
         (note, (feed_got,), []),
         (add_all, (own, parts[2], long_got), [(rows, width)])]
        + [(add_all, (own, parts[n + k], got[k]), [(rows, width)]) for k in roots]
    )
    ra_got, rb_got = trade(ra, "batch", 2), trade(rb, "batch", 4)
    long_got = return_long(held, n, 1, False)
    got = [return_short(shorts[k][0], n, k, 2) for k in roots]
    s_up, s_down = call(
        functools.partial(unpack_feed_kernel, [(0, 2, 0, 0, 1), (0, 2, 1, hidden, hidden // width)]),
        (codes, feed, feed_got),
        [(feed_up.shape, WIDE), (feed_down.shape, WIDE)],
        6,
        smem=1,
        room=room,
    )
    (rest,), _, (held,), *shorts = small_steps(
        [(beside, (ra, ra_got, rb, rb_got), [shape(16, sum(wide_rest))]),
         (note, (s_down[:8, :128],), []),
         (add_all, (own, parts[1], long_got), [(rows, width)])]
        + [(add_all, (own, shorts[k][0], got[k]), [(rows, width)]) for k in roots]
    )
    shorts = return_short_rest([v for v, in shorts], n)
    long_got = return_long(held, n, 1, False)
    rest_got = trade(rest, "batch", 1)
    input_gradient, encoder_gradient = call(
        functools.partial(last_kernel, n),
        (order, ranks, decoder_input, self_grad, own, norm_gains, parts[0], long_got, e_long,
         *shorts, *e_short),
        [(decoder_input.shape, WIDE), (decoder_input.shape, WIDE)],
        3,
        smem=2,
        room=room,
    )
    at = hidden
    places = [(0, 2, 0, 0, 1), (0, 2, 0, 2 * width, 1), (0, 2, 0, 3 * width, 1),
              (0, 2, 1, at, 1), (0, 2, 1, at + 3 * width, 1), (0, 2, 1, at + 4 * width, 1)]
    s_cm, s_cq, s_cout, s_in, s_out, up_bias, down_bias, gains, shifts = call(
        functools.partial(unpack_rest_kernel, places),
        (codes, rest, rest_got),
        [(s, WIDE) for s in (cross_memory.shape, cross_query.shape, cross_outward.shape,
                             self_inward.shape, self_outward.shape, (1, hidden), (1, width),
                             norm_gains.shape, norm_shifts.shape)],
        5,
        scratch=[((width, 128), WIDE)],
        smem=1,
        room=room,
    )
    return (
        layer_output, input_gradient, encoder_gradient, s_in, s_out, s_cq, s_cm, s_cout,
        s_up, up_bias[0], s_down, down_bias[0], gains, shifts,
    )


def solution(mesh):
    blocked = P("batch", "blk", None)
    placed = (blocked, blocked, P("batch"), P("batch", None)) + (P(),) * 11 + (blocked,)
    return jax.shard_map(
        on_device,
        mesh=mesh,
        in_specs=placed,
        out_specs=(blocked,) * 3 + (P(),) * 11,
        check_vma=False,
    )
```

profile of v0, /device:TPU:0, one launch (start us, length us, event | category | flops | bytes accessed | tf_op | source)
XLA Modules:
  0.0 272.6 jit_solution(4054293489494853312)
XLA Ops:
  3.3 1.8 select_bitcast_fusion
  5.0 1.8 select_bitcast_fusion.1
  7.0 6.1 %collective-permute-start.6 = (bf16[512,512]{1,0:T(8,128)(2,1)S(1)}, bf16[512,512]{1,0:T(8,128)(2,1)S(1)}, u32[]{:S(2)}, u32[]{:S(2)}) collective-permute-start(bf16[512,512]{1,0:T(8,128)(2,1)S(1)} %maximum_select_fusion), channel_id=1, source_target_pairs={{0,2},{4,6},{8,10},{12,14},{16,18},{20,22},{24,26},{28,30}} | collective-permute-start | bytes 1572872 | tf_op jit(solution)/shard_map/ppermute | solution.py:654
  13.1 1.7 collective-permute-start.2
  14.8 2.0 collective-permute-start.1
  16.8 3.2 %collective-permute-start = (bf16[256,512]{1,0:T(8,128)(2,1)}, bf16[256,512]{1,0:T(8,128)(2,1)}, u32[]{:S(2)}, u32[]{:S(2)}) collective-permute-start(bf16[256,512]{1,0:T(8,128)(2,1)} %get-tuple-element.216), channel_id=1, source_target_pairs={{0,1},{1,2},{2,3},{4,5},{5,6},{6,7},{8,9},{9,10},{10,11},{12,13},{... | collective-permute-start | bytes 786440 | tf_op jit(solution)/shard_map/ppermute | solution.py:625
  19.9 5.5 %collective-permute-done.6 = bf16[512,512]{1,0:T(8,128)(2,1)S(1)} collective-permute-done((bf16[512,512]{1,0:T(8,128)(2,1)S(1)}, bf16[512,512]{1,0:T(8,128)(2,1)S(1)}, u32[]{:S(2)}, u32[]{:S(2)}) %collective-permute-start.6) | collective-permute-done | bytes 524320 | tf_op jit(solution)/shard_map/ppermute | solution.py:654
  26.2 2.0 collective-permute-start.8
  28.3 2.8 %collective-permute-done.2.refs_2_ = bf16[256,512]{1,0:T(8,128)(2,1)S(1)} collective-permute-done((bf16[256,512]{1,0:T(8,128)(2,1)}, bf16[256,512]{1,0:T(8,128)(2,1)S(1)}, u32[]{:S(2)}, u32[]{:S(2)}) %collective-permute-start.2) | collective-permute-done | bytes 262176 | tf_op jit(solution)/shard_map/ppermute | solution.py:625
  31.2 5.6 %collective-permute-done.1.refs_1_ = bf16[256,512]{1,0:T(8,128)(2,1)} collective-permute-done((bf16[256,512]{1,0:T(8,128)(2,1)}, bf16[256,512]{1,0:T(8,128)(2,1)}, u32[]{:S(2)}, u32[]{:S(2)}) %collective-permute-start.1) | collective-permute-done | bytes 262176 | tf_op jit(solution)/shard_map/ppermute | solution.py:625
  36.8 5.6 %collective-permute-done.refs_0_ = bf16[256,512]{1,0:T(8,128)(2,1)} collective-permute-done((bf16[256,512]{1,0:T(8,128)(2,1)}, bf16[256,512]{1,0:T(8,128)(2,1)}, u32[]{:S(2)}, u32[]{:S(2)}) %collective-permute-start) | collective-permute-done | bytes 262176 | tf_op jit(solution)/shard_map/ppermute | solution.py:625
  42.4 3.2 %collective-permute-start.5 = (bf16[256,512]{1,0:T(8,128)(2,1)}, bf16[256,512]{1,0:T(8,128)(2,1)S(1)}, u32[]{:S(2)}, u32[]{:S(2)}) collective-permute-start(bf16[256,512]{1,0:T(8,128)(2,1)} %get-tuple-element.112), channel_id=1, source_target_pairs={{0,3},{1,0},{2,1},{3,2},{4,7},{5,4},{6,5},{7,6},{8,11},{9,8},{10,9... | collective-permute-start | bytes 786440 | tf_op jit(solution)/shard_map/ppermute | solution.py:625
  45.6 5.4 %collective-permute-start.4 = (bf16[256,512]{1,0:T(8,128)(2,1)}, bf16[256,512]{1,0:T(8,128)(2,1)S(1)}, u32[]{:S(2)}, u32[]{:S(2)}) collective-permute-start(bf16[256,512]{1,0:T(8,128)(2,1)} %get-tuple-element.112), channel_id=1, source_target_pairs={{0,2},{1,3},{2,0},{3,1},{4,6},{5,7},{6,4},{7,5},{8,10},{9,11},{10,... | collective-permute-start | bytes 786440 | tf_op jit(solution)/shard_map/ppermute | solution.py:625
  51.0 2.0 collective-permute-start.3
  53.1 1.9 collective-permute-start.7
  57.2 11.5 %shard_map.263 = (bf16[512,512]{1,0:T(8,128)(2,1)S(1)}, bf16[1280,1024]{1,0:T(8,128)(2,1)S(1)}, bf16[1280,2048]{1,0:T(8,128)(2,1)}, bf16[512,512]{1,0:T(8,128)(2...) custom-call(s32[2]{0:T(128)S(1)} %pad_add_fusion.order, ...), custom_call_target="tpu_custom_call" | custom-call | flops 12000000000 | tf_op jit(solution)/shard_map/pallas_call | solution.py:595
  71.7 2.7 %collective-permute-done.4.refs_1_ = bf16[256,512]{1,0:T(8,128)(2,1)S(1)} collective-permute-done((bf16[256,512]{1,0:T(8,128)(2,1)}, bf16[256,512]{1,0:T(8,128)(2,1)S(1)}, u32[]{:S(2)}, u32[]{:S(2)}) %collective-permute-start.4) | collective-permute-done | bytes 262176 | tf_op jit(solution)/shard_map/ppermute | solution.py:625
  74.5 10.0 %shard_map.264 = (bf16[1280,1024]{1,0:T(8,128)(2,1)S(1)}, bf16[1280,2048]{1,0:T(8,128)(2,1)}, bf16[512,512]{1,0:T(8,128)(2,1)S(1)}, f32[8,512]{1,0:T(8,128)S(1)}...) custom-call(s32[2]{0:T(128)S(1)} %pad_add_fusion.order, s32[1]{0:T(128)} %bitcast.2.rank, ...), custom_call_target="tpu_custom_call" | custom-call | flops 11000000512 | tf_op jit(solution)/shard_map/pallas_call | solution.py:595
  86.1 14.9 %shard_map.265 = (bf16[2,256,512]{2,1,0:T(8,128)(2,1)}, f32[512,512]{1,0:T(8,128)S(1)}, bf16[16,16,4096]{2,1,0:T(8,128)(2,1)S(1)}, bf16[16,16,4096]{2,1,0:T(8,12...) custom-call(s32[2]{0:T(128)S(1)} %pad_add_fusion.order, s32[2]{0:T(128)S(1)} %pad_add_fusion.1.codes, ...), custom_call_target="tpu_custom_call" | custom-call | flops 14000000000 | tf_op jit(solution)/shard_map/pallas_call | solution.py:595
  103.2 1.7 copy-done.21
  106.2 12.2 %shard_map.266 = (bf16[256,512]{1,0:T(8,128)(2,1)S(1)}, bf16[512,512]{1,0:T(8,128)(2,1)S(1)}, bf16[256,512]{1,0:T(8,128)(2,1)S(1)}, bf16[256,512]{1,0:T(8,128)(2...) custom-call(s32[2]{0:T(128)S(1)} %pad_add_fusion.order, ...), custom_call_target="tpu_custom_call" | custom-call | flops 14000000000 | tf_op jit(solution)/shard_map/pallas_call | solution.py:595
  119.8 3.8 %collective-permute-start.12 = (bf16[512,512]{1,0:T(8,128)(2,1)S(1)}, bf16[512,512]{1,0:T(8,128)(2,1)S(1)}, u32[]{:S(2)}, u32[]{:S(2)}) collective-permute-start(bf16[512,512]{1,0:T(8,128)(2,1)S(1)} %get-tuple-element.146.refs_6_), channel_id=1, source_target_pairs={{0,3},{1,0},{2,1},{3,2},{4,7},{5,4},{6,5},{7,6},{8,11},{9,8},{10,9... | collective-permute-start | bytes 1572872 | tf_op jit(solution)/shard_map/ppermute | solution.py:631
  123.6 1.6 copy-done.16
  129.8 14.9 %shard_map.268 = (bf16[256,512]{1,0:T(8,128)(2,1)S(1)}, bf16[256,512]{1,0:T(8,128)(2,1)S(1)}, bf16[256,512]{1,0:T(8,128)(2,1)S(1)}, bf16[256,512]{1,0:T(8,128)(2...) custom-call(s32[2]{0:T(128)S(1)} %pad_add_fusion.order, ...), custom_call_target="tpu_custom_call" | custom-call | flops 16000000000 | tf_op jit(solution)/shard_map/pallas_call | solution.py:595
  144.7 1.8 collective-permute-done.12.refs_7_
  152.7 5.4 %collective-permute-done.16.refs_3_ = bf16[4,16,2048]{2,1,0:T(8,128)(2,1)S(1)} collective-permute-done((bf16[4,16,2048]{2,1,0:T(8,128)(2,1)S(1)}, bf16[4,16,2048]{2,1,0:T(8,128)(2,1)S(1)}, u32[]{:S(2)}, u32[]{:S(2)}) %collective-permute-start.16) | collective-permute-done | bytes 262176 | tf_op jit(solution)/shard_map/ppermute | solution.py:674
  158.1 4.3 %collective-permute-done.18.refs_8_ = bf16[256,512]{1,0:T(8,128)(2,1)S(1)} collective-permute-done((bf16[256,512]{1,0:T(8,128)(2,1)S(1)}, bf16[256,512]{1,0:T(8,128)(2,1)S(1)}, u32[]{:S(2)}, u32[]{:S(2)}) %collective-permute-start.18) | collective-permute-done | bytes 262176 | tf_op jit(solution)/shard_map/ppermute | solution.py:636
  164.1 4.1 %collective-permute-start.23 = (bf16[1,16,4096]{2,1,0:T(8,128)(2,1)S(1)}, bf16[1,16,4096]{2,1,0:T(8,128)(2,1)S(1)}, u32[]{:S(2)}, u32[]{:S(2)}) collective-permute-start(bf16[1,16,4096]{2,1,0:T(8,128)(2,1)S(1)} %get-tuple-element.164), channel_id=1, source_target_pairs={{0,3},{1,2},{2,1},{3,0},{4,7},{5,6},{6,5},{7,4},{8,11},{9,10},{10,... | collective-permute-start | bytes 393224 | tf_op jit(solution)/shard_map/ppermute | solution.py:674
  168.3 1.6 collective-permute-done.21.refs_6_
  169.9 6.2 %collective-permute-done.22.refs_7_ = bf16[1,16,4096]{2,1,0:T(8,128)(2,1)S(1)} collective-permute-done((bf16[1,16,4096]{2,1,0:T(8,128)(2,1)S(1)}, bf16[1,16,4096]{2,1,0:T(8,128)(2,1)S(1)}, u32[]{:S(2)}, u32[]{:S(2)}) %collective-permute-start.22) | collective-permute-done | bytes 131104 | tf_op jit(solution)/shard_map/ppermute | solution.py:674
  180.8 2.0 collective-permute-start.27
  183.8 3.4 %collective-permute-done.28.refs_7_ = bf16[1,16,4096]{2,1,0:T(8,128)(2,1)S(1)} collective-permute-done((bf16[1,16,4096]{2,1,0:T(8,128)(2,1)S(1)}, bf16[1,16,4096]{2,1,0:T(8,128)(2,1)S(1)}, u32[]{:S(2)}, u32[]{:S(2)}) %collective-permute-start.28) | collective-permute-done | bytes 131104 | tf_op jit(solution)/shard_map/ppermute | solution.py:674
  187.2 4.7 %collective-permute-done.27.refs_6_ = bf16[1,16,4096]{2,1,0:T(8,128)(2,1)S(1)} collective-permute-done((bf16[1,16,4096]{2,1,0:T(8,128)(2,1)S(1)}, bf16[1,16,4096]{2,1,0:T(8,128)(2,1)S(1)}, u32[]{:S(2)}, u32[]{:S(2)}) %collective-permute-start.27) | collective-permute-done | bytes 131104 | tf_op jit(solution)/shard_map/ppermute | solution.py:674
  193.4 2.2 collective-permute-start.30
  195.6 2.2 collective-permute-start.31
  197.8 1.6 collective-permute-done.29.refs_2_
  199.5 6.4 %collective-permute-done.30.refs_3_ = bf16[1,16,4224]{2,1,0:T(8,128)(2,1)S(1)} collective-permute-done((bf16[1,16,4224]{2,1,0:T(8,128)(2,1)S(1)}, bf16[1,16,4224]{2,1,0:T(8,128)(2,1)S(1)}, u32[]{:S(2)}, u32[]{:S(2)}) %collective-permute-start.30) | collective-permute-done | bytes 135200 | tf_op jit(solution)/shard_map/ppermute | solution.py:674
  206.0 1.8 collective-permute-start.37
  210.1 2.1 collective-permute-start.35
  213.1 3.1 %collective-permute-done.36.refs_3_ = bf16[1,16,4224]{2,1,0:T(8,128)(2,1)S(1)} collective-permute-done((bf16[1,16,4224]{2,1,0:T(8,128)(2,1)S(1)}, bf16[1,16,4224]{2,1,0:T(8,128)(2,1)S(1)}, u32[]{:S(2)}, u32[]{:S(2)}) %collective-permute-start.36) | collective-permute-done | bytes 135200 | tf_op jit(solution)/shard_map/ppermute | solution.py:674
  216.1 4.2 %collective-permute-done.35.refs_2_ = bf16[1,16,4224]{2,1,0:T(8,128)(2,1)S(1)} collective-permute-done((bf16[1,16,4224]{2,1,0:T(8,128)(2,1)S(1)}, bf16[1,16,4224]{2,1,0:T(8,128)(2,1)S(1)}, u32[]{:S(2)}, u32[]{:S(2)}) %collective-permute-start.35) | collective-permute-done | bytes 135200 | tf_op jit(solution)/shard_map/ppermute | solution.py:674
  225.3 7.5 %collective-permute-done.42.refs_7_ = bf16[256,512]{1,0:T(8,128)(2,1)S(1)} collective-permute-done((bf16[256,512]{1,0:T(8,128)(2,1)S(1)}, bf16[256,512]{1,0:T(8,128)(2,1)S(1)}, u32[]{:S(2)}, u32[]{:S(2)}) %collective-permute-start.42) | collective-permute-done | bytes 262176 | tf_op jit(solution)/shard_map/ppermute | solution.py:631
  232.8 4.8 %collective-permute-done.43.refs_10_ = bf16[256,512]{1,0:T(8,128)(2,1)S(1)} collective-permute-done((bf16[256,512]{1,0:T(8,128)(2,1)S(1)}, bf16[256,512]{1,0:T(8,128)(2,1)S(1)}, u32[]{:S(2)}, u32[]{:S(2)}) %collective-permute-start.43) | collective-permute-done | bytes 262176 | tf_op jit(solution)/shard_map/ppermute | solution.py:636
  242.7 4.5 %shard_map.276 = (f32[512,2048]{1,0:T(8,128)}, f32[2048,512]{1,0:T(8,128)}) custom-call(s32[2]{0:T(128)S(1)} %pad_add_fusion.1.codes, bf16[16,16,4096]{2,1,0:T(8,128)(2,1)S(1)} %get-tuple-element.181.refs_0_, bf16[16,16,4096]{2,1,0:T(8,128)(2,1)S(1)} %collective-permute-done.41.refs_4_.refs_1_), custom_call_target="tpu_custom_call" | custom-call | flops 6000000000 | tf_op jit(solution)/shard_map/pallas_call | solution.py:595
  247.9 5.0 %collective-permute-done.46.refs_7_ = bf16[256,512]{1,0:T(8,128)(2,1)S(1)} collective-permute-done((bf16[256,512]{1,0:T(8,128)(2,1)S(1)}, bf16[256,512]{1,0:T(8,128)(2,1)S(1)}, u32[]{:S(2)}, u32[]{:S(2)}) %collective-permute-start.46) | collective-permute-done | bytes 262176 | tf_op jit(solution)/shard_map/ppermute | solution.py:631
  256.7 9.3 %collective-permute-done.48.part_got = bf16[256,512]{1,0:T(8,128)(2,1)S(1)} collective-permute-done((bf16[256,512]{1,0:T(8,128)(2,1)S(1)}, bf16[256,512]{1,0:T(8,128)(2,1)S(1)}, u32[]{:S(2)}, u32[]{:S(2)}) %collective-permute-start.48) | collective-permute-done | bytes 262176 | tf_op jit(solution)/shard_map/ppermute | solution.py:631
  266.0 2.6 shard_map.278
  268.6 3.9 %shard_map.279 = (f32[512,1024]{1,0:T(8,128)}, f32[512,512]{1,0:T(8,128)}, f32[512,512]{1,0:T(8,128)}, f32[512,1536]{1,0:T(8,128)}, f32[512,512]{1,0:T(8,128)}, ...) custom-call(s32[2]{0:T(128)S(1)} %pad_add_fusion.1.codes, ...), custom_call_target="tpu_custom_call" | custom-call | flops 5000000000 | tf_op jit(solution)/shard_map/pallas_call | solution.py:595
  (152 shorter events, 51.3 us)
Async XLA Ops:
  7.0 18.4 %collective-permute-start.6 = (bf16[512,512]{1,0:T(8,128)(2,1)S(1)}, bf16[512,512]{1,0:T(8,128)(2,1)S(1)}, u32[]{:S(2)}, u32[]{:S(2)}) collective-permute-start(bf16[512,512]{1,0:T(8,128)(2,1)S(1)} %maximum_select_fusion), channel_id=1, source_target_pairs={{0,2},{4,6},{8,10},{12,14},{16,18},{20,22},{24,26},{28,30}} | collective-permute-start | bytes 1572872 | tf_op jit(solution)/shard_map/ppermute | solution.py:654
  13.1 18.1 %collective-permute-start.2 = (bf16[256,512]{1,0:T(8,128)(2,1)}, bf16[256,512]{1,0:T(8,128)(2,1)S(1)}, u32[]{:S(2)}, u32[]{:S(2)}) collective-permute-start(bf16[256,512]{1,0:T(8,128)(2,1)} %get-tuple-element.216), channel_id=1, source_target_pairs={{0,3},{4,7},{8,11},{12,15},{16,19},{20,23},{24,27},{28,31}} | collective-permute-start | bytes 786440 | tf_op jit(solution)/shard_map/ppermute | solution.py:625
  14.8 22.0 %collective-permute-start.1 = (bf16[256,512]{1,0:T(8,128)(2,1)}, bf16[256,512]{1,0:T(8,128)(2,1)}, u32[]{:S(2)}, u32[]{:S(2)}) collective-permute-start(bf16[256,512]{1,0:T(8,128)(2,1)} %get-tuple-element.216), channel_id=1, source_target_pairs={{0,2},{1,3},{4,6},{5,7},{8,10},{9,11},{12,14},{13,15},{16,18},{17,... | collective-permute-start | bytes 786440 | tf_op jit(solution)/shard_map/ppermute | solution.py:625
  16.8 25.6 %collective-permute-start = (bf16[256,512]{1,0:T(8,128)(2,1)}, bf16[256,512]{1,0:T(8,128)(2,1)}, u32[]{:S(2)}, u32[]{:S(2)}) collective-permute-start(bf16[256,512]{1,0:T(8,128)(2,1)} %get-tuple-element.216), channel_id=1, source_target_pairs={{0,1},{1,2},{2,3},{4,5},{5,6},{6,7},{8,9},{9,10},{10,11},{12,13},{... | collective-permute-start | bytes 786440 | tf_op jit(solution)/shard_map/ppermute | solution.py:625
  26.2 28.9 %collective-permute-start.8 = (bf16[256,512]{1,0:T(8,128)(2,1)}, bf16[256,512]{1,0:T(8,128)(2,1)}, u32[]{:S(2)}, u32[]{:S(2)}) collective-permute-start(bf16[256,512]{1,0:T(8,128)(2,1)} %get-tuple-element.210), channel_id=1, source_target_pairs={{0,1},{2,3},{4,5},{6,7},{8,9},{10,11},{12,13},{14,15},{16,17},{18,... | collective-permute-start | bytes 786440 | tf_op jit(solution)/shard_map/ppermute | solution.py:664
  42.4 29.3 %collective-permute-start.5 = (bf16[256,512]{1,0:T(8,128)(2,1)}, bf16[256,512]{1,0:T(8,128)(2,1)S(1)}, u32[]{:S(2)}, u32[]{:S(2)}) collective-permute-start(bf16[256,512]{1,0:T(8,128)(2,1)} %get-tuple-element.112), channel_id=1, source_target_pairs={{0,3},{1,0},{2,1},{3,2},{4,7},{5,4},{6,5},{7,6},{8,11},{9,8},{10,9... | collective-permute-start | bytes 786440 | tf_op jit(solution)/shard_map/ppermute | solution.py:625
  45.6 28.9 %collective-permute-start.4 = (bf16[256,512]{1,0:T(8,128)(2,1)}, bf16[256,512]{1,0:T(8,128)(2,1)S(1)}, u32[]{:S(2)}, u32[]{:S(2)}) collective-permute-start(bf16[256,512]{1,0:T(8,128)(2,1)} %get-tuple-element.112), channel_id=1, source_target_pairs={{0,2},{1,3},{2,0},{3,1},{4,6},{5,7},{6,4},{7,5},{8,10},{9,11},{10,... | collective-permute-start | bytes 786440 | tf_op jit(solution)/shard_map/ppermute | solution.py:625
  51.0 23.4 %collective-permute-start.3 = (bf16[256,512]{1,0:T(8,128)(2,1)}, bf16[256,512]{1,0:T(8,128)(2,1)S(1)}, u32[]{:S(2)}, u32[]{:S(2)}) collective-permute-start(bf16[256,512]{1,0:T(8,128)(2,1)} %get-tuple-element.112), channel_id=1, source_target_pairs={{0,1},{1,2},{2,3},{3,0},{4,5},{5,6},{6,7},{7,4},{8,9},{9,10},{10,1... | collective-permute-start | bytes 786440 | tf_op jit(solution)/shard_map/ppermute | solution.py:625
  53.1 21.4 %collective-permute-start.7 = (bf16[256,512]{1,0:T(8,128)(2,1)S(1)}, bf16[256,512]{1,0:T(8,128)(2,1)S(1)}, u32[]{:S(2)}, u32[]{:S(2)}) collective-permute-start(bf16[256,512]{1,0:T(8,128)(2,1)S(1)} %add.69), channel_id=1, source_target_pairs={{0,1},{2,3},{4,5},{6,7},{8,9},{10,11},{12,13},{14,15},{16,17},{18,... | collective-permute-start | bytes 786440 | tf_op jit(solution)/shard_map/ppermute | solution.py:664
  103.2 20.4 %collective-permute-start.9 = (bf16[16,16,4096]{2,1,0:T(8,128)(2,1)S(1)}, bf16[16,16,4096]{2,1,0:T(8,128)(2,1)S(1)}, u32[]{:S(2)}, u32[]{:S(2)}) collective-permute-start(bf16[16,16,4096]{2,1,0:T(8,128)(2,1)S(1)} %get-tuple-element.138), channel_id=1, source_target_pairs={{0,4},{4,0},{8,12},{12,8},{16,20},{20,16},{24,28},{28,24},{1,5},{5... | collective-permute-start | bytes 6291464 | tf_op jit(solution)/shard_map/ppermute | solution.py:674
  119.8 24.9 %collective-permute-start.13 = (bf16[256,512]{1,0:T(8,128)(2,1)S(1)}, bf16[256,512]{1,0:T(8,128)(2,1)S(1)}, u32[]{:S(2)}, u32[]{:S(2)}) collective-permute-start(bf16[256,512]{1,0:T(8,128)(2,1)S(1)} %get-tuple-element.147), channel_id=1, source_target_pairs={{0,2},{1,3},{2,0},{3,1},{4,6},{5,7},{6,4},{7,5},{8,10},{9,11},{10,... | collective-permute-start | bytes 786440 | tf_op jit(solution)/shard_map/ppermute | solution.py:631
  119.8 24.9 %collective-permute-start.14 = (bf16[256,512]{1,0:T(8,128)(2,1)S(1)}, bf16[256,512]{1,0:T(8,128)(2,1)S(1)}, u32[]{:S(2)}, u32[]{:S(2)}) collective-permute-start(bf16[256,512]{1,0:T(8,128)(2,1)S(1)} %get-tuple-element.148), channel_id=1, source_target_pairs={{0,1},{1,2},{2,3},{3,0},{4,5},{5,6},{6,7},{7,4},{8,9},{9,10},{10,1... | collective-permute-start | bytes 786440 | tf_op jit(solution)/shard_map/ppermute | solution.py:631
  119.8 26.7 %collective-permute-start.12 = (bf16[512,512]{1,0:T(8,128)(2,1)S(1)}, bf16[512,512]{1,0:T(8,128)(2,1)S(1)}, u32[]{:S(2)}, u32[]{:S(2)}) collective-permute-start(bf16[512,512]{1,0:T(8,128)(2,1)S(1)} %get-tuple-element.146.refs_6_), channel_id=1, source_target_pairs={{0,3},{1,0},{2,1},{3,2},{4,7},{5,4},{6,5},{7,6},{8,11},{9,8},{10,9... | collective-permute-start | bytes 1572872 | tf_op jit(solution)/shard_map/ppermute | solution.py:631
  125.5 21.1 %collective-permute-start.10 = (bf16[8,16,2048]{2,1,0:T(8,128)(2,1)S(1)}, bf16[8,16,2048]{2,1,0:T(8,128)(2,1)S(1)}, u32[]{:S(2)}, u32[]{:S(2)}) collective-permute-start(bf16[8,16,2048]{2,1,0:T(8,128)(2,1)S(1)} %get-tuple-element.142), channel_id=1, source_target_pairs={{0,8},{4,12},{8,0},{12,4},{16,24},{20,28},{24,16},{28,20},{1,9},{5... | collective-permute-start | bytes 1572872 | tf_op jit(solution)/shard_map/ppermute | solution.py:674
  127.0 19.5 %collective-permute-start.11 = (bf16[8,16,2048]{2,1,0:T(8,128)(2,1)S(1)}, bf16[8,16,2048]{2,1,0:T(8,128)(2,1)S(1)}, u32[]{:S(2)}, u32[]{:S(2)}) collective-permute-start(bf16[8,16,2048]{2,1,0:T(8,128)(2,1)S(1)} %get-tuple-element.144), channel_id=1, source_target_pairs={{0,16},{4,20},{8,24},{12,28},{16,0},{20,4},{24,8},{28,12},{1,17},{... | collective-permute-start | bytes 1572872 | tf_op jit(solution)/shard_map/ppermute | solution.py:674
  148.1 14.2 %collective-permute-start.17 = (bf16[16,16,4224]{2,1,0:T(8,128)(2,1)S(1)}, bf16[16,16,4224]{2,1,0:T(8,128)(2,1)S(1)}, u32[]{:S(2)}, u32[]{:S(2)}) collective-permute-start(bf16[16,16,4224]{2,1,0:T(8,128)(2,1)S(1)} %copy-done.35), channel_id=1, source_target_pairs={{0,4},{4,0},{8,12},{12,8},{16,20},{20,16},{24,28},{28,24},{1,5},{5... | collective-permute-start | bytes 6488072 | tf_op jit(solution)/shard_map/ppermute | solution.py:674
  148.1 10.0 %collective-permute-start.15 = (bf16[4,16,2048]{2,1,0:T(8,128)(2,1)S(1)}, bf16[4,16,2048]{2,1,0:T(8,128)(2,1)S(1)}, u32[]{:S(2)}, u32[]{:S(2)}) collective-permute-start(bf16[4,16,2048]{2,1,0:T(8,128)(2,1)S(1)} %get-tuple-element.150), channel_id=1, source_target_pairs={{0,16},{4,20},{8,24},{12,28},{16,0},{20,4},{24,8},{28,12},{1,17},{... | collective-permute-start | bytes 786440 | tf_op jit(solution)/shard_map/ppermute | solution.py:674
  149.6 8.4 %collective-permute-start.16 = (bf16[4,16,2048]{2,1,0:T(8,128)(2,1)S(1)}, bf16[4,16,2048]{2,1,0:T(8,128)(2,1)S(1)}, u32[]{:S(2)}, u32[]{:S(2)}) collective-permute-start(bf16[4,16,2048]{2,1,0:T(8,128)(2,1)S(1)} %get-tuple-element.152), channel_id=1, source_target_pairs={{0,8},{4,12},{8,0},{12,4},{16,24},{20,28},{24,16},{28,20},{1,9},{5... | collective-permute-start | bytes 786440 | tf_op jit(solution)/shard_map/ppermute | solution.py:674
  151.1 11.2 %collective-permute-start.18 = (bf16[256,512]{1,0:T(8,128)(2,1)S(1)}, bf16[256,512]{1,0:T(8,128)(2,1)S(1)}, u32[]{:S(2)}, u32[]{:S(2)}) collective-permute-start(bf16[256,512]{1,0:T(8,128)(2,1)S(1)} %get-tuple-element.156.refs_7_), channel_id=1, source_target_pairs={{2,0},{6,4},{10,8},{14,12},{18,16},{22,20},{26,24},{30,28}} | collective-permute-start | bytes 786440 | tf_op jit(solution)/shard_map/ppermute | solution.py:636
  162.8 14.0 %collective-permute-start.20 = (bf16[8,16,2176]{2,1,0:T(8,128)(2,1)S(1)}, bf16[8,16,2176]{2,1,0:T(8,128)(2,1)S(1)}, u32[]{:S(2)}, u32[]{:S(2)}) collective-permute-start(bf16[8,16,2176]{2,1,0:T(8,128)(2,1)S(1)} %get-tuple-element.160), channel_id=1, source_target_pairs={{0,16},{4,20},{8,24},{12,28},{16,0},{20,4},{24,8},{28,12},{1,17},{... | collective-permute-start | bytes 1671176 | tf_op jit(solution)/shard_map/ppermute | solution.py:674
  163.4 12.9 %collective-permute-start.19 = (bf16[8,16,2048]{2,1,0:T(8,128)(2,1)S(1)}, bf16[8,16,2048]{2,1,0:T(8,128)(2,1)S(1)}, u32[]{:S(2)}, u32[]{:S(2)}) collective-permute-start(bf16[8,16,2048]{2,1,0:T(8,128)(2,1)S(1)} %get-tuple-element.158), channel_id=1, source_target_pairs={{0,8},{4,12},{8,0},{12,4},{16,24},{20,28},{24,16},{28,20},{1,9},{5... | collective-permute-start | bytes 1572872 | tf_op jit(solution)/shard_map/ppermute | solution.py:674
  163.9 12.2 %collective-permute-start.22 = (bf16[1,16,4096]{2,1,0:T(8,128)(2,1)S(1)}, bf16[1,16,4096]{2,1,0:T(8,128)(2,1)S(1)}, u32[]{:S(2)}, u32[]{:S(2)}) collective-permute-start(bf16[1,16,4096]{2,1,0:T(8,128)(2,1)S(1)} %get-tuple-element.163), channel_id=1, source_target_pairs={{0,2},{1,3},{2,0},{3,1},{4,6},{5,7},{6,4},{7,5},{8,10},{9,11},{10,... | collective-permute-start | bytes 393224 | tf_op jit(solution)/shard_map/ppermute | solution.py:674
  164.1 12.0 %collective-permute-start.23 = (bf16[1,16,4096]{2,1,0:T(8,128)(2,1)S(1)}, bf16[1,16,4096]{2,1,0:T(8,128)(2,1)S(1)}, u32[]{:S(2)}, u32[]{:S(2)}) collective-permute-start(bf16[1,16,4096]{2,1,0:T(8,128)(2,1)S(1)} %get-tuple-element.164), channel_id=1, source_target_pairs={{0,3},{1,2},{2,1},{3,0},{4,7},{5,6},{6,5},{7,4},{8,11},{9,10},{10,... | collective-permute-start | bytes 393224 | tf_op jit(solution)/shard_map/ppermute | solution.py:674
  177.0 15.0 %collective-permute-start.25 = (bf16[4,16,2176]{2,1,0:T(8,128)(2,1)S(1)}, bf16[4,16,2176]{2,1,0:T(8,128)(2,1)S(1)}, u32[]{:S(2)}, u32[]{:S(2)}) collective-permute-start(bf16[4,16,2176]{2,1,0:T(8,128)(2,1)S(1)} %get-tuple-element.168), channel_id=1, source_target_pairs={{0,8},{4,12},{8,0},{12,4},{16,24},{20,28},{24,16},{28,20},{1,9},{5... | collective-permute-start | bytes 835592 | tf_op jit(solution)/shard_map/ppermute | solution.py:674
  177.9 14.0 %collective-permute-start.24 = (bf16[4,16,2048]{2,1,0:T(8,128)(2,1)S(1)}, bf16[4,16,2048]{2,1,0:T(8,128)(2,1)S(1)}, u32[]{:S(2)}, u32[]{:S(2)}) collective-permute-start(bf16[4,16,2048]{2,1,0:T(8,128)(2,1)S(1)} %get-tuple-element.166), channel_id=1, source_target_pairs={{0,16},{4,20},{8,24},{12,28},{16,0},{20,4},{24,8},{28,12},{1,17},{... | collective-permute-start | bytes 786440 | tf_op jit(solution)/shard_map/ppermute | solution.py:674
  179.4 7.8 %collective-permute-start.28 = (bf16[1,16,4096]{2,1,0:T(8,128)(2,1)S(1)}, bf16[1,16,4096]{2,1,0:T(8,128)(2,1)S(1)}, u32[]{:S(2)}, u32[]{:S(2)}) collective-permute-start(bf16[1,16,4096]{2,1,0:T(8,128)(2,1)S(1)} %get-tuple-element.169.refs_4_), channel_id=1, source_target_pairs={{0,3},{1,2},{2,1},{3,0},{4,7},{5,6},{6,5},{7,4},{8,11},{9,10},{10,... | collective-permute-start | bytes 393224 | tf_op jit(solution)/shard_map/ppermute | solution.py:674
  180.8 11.1 %collective-permute-start.27 = (bf16[1,16,4096]{2,1,0:T(8,128)(2,1)S(1)}, bf16[1,16,4096]{2,1,0:T(8,128)(2,1)S(1)}, u32[]{:S(2)}, u32[]{:S(2)}) collective-permute-start(bf16[1,16,4096]{2,1,0:T(8,128)(2,1)S(1)} %get-tuple-element.169.refs_4_), channel_id=1, source_target_pairs={{0,2},{1,3},{2,0},{3,1},{4,6},{5,7},{6,4},{7,5},{8,10},{9,11},{10,... | collective-permute-start | bytes 393224 | tf_op jit(solution)/shard_map/ppermute | solution.py:674
  182.8 9.1 %collective-permute-start.26 = (bf16[1,16,4096]{2,1,0:T(8,128)(2,1)S(1)}, bf16[1,16,4096]{2,1,0:T(8,128)(2,1)S(1)}, u32[]{:S(2)}, u32[]{:S(2)}) collective-permute-start(bf16[1,16,4096]{2,1,0:T(8,128)(2,1)S(1)} %get-tuple-element.169.refs_4_), channel_id=1, source_target_pairs={{0,1},{1,0},{2,3},{3,2},{4,5},{5,4},{6,7},{7,6},{8,9},{9,8},{10,11... | collective-permute-start | bytes 393224 | tf_op jit(solution)/shard_map/ppermute | solution.py:674
  192.0 13.8 %collective-permute-start.32 = (bf16[4,16,2048]{2,1,0:T(8,128)(2,1)S(1)}, bf16[4,16,2048]{2,1,0:T(8,128)(2,1)S(1)}, u32[]{:S(2)}, u32[]{:S(2)}) collective-permute-start(bf16[4,16,2048]{2,1,0:T(8,128)(2,1)S(1)} %get-tuple-element.174.refs_5_), channel_id=1, source_target_pairs={{0,16},{4,20},{8,24},{12,28},{16,0},{20,4},{24,8},{28,12},{1,17},{... | collective-permute-start | bytes 786440 | tf_op jit(solution)/shard_map/ppermute | solution.py:674
  192.9 12.9 %collective-permute-start.33 = (bf16[4,16,2048]{2,1,0:T(8,128)(2,1)S(1)}, bf16[4,16,2048]{2,1,0:T(8,128)(2,1)S(1)}, u32[]{:S(2)}, u32[]{:S(2)}) collective-permute-start(bf16[4,16,2048]{2,1,0:T(8,128)(2,1)S(1)} %get-tuple-element.175.refs_7_), channel_id=1, source_target_pairs={{0,8},{4,12},{8,0},{12,4},{16,24},{20,28},{24,16},{28,20},{1,9},{5... | collective-permute-start | bytes 786440 | tf_op jit(solution)/shard_map/ppermute | solution.py:674
  193.4 12.4 %collective-permute-start.30 = (bf16[1,16,4224]{2,1,0:T(8,128)(2,1)S(1)}, bf16[1,16,4224]{2,1,0:T(8,128)(2,1)S(1)}, u32[]{:S(2)}, u32[]{:S(2)}) collective-permute-start(bf16[1,16,4224]{2,1,0:T(8,128)(2,1)S(1)} %get-tuple-element.172), channel_id=1, source_target_pairs={{0,2},{1,3},{2,0},{3,1},{4,6},{5,7},{6,4},{7,5},{8,10},{9,11},{10,... | collective-permute-start | bytes 405512 | tf_op jit(solution)/shard_map/ppermute | solution.py:674
  195.6 10.2 %collective-permute-start.31 = (bf16[1,16,4224]{2,1,0:T(8,128)(2,1)S(1)}, bf16[1,16,4224]{2,1,0:T(8,128)(2,1)S(1)}, u32[]{:S(2)}, u32[]{:S(2)}) collective-permute-start(bf16[1,16,4224]{2,1,0:T(8,128)(2,1)S(1)} %get-tuple-element.173), channel_id=1, source_target_pairs={{0,3},{1,2},{2,1},{3,0},{4,7},{5,6},{6,5},{7,4},{8,11},{9,10},{10,... | collective-permute-start | bytes 405512 | tf_op jit(solution)/shard_map/ppermute | solution.py:674
  206.0 14.4 %collective-permute-start.37 = (bf16[8,16,2048]{2,1,0:T(8,128)(2,1)S(1)}, bf16[8,16,2048]{2,1,0:T(8,128)(2,1)S(1)}, u32[]{:S(2)}, u32[]{:S(2)}) collective-permute-start(bf16[8,16,2048]{2,1,0:T(8,128)(2,1)S(1)} %get-tuple-element.177.refs_4_), channel_id=1, source_target_pairs={{0,8},{4,12},{8,0},{12,4},{16,24},{20,28},{24,16},{28,20},{1,9},{5... | collective-permute-start | bytes 1572872 | tf_op jit(solution)/shard_map/ppermute | solution.py:674
  207.8 12.6 %collective-permute-start.38 = (bf16[8,16,2048]{2,1,0:T(8,128)(2,1)S(1)}, bf16[8,16,2048]{2,1,0:T(8,128)(2,1)S(1)}, u32[]{:S(2)}, u32[]{:S(2)}) collective-permute-start(bf16[8,16,2048]{2,1,0:T(8,128)(2,1)S(1)} %get-tuple-element.178.refs_6_), channel_id=1, source_target_pairs={{0,16},{4,20},{8,24},{12,28},{16,0},{20,4},{24,8},{28,12},{1,17},{... | collective-permute-start | bytes 1572872 | tf_op jit(solution)/shard_map/ppermute | solution.py:674
  208.7 7.5 %collective-permute-start.36 = (bf16[1,16,4224]{2,1,0:T(8,128)(2,1)S(1)}, bf16[1,16,4224]{2,1,0:T(8,128)(2,1)S(1)}, u32[]{:S(2)}, u32[]{:S(2)}) collective-permute-start(bf16[1,16,4224]{2,1,0:T(8,128)(2,1)S(1)} %get-tuple-element.176.refs_0_), channel_id=1, source_target_pairs={{0,3},{1,2},{2,1},{3,0},{4,7},{5,6},{6,5},{7,4},{8,11},{9,10},{10,... | collective-permute-start | bytes 405512 | tf_op jit(solution)/shard_map/ppermute | solution.py:674
  210.1 10.2 %collective-permute-start.35 = (bf16[1,16,4224]{2,1,0:T(8,128)(2,1)S(1)}, bf16[1,16,4224]{2,1,0:T(8,128)(2,1)S(1)}, u32[]{:S(2)}, u32[]{:S(2)}) collective-permute-start(bf16[1,16,4224]{2,1,0:T(8,128)(2,1)S(1)} %get-tuple-element.176.refs_0_), channel_id=1, source_target_pairs={{0,2},{1,3},{2,0},{3,1},{4,6},{5,7},{6,4},{7,5},{8,10},{9,11},{10,... | collective-permute-start | bytes 405512 | tf_op jit(solution)/shard_map/ppermute | solution.py:674
  212.1 8.2 %collective-permute-start.34 = (bf16[1,16,4224]{2,1,0:T(8,128)(2,1)S(1)}, bf16[1,16,4224]{2,1,0:T(8,128)(2,1)S(1)}, u32[]{:S(2)}, u32[]{:S(2)}) collective-permute-start(bf16[1,16,4224]{2,1,0:T(8,128)(2,1)S(1)} %get-tuple-element.176.refs_0_), channel_id=1, source_target_pairs={{0,1},{1,0},{2,3},{3,2},{4,5},{5,4},{6,7},{7,6},{8,9},{9,8},{10,11... | collective-permute-start | bytes 405512 | tf_op jit(solution)/shard_map/ppermute | solution.py:674
  220.5 17.1 %collective-permute-start.41 = (bf16[16,16,4096]{2,1,0:T(8,128)(2,1)S(1)}, bf16[16,16,4096]{2,1,0:T(8,128)(2,1)S(1)}, u32[]{:S(2)}, u32[]{:S(2)}) collective-permute-start(bf16[16,16,4096]{2,1,0:T(8,128)(2,1)S(1)} %get-tuple-element.181.refs_0_), channel_id=1, source_target_pairs={{0,4},{4,0},{8,12},{12,8},{16,20},{20,16},{24,28},{28,24},{1,5},{5... | collective-permute-start | bytes 6291464 | tf_op jit(solution)/shard_map/ppermute | solution.py:674
  220.6 17.0 %collective-permute-start.40 = (bf16[4,16,2176]{2,1,0:T(8,128)(2,1)S(1)}, bf16[4,16,2176]{2,1,0:T(8,128)(2,1)S(1)}, u32[]{:S(2)}, u32[]{:S(2)}) collective-permute-start(bf16[4,16,2176]{2,1,0:T(8,128)(2,1)S(1)} %get-tuple-element.180.refs_2_), channel_id=1, source_target_pairs={{0,8},{4,12},{8,0},{12,4},{16,24},{20,28},{24,16},{28,20},{1,9},{5... | collective-permute-start | bytes 835592 | tf_op jit(solution)/shard_map/ppermute | solution.py:674
  221.8 11.0 %collective-permute-start.42 = (bf16[256,512]{1,0:T(8,128)(2,1)S(1)}, bf16[256,512]{1,0:T(8,128)(2,1)S(1)}, u32[]{:S(2)}, u32[]{:S(2)}) collective-permute-start(bf16[256,512]{1,0:T(8,128)(2,1)S(1)} %get-tuple-element.185), channel_id=1, source_target_pairs={{1,0},{2,1},{3,2},{5,4},{6,5},{7,6},{9,8},{10,9},{11,10},{13,12},{... | collective-permute-start | bytes 786440 | tf_op jit(solution)/shard_map/ppermute | solution.py:631
  223.0 14.6 %collective-permute-start.43 = (bf16[256,512]{1,0:T(8,128)(2,1)S(1)}, bf16[256,512]{1,0:T(8,128)(2,1)S(1)}, u32[]{:S(2)}, u32[]{:S(2)}) collective-permute-start(bf16[256,512]{1,0:T(8,128)(2,1)S(1)} %get-tuple-element.186.refs_9_), channel_id=1, source_target_pairs={{1,0},{3,2},{5,4},{7,6},{9,8},{11,10},{13,12},{15,14},{17,16},{19,... | collective-permute-start | bytes 786440 | tf_op jit(solution)/shard_map/ppermute | solution.py:636
  224.3 13.3 %collective-permute-start.39 = (bf16[4,16,2048]{2,1,0:T(8,128)(2,1)S(1)}, bf16[4,16,2048]{2,1,0:T(8,128)(2,1)S(1)}, u32[]{:S(2)}, u32[]{:S(2)}) collective-permute-start(bf16[4,16,2048]{2,1,0:T(8,128)(2,1)S(1)} %get-tuple-element.179.refs_0_), channel_id=1, source_target_pairs={{0,16},{4,20},{8,24},{12,28},{16,0},{20,4},{24,8},{28,12},{1,17},{... | collective-permute-start | bytes 786440 | tf_op jit(solution)/shard_map/ppermute | solution.py:674
  237.8 15.1 %collective-permute-start.46 = (bf16[256,512]{1,0:T(8,128)(2,1)S(1)}, bf16[256,512]{1,0:T(8,128)(2,1)S(1)}, u32[]{:S(2)}, u32[]{:S(2)}) collective-permute-start(bf16[256,512]{1,0:T(8,128)(2,1)S(1)} %get-tuple-element.191), channel_id=1, source_target_pairs={{1,0},{2,1},{3,2},{5,4},{6,5},{7,6},{9,8},{10,9},{11,10},{13,12},{... | collective-permute-start | bytes 786440 | tf_op jit(solution)/shard_map/ppermute | solution.py:631
  239.1 13.8 %collective-permute-start.47 = (bf16[256,512]{1,0:T(8,128)(2,1)S(1)}, bf16[256,512]{1,0:T(8,128)(2,1)S(1)}, u32[]{:S(2)}, u32[]{:S(2)}) collective-permute-start(bf16[256,512]{1,0:T(8,128)(2,1)S(1)} %get-tuple-element.192.refs_9_), channel_id=1, source_target_pairs={{2,0},{6,4},{10,8},{14,12},{18,16},{22,20},{26,24},{30,28}} | collective-permute-start | bytes 786440 | tf_op jit(solution)/shard_map/ppermute | solution.py:636
  240.4 13.2 %collective-permute-start.44 = (bf16[8,16,2048]{2,1,0:T(8,128)(2,1)S(1)}, bf16[8,16,2048]{2,1,0:T(8,128)(2,1)S(1)}, u32[]{:S(2)}, u32[]{:S(2)}) collective-permute-start(bf16[8,16,2048]{2,1,0:T(8,128)(2,1)S(1)} %get-tuple-element.187.refs_0_), channel_id=1, source_target_pairs={{0,8},{4,12},{8,0},{12,4},{16,24},{20,28},{24,16},{28,20},{1,9},{5... | collective-permute-start | bytes 1572872 | tf_op jit(solution)/shard_map/ppermute | solution.py:674
  241.5 13.6 %collective-permute-start.45 = (bf16[8,16,2176]{2,1,0:T(8,128)(2,1)S(1)}, bf16[8,16,2176]{2,1,0:T(8,128)(2,1)S(1)}, u32[]{:S(2)}, u32[]{:S(2)}) collective-permute-start(bf16[8,16,2176]{2,1,0:T(8,128)(2,1)S(1)} %get-tuple-element.188.refs_2_), channel_id=1, source_target_pairs={{0,16},{4,20},{8,24},{12,28},{16,0},{20,4},{24,8},{28,12},{1,17},{... | collective-permute-start | bytes 1671176 | tf_op jit(solution)/shard_map/ppermute | solution.py:674
  255.3 13.3 %collective-permute-start.49 = (bf16[16,16,4224]{2,1,0:T(8,128)(2,1)S(1)}, bf16[16,16,4224]{2,1,0:T(8,128)(2,1)S(1)}, u32[]{:S(2)}, u32[]{:S(2)}) collective-permute-start(bf16[16,16,4224]{2,1,0:T(8,128)(2,1)S(1)} %get-tuple-element.199.refs_0_), channel_id=1, source_target_pairs={{0,4},{4,0},{8,12},{12,8},{16,20},{20,16},{24,28},{28,24},{1,5},{5... | collective-permute-start | bytes 6488072 | tf_op jit(solution)/shard_map/ppermute | solution.py:674
  255.4 10.6 %collective-permute-start.48 = (bf16[256,512]{1,0:T(8,128)(2,1)S(1)}, bf16[256,512]{1,0:T(8,128)(2,1)S(1)}, u32[]{:S(2)}, u32[]{:S(2)}) collective-permute-start(bf16[256,512]{1,0:T(8,128)(2,1)S(1)} %get-tuple-element.193), channel_id=1, source_target_pairs={{1,0},{2,1},{3,2},{5,4},{6,5},{7,6},{9,8},{10,9},{11,10},{13,12},{... | collective-permute-start | bytes 786440 | tf_op jit(solution)/shard_map/ppermute | solution.py:631
  (38 other events, 435.8 us)
where the time goes:
time: 273 us
  waiting for transfers between devices  94.5 us (35%)
  Pallas kernels  76.5 us (28%)
  starting transfers between devices  75.1 us (28%)
  local copies, waits for them, and re-layouts  19.4 us (7%)
  other arithmetic  4.66 us (2%)
    pallas_call x17, Pallas kernels, call(): pl.pallas_call(kernel, out_shape=[jax.ShapeDtypeStruct(s, t) for s, t in...  76.5 us
    ppermute x32, waiting for transfers between devices, trade(): lax.ppermute(v, axis, [(i, i ^ distance) for i in range(lax.axis_size(axi...  39.5 us
    ppermute x32, starting transfers between devices, trade(): lax.ppermute(v, axis, [(i, i ^ distance) for i in range(lax.axis_size(axi...  35.8 us
    ppermute x6, waiting for transfers between devices, return_long(): return lax.ppermute(block, 'blk', pairs)  23.7 us
    ppermute x6, starting transfers between devices, send_long(): got.append(lax.ppermute(block, 'blk', pairs))  17.5 us
    unnamed x72, local copies, waits for them, and re-layouts  17.4 us
    ppermute x6, waiting for transfers between devices, send_long(): got.append(lax.ppermute(block, 'blk', pairs))  16.8 us
    ppermute x3, waiting for transfers between devices, return_short(): return lax.ppermute(held, 'blk', pairs)  9.1 us
  transfers between devices with their start and end apart: 50, of which 24 were waited for; matrix products, arithmetic and copies ran while one was open for 1% of the time, Pallas kernels for 17%

commit v1 on v0

--- a/solution.py
+++ b/solution.py
@@ -160,9 +160,16 @@
         done(pair)
 
 
-def columns_copy(source, target, sem, place, wide):
-    at = columns(place, wide)
-    return pltpu.make_async_copy(source.at[:, at], target.at[:, at], sem)
+def saves(kv, p, kept, sems):
+    rows, width = slice(0, kv.shape[0]), kv.shape[1]
+    wide = 2 * PAIR * p.shape[1] // width
+
+    def p_save(pair):
+        at = pl.ds(pl.multiple_of(width + pair * wide, PAIR), wide)
+        return pltpu.make_async_copy(p.at[:, columns(pair, wide)], kept.at[rows, at], sems.at[pair])
+
+    pairs = width // (2 * PAIR)
+    return pltpu.make_async_copy(kv, kept.at[rows, :width], sems.at[pairs]), p_save
 
 
 def plan_of(n):
@@ -177,18 +184,26 @@
         out[j] = total
 
 
+def pick_kernel(lengths, x, enc, x_long, e_long, *shorts):
+    rows = x_long.shape[0]
+    long = jnp.where(lengths[1] > lengths[0], 1, 0)
+    x_long[...] = x[long]
+    e_long[...] = enc[long]
+    for root, ref in enumerate(shorts):
+        share = (lax.axis_index("blk") == root).astype(jnp.int32).astype(WIDE)
+        ref[:rows] = (x[1 - long].astype(WIDE) * share).astype(LOW)
+        ref[rows:] = (enc[1 - long].astype(WIDE) * share).astype(LOW)
+
+
 def self_kernel(n, terms, order, rank, x, *refs):
     xl, refs = refs[: n - 1], refs[n - 1 :]
     shorts, refs = refs[: terms * (n // 4)], refs[terms * (n // 4) :]
     (
         w_in, w_out, w_cq, gains, shifts,
-        q, kv_far, p_far, mixed, inverse, after, cq, n1, xs, kv, p, sems,
+        q, kept, mixed, inverse, after, cq, n1, xs, kv, p, sems,
     ) = refs
     pairs = q.shape[1] // PAIR
-    kv_save = pltpu.make_async_copy(kv, kv_far, sems.at[pairs])
-
-    def p_save(pair):
-        return columns_copy(p, p_far, sems.at[pair], pair, p.shape[1] // pairs)
+    kv_save, p_save = saves(kv, p, kept, sems)
     add_terms(xs, shorts, terms)
     rows, width = x.shape[1:]
     r = rank[0]
@@ -233,12 +248,9 @@
 def cross_kernel(n, terms, order, rank, breaks, enc, *refs):
     el, refs = refs[: n - 1], refs[n - 1 :]
     shorts, refs = refs[: terms * (n // 4)], refs[terms * (n // 4) :]
-    cq, after, w_cm, w_out, kv_far, p_far, mixed, inverse, crossed, es, kv, p, sems = refs
+    cq, after, w_cm, w_out, kept, mixed, inverse, crossed, es, kv, p, sems = refs
     pairs = cq.shape[1] // PAIR
-    kv_save = pltpu.make_async_copy(kv, kv_far, sems.at[pairs])
-
-    def p_save(pair):
-        return columns_copy(p, p_far, sems.at[pair], pair, p.shape[1] // pairs)
+    kv_save, p_save = saves(kv, p, kept, sems)
     add_terms(es, shorts, terms)
     rows, width = enc.shape[1:]
     r = rank[0]
@@ -330,18 +342,21 @@
         save.wait()
 
 
-def loads(kv_far, p_far, kv, p, sems):
-    pairs = kv.shape[1] // (2 * PAIR)
+def loads(kept, kv, p, sems):
+    rows, width, wide = slice(0, kv.shape[0]), kv.shape[1], p.shape[2]
+    pairs = width // (2 * PAIR)
 
     def p_copy(pair):
-        at = columns(pair, p.shape[2])
-        return pltpu.make_async_copy(p_far.at[:, at], p.at[lax.rem(pair, 2)], sems.at[pair])
+        at = pl.ds(pl.multiple_of(width + pair * wide, PAIR), wide)
+        return pltpu.make_async_copy(kept.at[rows, at], p.at[lax.rem(pair, 2)], sems.at[pair])
 
     def kv_copies(pair):
-        return (
-            columns_copy(kv_far, kv, sems.at[pairs + pair], pair, PAIR),
-            columns_copy(kv_far, kv, sems.at[2 * pairs + pair], pairs + pair, PAIR),
-        )
+        return [
+            pltpu.make_async_copy(
+                kept.at[rows, columns(i, PAIR)], kv.at[:, columns(i, PAIR)], sems.at[pairs + i]
+            )
+            for i in (pair, pairs + pair)
+        ]
 
     for pair in range(pairs):
         if pair < 2:
@@ -371,9 +386,9 @@
 
 def cross_back_kernel(n, order, enc, *refs):
     el, es, refs = refs[: n - 1], refs[n - 1], refs[n:]
-    (grad, mixed, inverse, cq, kv_far, p_far, after, n1, w_cm, w_cout, w_cq, gains) = refs[:12]
-    parts, (self_grad, g_cross, g_small, dq, up, dkv, kv, p, sems) = refs[12:-9], refs[-9:]
-    ready, done = loads(kv_far, p_far, kv, p, sems)
+    (grad, mixed, inverse, cq, kept, after, n1, w_cm, w_cout, w_cq, gains) = refs[:11]
+    parts, (self_grad, g_cross, g_small, dq, up, dkv, kv, p, sems) = refs[11:-9], refs[-9:]
+    ready, done = loads(kept, kv, p, sems)
     rows, width = enc.shape[1:]
     low = grad[...].astype(LOW)
     g_cross[:, 3 * width :] = tn(mixed[...], low).astype(LOW)
@@ -398,11 +413,11 @@
 def self_back_kernel(n, order, codes, x, *refs):
     xl, refs = refs[: n - 1], refs[n - 1 :]
     (
-        xs, self_grad, mixed, inverse, q, kv_far, p_far, w_in, w_out, gains, shifts, small_feed, g_bias,
+        xs, self_grad, mixed, inverse, q, kept, w_in, w_out, gains, shifts, small_feed, g_bias,
         small_cross, g_cross, _,
-    ) = refs[:16]
-    parts, (own, near, far, sums, dq, up, dkv, kv, p, sems) = refs[16:-10], refs[-10:]
-    ready, done = loads(kv_far, p_far, kv, p, sems)
+    ) = refs[:15]
+    parts, (own, near, far, sums, dq, up, dkv, kv, p, sems) = refs[15:-10], refs[-10:]
+    ready, done = loads(kept, kv, p, sems)
     rows, width = x.shape[1:]
     low = self_grad[...].astype(LOW)
     up[...] = nt(low, w_out[...]).astype(LOW)
@@ -647,12 +662,11 @@
     return got
 
 
-def send_short_first(block, n, rank):
-    got = []
-    for root in range(n // 4):
-        held = jnp.where(rank == root, block, jnp.zeros_like(block))
-        got.append([held, lax.ppermute(held, "blk", [(root, (root + n // 2) % n)])])
-    return got
+def send_short_first(shorts, n):
+    return [
+        [held, lax.ppermute(held, "blk", [(root, (root + n // 2) % n)])]
+        for root, held in enumerate(shorts)
+    ]
 
 
 def send_short_rest(terms, n):
@@ -717,53 +731,59 @@
     nk = (n + n // 4) * rows
     pairs = width // PAIR
 
-    def pick(v, i):
-        return jnp.where(order[i] == 0, v[0], v[1])
-
     sharing = Sharing(lax.axis_size("batch"), n)
     codes = sharing.codes()
     chunks = sharing.chunks
     tall = width // chunks
     blocks = nk // rows
 
-    room = 62 if n > 4 else 40
-    x_long, x_short = pick(decoder_input, 0), pick(decoder_input, 1)
-    e_long, e_short = pick(encoder_output, 0), pick(encoder_output, 1)
-    firsts = send_short_first(jnp.concatenate([x_short, e_short]), n, rank)
+    room = 62 if n > 4 else 22
+    block = ((rows, width), LOW)
+    x_long, e_long, *shorts = call(
+        pick_kernel,
+        (sequence_lengths, decoder_input, encoder_output),
+        [block, block] + [((both, width), LOW)] * (n // 4),
+        1,
+        smem=1,
+        room=60,
+    )
+    firsts = send_short_first(shorts, n)
     xl = send_long(x_long, n, False)
     xs = send_short_rest([[v[:rows] for v in terms] for terms in firsts], n)
     shorts = len(xs) // (n // 4)
-    e_long = tied(e_long, *xl)
+    e_long = tied(e_long, *[terms[1] for terms in firsts])
     es = send_short_rest([[tied(v[rows:], *xl) for v in terms] for terms in firsts], n)
     el = send_long(e_long, n, True)
 
-    kept = [((nk, 2 * width), LOW), ((nk, pairs * both), LOW)]
-    loaded = [kept[0], ((2, nk, both), LOW)]
+    pair_rows = ((nk, 2 * width), LOW)
+    saved = [pair_rows, ((nk, pairs * both), LOW)]
+    loaded = [pair_rows, ((2, nk, both), LOW)]
+    kept_shape = ((nk * (9 if n == 4 else 1), 2 * width + pairs * both), LOW)
     inverses = ((2 * pairs, both), WIDE)
     low_rows, wide_rows = ((both, width), LOW), ((both, width), WIDE)
-    q, kv, p, mixed, inverse, after, cq, n1, xs = call(
+    q, kept, mixed, inverse, after, cq, n1, xs = call(
         functools.partial(self_kernel, n, shorts),
         (order, ranks, decoder_input, *xl, *xs, self_inward, self_outward, cross_query,
          norm_gains, norm_shifts),
-        [low_rows, *kept, low_rows, inverses, wide_rows, low_rows, low_rows,
+        [low_rows, kept_shape, low_rows, inverses, wide_rows, low_rows, low_rows,
          ((n // 4, rows, width), LOW)],
         12,
-        scratch=kept,
+        scratch=saved,
         smem=2,
         room=room,
-        far_outs=(1, 2),
+        far_outs=(1,),
         sems=pairs + 1,
     )
-    ckv, cp, cmixed, cinverse, crossed, es = call(
+    cross_kept, cmixed, cinverse, crossed, es = call(
         functools.partial(cross_kernel, n, shorts),
         (order, ranks, chain_breaks, encoder_output, *el, *es, cq, after, cross_memory,
          cross_outward),
-        [*kept, low_rows, inverses, wide_rows, ((n // 4, rows, width), LOW)],
+        [kept_shape, low_rows, inverses, wide_rows, ((n // 4, rows, width), LOW)],
         11,
-        scratch=kept,
+        scratch=saved,
         smem=3,
         room=room,
-        far_outs=(0, 1),
+        far_outs=(0,),
         sems=pairs + 1,
     )
     half = chunks // 2
@@ -794,13 +814,13 @@
     *e_parts, self_grad, g_cross, small_cross = call(
         functools.partial(cross_back_kernel, n),
         (order, encoder_output, *el, es, cross_grad, cmixed, cinverse,
-         cq, ckv, cp, after, n1, cross_memory, cross_outward, cross_query, norm_gains),
+         cq, cross_kept, after, n1, cross_memory, cross_outward, cross_query, norm_gains),
         part_shapes + [((both, width), WIDE), ((width, 4 * width), LOW), ((2, width), WIDE)],
         14,
-        scratch=[low_rows, low_rows, kept[0], *loaded],
+        scratch=[low_rows, low_rows, pair_rows, *loaded],
         smem=1,
         room=room,
-        far_ins=(n + 6, n + 7),
+        far_ins=(n + 6,),
         sems=3 * pairs,
     )
     (a, a_send, b, b_send), _ = small_steps(
@@ -811,16 +831,16 @@
     e_got = [return_long(e_parts[d], n, d, True) for d in range(1, n)]
     *parts, own, near, far = call(
         functools.partial(self_back_kernel, n),
-        (order, codes, decoder_input, *xl, xs, self_grad, mixed, inverse, q, kv, p, self_inward,
+        (order, codes, decoder_input, *xl, xs, self_grad, mixed, inverse, q, kept, self_inward,
          self_outward, norm_gains, norm_shifts, small_feed, g_bias, small_cross, g_cross, a),
         [((rows, width), LOW)] * blocks
         + [((both, width), WIDE), (shape(half, sum(wide_rest)), LOW),
            (shape(half, sum(wide_rest)), LOW)],
         16,
-        scratch=[(shape(chunks, sum(wide_rest)), LOW), low_rows, low_rows, kept[0], *loaded],
+        scratch=[(shape(chunks, sum(wide_rest)), LOW), low_rows, low_rows, pair_rows, *loaded],
         smem=2,
         room=room,
-        far_ins=(n + 7, n + 8),
+        far_ins=(n + 7,),
         far_outs=(blocks + 1, blocks + 2),
         sems=3 * pairs,
     )
@@ -832,10 +852,15 @@
     )
     a_got, b_got = trade(a_send, "batch", 4), trade(b_send, "batch", 2)
     e_got = [return_short(e_short[k], n, k, 2) for k in roots]
-    feed, (a, a_send, b, b_send), *e_short = small_steps(
+    held = tied(parts[n - 1], a_send)
+    for d in range(n - 2, 2, -1):
+        held = parts[d] + return_long(held, n, 1, False)
+    long_got = return_long(held, n, 1, False)
+    feed, (a, a_send, b, b_send), (held,), *e_short = small_steps(
         [(add_to_pieces, (a, a_got, b, b_got), [shape(1, sum(wide))] * 4),
          (add_core, (near, trade(tied(far, a_send), "batch", 1)),
-          [shape(8, w) for w in wide_rest for _ in "ks"])]
+          [shape(8, w) for w in wide_rest for _ in "ks"]),
+         (add_all, (own, parts[2], long_got), [(rows, width)])]
         + [(add_all, (own, e_short[k], e_got[k]), [(rows, width)]) for k in roots]
     )
     e_short = return_short_rest([v for v, in e_short], n)
@@ -864,16 +889,14 @@
     )
     ra_got, rb_got = trade(ra, "batch", 4), trade(rb, "batch", 2)
     feed_got = trade(feed, "batch", 1)
-    held, *shorts = tied((parts[n - 1], *parts[n:]), ra)
-    for d in range(n - 2, 2, -1):
-        held = parts[d] + return_long(held, n, 1, False)
+    held, *shorts = tied((held, *parts[n:]), ra)
     long_got = return_long(held, n, 1, False)
     got = [return_short(shorts[k], n, k, 1) for k in roots]
     (ra,), (rb,), _, (held,), *shorts = small_steps(
         [(join, (ra, ra_got), [shape(8, wide_rest[0])]),
          (join, (rb, rb_got), [shape(8, wide_rest[1])]),
          (note, (feed_got,), []),
-         (add_all, (own, parts[2], long_got), [(rows, width)])]
+         (add_all, (own, parts[1], long_got), [(rows, width)])]
         + [(add_all, (own, parts[n + k], got[k]), [(rows, width)]) for k in roots]
     )
     ra_got, rb_got = trade(ra, "batch", 2), trade(rb, "batch", 4)
@@ -887,14 +910,12 @@
         smem=1,
         room=room,
     )
-    (rest,), _, (held,), *shorts = small_steps(
+    (rest,), _, *shorts = small_steps(
         [(beside, (ra, ra_got, rb, rb_got), [shape(16, sum(wide_rest))]),
-         (note, (s_down[:8, :128],), []),
-         (add_all, (own, parts[1], long_got), [(rows, width)])]
+         (note, (s_down[:8, :128], long_got), [])]
         + [(add_all, (own, shorts[k][0], got[k]), [(rows, width)]) for k in roots]
     )
     shorts = return_short_rest([v for v, in shorts], n)
-    long_got = return_long(held, n, 1, False)
     rest_got = trade(rest, "batch", 1)
     input_gradient, encoder_gradient = call(
         functools.partial(last_kernel, n),

time: 273 us -> 255 us (0.934)
  local copies, waits for them, and re-layouts: 19.4 us -> 4.29 us
  waiting for transfers between devices: 94.5 us -> 82 us
  starting transfers between devices: 75.1 us -> 86.1 us
    ppermute x6, waiting for transfers between devices: 16.8 us -> 1.85 us  [send_long(): got.append(lax.ppermute(block, 'blk', pairs))]
    unnamed x72 -> x38, local copies, waits for them, and re-layouts: 17.4 us -> 3.01 us
    ppermute x3, waiting for transfers between devices: 9.1 us -> 15.8 us  [return_short(): return lax.ppermute(held, 'blk', pairs)]
    ppermute x2, starting transfers between devices: 3.91 us -> 10.4 us  [send_short_rest(): terms[root].append(lax.ppermute(held, 'blk', pairs))]
    ppermute x32, waiting for transfers between devices: 39.5 us -> 34.6 us  [trade(): lax.ppermute(v, axis, [(i, i ^ distance) for i in range(lax.axis_size(axi...]
    ppermute x2, waiting for transfers between devices: 0.01 us -> 3.83 us  [send_short_rest(): terms[root].append(lax.ppermute(held, 'blk', pairs))]
    ppermute x6, waiting for transfers between devices: 23.7 us -> 19.9 us  [return_long(): return lax.ppermute(block, 'blk', pairs)]
    select_n x3 -> x0, other arithmetic: 3.65 us -> none  [the longest x2 3.56 us: pick(): return jnp.where(order[i] == 0, v[0], v[1])]
  transfers between devices with their start and end apart: 50 -> 50, of which waited for: 24 -> 21; matrix products, arithmetic and copies ran while one was open for 1% -> 1% of each run, Pallas kernels for 17% -> 18%
where the time goes in v1:
time: 255 us
  starting transfers between devices  86.1 us (34%)
  waiting for transfers between devices  82 us (32%)
  Pallas kernels  77.8 us (31%)
  local copies, waits for them, and re-layouts  4.29 us (2%)
    pallas_call x18, Pallas kernels, call(): pl.pallas_call(kernel, out_shape=[jax.ShapeDtypeStruct(s, t) for s, t in...  77.8 us
    ppermute x32, starting transfers between devices, trade(): lax.ppermute(v, axis, [(i, i ^ distance) for i in range(lax.axis_size(axi...  38.1 us
    ppermute x32, waiting for transfers between devices, trade(): lax.ppermute(v, axis, [(i, i ^ distance) for i in range(lax.axis_size(axi...  34.6 us
    ppermute x6, waiting for transfers between devices, return_long(): return lax.ppermute(block, 'blk', pairs)  19.9 us
    ppermute x6, starting transfers between devices, send_long(): got.append(lax.ppermute(block, 'blk', pairs))  16.1 us
    ppermute x3, waiting for transfers between devices, return_short(): return lax.ppermute(held, 'blk', pairs)  15.8 us
    ppermute x6, starting transfers between devices, return_long(): return lax.ppermute(block, 'blk', pairs)  11.1 us
    ppermute x2, starting transfers between devices, send_short_rest(): terms[root].append(lax.ppermute(held, 'blk', pairs))  10.4 us
  transfers between devices with their start and end apart: 50, of which 21 were waited for; matrix products, arithmetic and copies ran while one was open for 1% of the time, Pallas kernels for 18%

profile of v1, /device:TPU:0, one launch (start us, length us, event | category | flops | bytes accessed | tf_op | source)
XLA Modules:
  0.0 254.8 jit_solution(2464725175544047698)
XLA Ops:
  0.7 2.2 shard_map.263
  2.9 6.2 %collective-permute-start = (bf16[512,512]{1,0:T(8,128)(2,1)}, bf16[512,512]{1,0:T(8,128)(2,1)S(1)}, u32[]{:S(2)}, u32[]{:S(2)}) collective-permute-start(bf16[512,512]{1,0:T(8,128)(2,1)} %get-tuple-element.115), channel_id=1, source_target_pairs={{0,2},{4,6},{8,10},{12,14},{16,18},{20,22},{24,26},{28,30}} | collective-permute-start | bytes 1572872 | tf_op jit(solution)/shard_map/ppermute | solution.py:667
  9.2 1.6 collective-permute-start.6
  10.8 2.0 collective-permute-start.5
  12.8 3.2 %collective-permute-start.4 = (bf16[256,512]{1,0:T(8,128)(2,1)}, bf16[256,512]{1,0:T(8,128)(2,1)}, u32[]{:S(2)}, u32[]{:S(2)}) collective-permute-start(bf16[256,512]{1,0:T(8,128)(2,1)} %get-tuple-element.117), channel_id=1, source_target_pairs={{0,1},{1,2},{2,3},{4,5},{5,6},{6,7},{8,9},{9,10},{10,11},{12,13},{... | collective-permute-start | bytes 786440 | tf_op jit(solution)/shard_map/ppermute | solution.py:640
  16.0 5.9 %collective-permute-done = bf16[512,512]{1,0:T(8,128)(2,1)S(1)} collective-permute-done((bf16[512,512]{1,0:T(8,128)(2,1)}, bf16[512,512]{1,0:T(8,128)(2,1)S(1)}, u32[]{:S(2)}, u32[]{:S(2)}) %collective-permute-start) | collective-permute-done | bytes 524320 | tf_op jit(solution)/shard_map/ppermute | solution.py:667
  21.8 1.9 slice_add_fusion
  23.7 2.0 collective-permute-start.8
  27.8 3.4 %collective-permute-start.2 = (bf16[256,512]{1,0:T(8,128)(2,1)}, bf16[256,512]{1,0:T(8,128)(2,1)S(1)}, u32[]{:S(2)}, u32[]{:S(2)}) collective-permute-start(bf16[256,512]{1,0:T(8,128)(2,1)} %get-tuple-element.116), channel_id=1, source_target_pairs={{0,2},{1,3},{2,0},{3,1},{4,6},{5,7},{6,4},{7,5},{8,10},{9,11},{10,... | collective-permute-start | bytes 786440 | tf_op jit(solution)/shard_map/ppermute | solution.py:640
  31.2 1.8 collective-permute-done.5.refs_1_
  33.1 6.0 %collective-permute-start.1 = (bf16[256,512]{1,0:T(8,128)(2,1)}, bf16[256,512]{1,0:T(8,128)(2,1)S(1)}, u32[]{:S(2)}, u32[]{:S(2)}) collective-permute-start(bf16[256,512]{1,0:T(8,128)(2,1)} %get-tuple-element.116), channel_id=1, source_target_pairs={{0,1},{1,2},{2,3},{3,0},{4,5},{5,6},{6,7},{7,4},{8,9},{9,10},{10,1... | collective-permute-start | bytes 786440 | tf_op jit(solution)/shard_map/ppermute | solution.py:640
  39.1 8.4 %collective-permute-start.7 = (bf16[256,512]{1,0:T(8,128)(2,1)S(1)}, bf16[256,512]{1,0:T(8,128)(2,1)S(1)}, u32[]{:S(2)}, u32[]{:S(2)}) collective-permute-start(bf16[256,512]{1,0:T(8,128)(2,1)S(1)} %add.69), channel_id=1, source_target_pairs={{0,1},{2,3},{4,5},{6,7},{8,9},{10,11},{12,13},{14,15},{16,17},{18,... | collective-permute-start | bytes 786440 | tf_op jit(solution)/shard_map/ppermute | solution.py:678
  50.5 11.1 %shard_map.264 = (bf16[512,512]{1,0:T(8,128)(2,1)S(1)}, bf16[11520,3072]{1,0:T(8,128)(2,1)}, bf16[512,512]{1,0:T(8,128)(2,1)S(1)}, f32[8,512]{1,0:T(8,128)S(1)},...) custom-call(s32[2]{0:T(128)S(1)} %pad_add_fusion.order, ...), custom_call_target="tpu_custom_call" | custom-call | flops 12000000000 | tf_op jit(solution)/shard_map/pallas_call | solution.py:610
  61.7 3.8 %collective-permute-done.7.refs_5_ = bf16[256,512]{1,0:T(8,128)(2,1)S(1)} collective-permute-done((bf16[256,512]{1,0:T(8,128)(2,1)S(1)}, bf16[256,512]{1,0:T(8,128)(2,1)S(1)}, u32[]{:S(2)}, u32[]{:S(2)}) %collective-permute-start.7) | collective-permute-done | bytes 262176 | tf_op jit(solution)/shard_map/ppermute | solution.py:678
  65.6 9.8 %shard_map.265 = (bf16[11520,3072]{1,0:T(8,128)(2,1)}, bf16[512,512]{1,0:T(8,128)(2,1)S(1)}, f32[8,512]{1,0:T(8,128)S(1)}, f32[512,512]{1,0:T(8,128)S(1)}, bf16[1,256,512]{2,1,0:T(8,128)(2,1)S(1)}) custom-call(s32[2]{0:T(128)S(1)} %pad_add_fusion.order, s32[1]{0:T(128)} %bitcast.2.rank, s32[2,4]{1,0:T(2,128)S(1)} %copy-done.15, ...), custom_call_target="tpu_custom_call" | custom-call | flops 11000000512 | tf_op jit(solution)/shard_map/pallas_call | solution.py:610
  75.5 14.8 %shard_map.266 = (bf16[2,256,512]{2,1,0:T(8,128)(2,1)}, f32[512,512]{1,0:T(8,128)S(1)}, bf16[16,16,4096]{2,1,0:T(8,128)(2,1)S(1)}, bf16[16,16,4096]{2,1,0:T(8,12...) custom-call(s32[2]{0:T(128)S(1)} %pad_add_fusion.order, s32[2]{0:T(128)S(1)} %pad_add_fusion.1.codes, ...), custom_call_target="tpu_custom_call" | custom-call | flops 14000000000 | tf_op jit(solution)/shard_map/pallas_call | solution.py:610
  90.4 12.7 %shard_map.267 = (bf16[256,512]{1,0:T(8,128)(2,1)S(1)}, bf16[512,512]{1,0:T(8,128)(2,1)S(1)}, bf16[256,512]{1,0:T(8,128)(2,1)S(1)}, bf16[256,512]{1,0:T(8,128)(2...) custom-call(s32[2]{0:T(128)S(1)} %pad_add_fusion.order, ...), custom_call_target="tpu_custom_call" | custom-call | flops 14000000000 | tf_op jit(solution)/shard_map/pallas_call | solution.py:610
  103.1 3.4 %collective-permute-start.13 = (bf16[256,512]{1,0:T(8,128)(2,1)S(1)}, bf16[256,512]{1,0:T(8,128)(2,1)S(1)}, u32[]{:S(2)}, u32[]{:S(2)}) collective-permute-start(bf16[256,512]{1,0:T(8,128)(2,1)S(1)} %get-tuple-element.150), channel_id=1, source_target_pairs={{0,2},{1,3},{2,0},{3,1},{4,6},{5,7},{6,4},{7,5},{8,10},{9,11},{10,... | collective-permute-start | bytes 786440 | tf_op jit(solution)/shard_map/ppermute | solution.py:646
  106.5 3.8 %collective-permute-start.12 = (bf16[512,512]{1,0:T(8,128)(2,1)S(1)}, bf16[512,512]{1,0:T(8,128)(2,1)S(1)}, u32[]{:S(2)}, u32[]{:S(2)}) collective-permute-start(bf16[512,512]{1,0:T(8,128)(2,1)S(1)} %get-tuple-element.149.refs_6_), channel_id=1, source_target_pairs={{0,3},{1,0},{2,1},{3,2},{4,7},{5,4},{6,5},{7,6},{8,11},{9,8},{10,9... | collective-permute-start | bytes 1572872 | tf_op jit(solution)/shard_map/ppermute | solution.py:646
  113.7 14.0 %shard_map.269 = (bf16[256,512]{1,0:T(8,128)(2,1)S(1)}, bf16[256,512]{1,0:T(8,128)(2,1)S(1)}, bf16[256,512]{1,0:T(8,128)(2,1)S(1)}, bf16[256,512]{1,0:T(8,128)(2...) custom-call(s32[2]{0:T(128)S(1)} %pad_add_fusion.order, ...), custom_call_target="tpu_custom_call" | custom-call | flops 16000000000 | tf_op jit(solution)/shard_map/pallas_call | solution.py:610
  127.7 2.8 %collective-permute-done.12.refs_7_ = bf16[512,512]{1,0:T(8,128)(2,1)S(1)} collective-permute-done((bf16[512,512]{1,0:T(8,128)(2,1)S(1)}, bf16[512,512]{1,0:T(8,128)(2,1)S(1)}, u32[]{:S(2)}, u32[]{:S(2)}) %collective-permute-start.12) | collective-permute-done | bytes 524320 | tf_op jit(solution)/shard_map/ppermute | solution.py:646
  135.2 1.6 collective-permute-start.15
  136.8 8.9 %collective-permute-done.18.refs_8_ = bf16[256,512]{1,0:T(8,128)(2,1)S(1)} collective-permute-done((bf16[256,512]{1,0:T(8,128)(2,1)S(1)}, bf16[256,512]{1,0:T(8,128)(2,1)S(1)}, u32[]{:S(2)}, u32[]{:S(2)}) %collective-permute-start.18) | collective-permute-done | bytes 262176 | tf_op jit(solution)/shard_map/ppermute | solution.py:646
  145.7 6.8 %collective-permute-done.19.refs_11_ = bf16[256,512]{1,0:T(8,128)(2,1)S(1)} collective-permute-done((bf16[256,512]{1,0:T(8,128)(2,1)S(1)}, bf16[256,512]{1,0:T(8,128)(2,1)S(1)}, u32[]{:S(2)}, u32[]{:S(2)}) %collective-permute-start.19) | collective-permute-done | bytes 262176 | tf_op jit(solution)/shard_map/ppermute | solution.py:651
  153.1 1.6 collective-permute-start.21
  156.1 4.4 %collective-permute-start.24 = (bf16[1,16,4096]{2,1,0:T(8,128)(2,1)S(1)}, bf16[1,16,4096]{2,1,0:T(8,128)(2,1)S(1)}, u32[]{:S(2)}, u32[]{:S(2)}) collective-permute-start(bf16[1,16,4096]{2,1,0:T(8,128)(2,1)S(1)} %get-tuple-element.170), channel_id=1, source_target_pairs={{0,3},{1,2},{2,1},{3,0},{4,7},{5,6},{6,5},{7,4},{8,11},{9,10},{10,... | collective-permute-start | bytes 393224 | tf_op jit(solution)/shard_map/ppermute | solution.py:688
  160.5 2.6 %collective-permute-done.22.refs_6_ = bf16[1,16,4096]{2,1,0:T(8,128)(2,1)S(1)} collective-permute-done((bf16[1,16,4096]{2,1,0:T(8,128)(2,1)S(1)}, bf16[1,16,4096]{2,1,0:T(8,128)(2,1)S(1)}, u32[]{:S(2)}, u32[]{:S(2)}) %collective-permute-start.22) | collective-permute-done | bytes 131104 | tf_op jit(solution)/shard_map/ppermute | solution.py:688
  163.1 5.6 %collective-permute-done.23.refs_7_ = bf16[1,16,4096]{2,1,0:T(8,128)(2,1)S(1)} collective-permute-done((bf16[1,16,4096]{2,1,0:T(8,128)(2,1)S(1)}, bf16[1,16,4096]{2,1,0:T(8,128)(2,1)S(1)}, u32[]{:S(2)}, u32[]{:S(2)}) %collective-permute-start.23) | collective-permute-done | bytes 131104 | tf_op jit(solution)/shard_map/ppermute | solution.py:688
  171.4 2.0 collective-permute-start.28
  173.4 1.6 collective-permute-start.27
  175.0 3.8 %collective-permute-done.29.refs_7_ = bf16[1,16,4096]{2,1,0:T(8,128)(2,1)S(1)} collective-permute-done((bf16[1,16,4096]{2,1,0:T(8,128)(2,1)S(1)}, bf16[1,16,4096]{2,1,0:T(8,128)(2,1)S(1)}, u32[]{:S(2)}, u32[]{:S(2)}) %collective-permute-start.29) | collective-permute-done | bytes 131104 | tf_op jit(solution)/shard_map/ppermute | solution.py:688
  178.9 4.2 %collective-permute-done.28.refs_6_ = bf16[1,16,4096]{2,1,0:T(8,128)(2,1)S(1)} collective-permute-done((bf16[1,16,4096]{2,1,0:T(8,128)(2,1)S(1)}, bf16[1,16,4096]{2,1,0:T(8,128)(2,1)S(1)}, u32[]{:S(2)}, u32[]{:S(2)}) %collective-permute-start.28) | collective-permute-done | bytes 131104 | tf_op jit(solution)/shard_map/ppermute | solution.py:688
  183.2 1.6 collective-permute-start.33
  186.8 3.5 %collective-permute-start.32 = (bf16[1,16,4224]{2,1,0:T(8,128)(2,1)S(1)}, bf16[1,16,4224]{2,1,0:T(8,128)(2,1)S(1)}, u32[]{:S(2)}, u32[]{:S(2)}) collective-permute-start(bf16[1,16,4224]{2,1,0:T(8,128)(2,1)S(1)} %get-tuple-element.179), channel_id=1, source_target_pairs={{0,3},{1,2},{2,1},{3,0},{4,7},{5,6},{6,5},{7,4},{8,11},{9,10},{10,... | collective-permute-start | bytes 405512 | tf_op jit(solution)/shard_map/ppermute | solution.py:688
  190.4 2.2 collective-permute-done.30.refs_2_
  192.6 6.0 %collective-permute-done.31.refs_3_ = bf16[1,16,4224]{2,1,0:T(8,128)(2,1)S(1)} collective-permute-done((bf16[1,16,4224]{2,1,0:T(8,128)(2,1)S(1)}, bf16[1,16,4224]{2,1,0:T(8,128)(2,1)S(1)}, u32[]{:S(2)}, u32[]{:S(2)}) %collective-permute-start.31) | collective-permute-done | bytes 135200 | tf_op jit(solution)/shard_map/ppermute | solution.py:688
  199.8 1.6 collective-permute-start.37
  201.4 3.1 %collective-permute-start.36 = (bf16[1,16,4224]{2,1,0:T(8,128)(2,1)S(1)}, bf16[1,16,4224]{2,1,0:T(8,128)(2,1)S(1)}, u32[]{:S(2)}, u32[]{:S(2)}) collective-permute-start(bf16[1,16,4224]{2,1,0:T(8,128)(2,1)S(1)} %get-tuple-element.182.refs_0_), channel_id=1, source_target_pairs={{0,2},{1,3},{2,0},{3,1},{4,6},{5,7},{6,4},{7,5},{8,10},{9,11},{10,... | collective-permute-start | bytes 405512 | tf_op jit(solution)/shard_map/ppermute | solution.py:688
  204.5 2.9 %collective-permute-done.37.refs_3_ = bf16[1,16,4224]{2,1,0:T(8,128)(2,1)S(1)} collective-permute-done((bf16[1,16,4224]{2,1,0:T(8,128)(2,1)S(1)}, bf16[1,16,4224]{2,1,0:T(8,128)(2,1)S(1)}, u32[]{:S(2)}, u32[]{:S(2)}) %collective-permute-start.37) | collective-permute-done | bytes 135200 | tf_op jit(solution)/shard_map/ppermute | solution.py:688
  207.3 4.3 %collective-permute-done.36.refs_2_ = bf16[1,16,4224]{2,1,0:T(8,128)(2,1)S(1)} collective-permute-done((bf16[1,16,4224]{2,1,0:T(8,128)(2,1)S(1)}, bf16[1,16,4224]{2,1,0:T(8,128)(2,1)S(1)}, u32[]{:S(2)}, u32[]{:S(2)}) %collective-permute-start.36) | collective-permute-done | bytes 135200 | tf_op jit(solution)/shard_map/ppermute | solution.py:688
  211.9 1.7 collective-permute-start.41
  217.6 7.1 %collective-permute-done.43.refs_7_ = bf16[256,512]{1,0:T(8,128)(2,1)S(1)} collective-permute-done((bf16[256,512]{1,0:T(8,128)(2,1)S(1)}, bf16[256,512]{1,0:T(8,128)(2,1)S(1)}, u32[]{:S(2)}, u32[]{:S(2)}) %collective-permute-start.43) | collective-permute-done | bytes 262176 | tf_op jit(solution)/shard_map/ppermute | solution.py:646
  224.7 4.8 %collective-permute-done.44.refs_10_ = bf16[256,512]{1,0:T(8,128)(2,1)S(1)} collective-permute-done((bf16[256,512]{1,0:T(8,128)(2,1)S(1)}, bf16[256,512]{1,0:T(8,128)(2,1)S(1)}, u32[]{:S(2)}, u32[]{:S(2)}) %collective-permute-start.44) | collective-permute-done | bytes 262176 | tf_op jit(solution)/shard_map/ppermute | solution.py:651
  234.2 4.5 %shard_map.277 = (f32[512,2048]{1,0:T(8,128)}, f32[2048,512]{1,0:T(8,128)}) custom-call(s32[2]{0:T(128)S(1)} %pad_add_fusion.1.codes, bf16[16,16,4096]{2,1,0:T(8,128)(2,1)S(1)} %get-tuple-element.187.refs_0_, bf16[16,16,4096]{2,1,0:T(8,128)(2,1)S(1)} %collective-permute-done.42.refs_4_.refs_1_), custom_call_target="tpu_custom_call" | custom-call | flops 6000000000 | tf_op jit(solution)/shard_map/pallas_call | solution.py:610
  240.6 4.2 %collective-permute-done.48.refs_8_ = bf16[256,512]{1,0:T(8,128)(2,1)S(1)} collective-permute-done((bf16[256,512]{1,0:T(8,128)(2,1)S(1)}, bf16[256,512]{1,0:T(8,128)(2,1)S(1)}, u32[]{:S(2)}, u32[]{:S(2)}) %collective-permute-start.48) | collective-permute-done | bytes 262176 | tf_op jit(solution)/shard_map/ppermute | solution.py:651
  246.6 2.6 %shard_map.279 = (f32[2,256,512]{2,1,0:T(8,128)}, f32[2,256,512]{2,1,0:T(8,128)}) custom-call(s32[2]{0:T(128)S(1)} %pad_add_fusion.order, s32[1]{0:T(128)} %bitcast.2.rank, bf16[2,256,512]{2,1,0:T(8,128)(2,1)S(1)} %copy-done.7, f32[512,512]{1,0:T(8,128)S(1)} %get-tuple-element.130.refs_4_.self_grad, ...), custom_call_target="tpu_custom_call" | custom-call | flops 3000000000 | tf_op jit(solution)/shard_map/pallas_call | solution.py:610
  249.3 1.6 collective-permute-done.49.refs_1_
  250.9 3.9 %shard_map.280 = (f32[512,1024]{1,0:T(8,128)}, f32[512,512]{1,0:T(8,128)}, f32[512,512]{1,0:T(8,128)}, f32[512,1536]{1,0:T(8,128)}, f32[512,512]{1,0:T(8,128)}, ...) custom-call(s32[2]{0:T(128)S(1)} %pad_add_fusion.1.codes, ...), custom_call_target="tpu_custom_call" | custom-call | flops 5000000000 | tf_op jit(solution)/shard_map/pallas_call | solution.py:610
  (116 shorter events, 32.7 us)
Async XLA Ops:
  2.9 18.9 %collective-permute-start = (bf16[512,512]{1,0:T(8,128)(2,1)}, bf16[512,512]{1,0:T(8,128)(2,1)S(1)}, u32[]{:S(2)}, u32[]{:S(2)}) collective-permute-start(bf16[512,512]{1,0:T(8,128)(2,1)} %get-tuple-element.115), channel_id=1, source_target_pairs={{0,2},{4,6},{8,10},{12,14},{16,18},{20,22},{24,26},{28,30}} | collective-permute-start | bytes 1572872 | tf_op jit(solution)/shard_map/ppermute | solution.py:667
  9.2 18.6 %collective-permute-start.6 = (bf16[256,512]{1,0:T(8,128)(2,1)}, bf16[256,512]{1,0:T(8,128)(2,1)S(1)}, u32[]{:S(2)}, u32[]{:S(2)}) collective-permute-start(bf16[256,512]{1,0:T(8,128)(2,1)} %get-tuple-element.117), channel_id=1, source_target_pairs={{0,3},{4,7},{8,11},{12,15},{16,19},{20,23},{24,27},{28,31}} | collective-permute-start | bytes 786440 | tf_op jit(solution)/shard_map/ppermute | solution.py:640
  10.8 22.3 %collective-permute-start.5 = (bf16[256,512]{1,0:T(8,128)(2,1)}, bf16[256,512]{1,0:T(8,128)(2,1)}, u32[]{:S(2)}, u32[]{:S(2)}) collective-permute-start(bf16[256,512]{1,0:T(8,128)(2,1)} %get-tuple-element.117), channel_id=1, source_target_pairs={{0,2},{1,3},{4,6},{5,7},{8,10},{9,11},{12,14},{13,15},{16,18},{17,... | collective-permute-start | bytes 786440 | tf_op jit(solution)/shard_map/ppermute | solution.py:640
  12.8 26.3 %collective-permute-start.4 = (bf16[256,512]{1,0:T(8,128)(2,1)}, bf16[256,512]{1,0:T(8,128)(2,1)}, u32[]{:S(2)}, u32[]{:S(2)}) collective-permute-start(bf16[256,512]{1,0:T(8,128)(2,1)} %get-tuple-element.117), channel_id=1, source_target_pairs={{0,1},{1,2},{2,3},{4,5},{5,6},{6,7},{8,9},{9,10},{10,11},{12,13},{... | collective-permute-start | bytes 786440 | tf_op jit(solution)/shard_map/ppermute | solution.py:640
  23.7 23.8 %collective-permute-start.8 = (bf16[256,512]{1,0:T(8,128)(2,1)}, bf16[256,512]{1,0:T(8,128)(2,1)}, u32[]{:S(2)}, u32[]{:S(2)}) collective-permute-start(bf16[256,512]{1,0:T(8,128)(2,1)} %get-tuple-element.214), channel_id=1, source_target_pairs={{0,1},{2,3},{4,5},{6,7},{8,9},{10,11},{12,13},{14,15},{16,17},{18,... | collective-permute-start | bytes 786440 | tf_op jit(solution)/shard_map/ppermute | solution.py:678
  27.8 33.9 %collective-permute-start.3 = (bf16[256,512]{1,0:T(8,128)(2,1)}, bf16[256,512]{1,0:T(8,128)(2,1)S(1)}, u32[]{:S(2)}, u32[]{:S(2)}) collective-permute-start(bf16[256,512]{1,0:T(8,128)(2,1)} %get-tuple-element.116), channel_id=1, source_target_pairs={{0,3},{1,0},{2,1},{3,2},{4,7},{5,4},{6,5},{7,6},{8,11},{9,8},{10,9... | collective-permute-start | bytes 786440 | tf_op jit(solution)/shard_map/ppermute | solution.py:640
  27.8 33.9 %collective-permute-start.2 = (bf16[256,512]{1,0:T(8,128)(2,1)}, bf16[256,512]{1,0:T(8,128)(2,1)S(1)}, u32[]{:S(2)}, u32[]{:S(2)}) collective-permute-start(bf16[256,512]{1,0:T(8,128)(2,1)} %get-tuple-element.116), channel_id=1, source_target_pairs={{0,2},{1,3},{2,0},{3,1},{4,6},{5,7},{6,4},{7,5},{8,10},{9,11},{10,... | collective-permute-start | bytes 786440 | tf_op jit(solution)/shard_map/ppermute | solution.py:640
  33.1 28.7 %collective-permute-start.1 = (bf16[256,512]{1,0:T(8,128)(2,1)}, bf16[256,512]{1,0:T(8,128)(2,1)S(1)}, u32[]{:S(2)}, u32[]{:S(2)}) collective-permute-start(bf16[256,512]{1,0:T(8,128)(2,1)} %get-tuple-element.116), channel_id=1, source_target_pairs={{0,1},{1,2},{2,3},{3,0},{4,5},{5,6},{6,7},{7,4},{8,9},{9,10},{10,1... | collective-permute-start | bytes 786440 | tf_op jit(solution)/shard_map/ppermute | solution.py:640
  39.1 26.4 %collective-permute-start.7 = (bf16[256,512]{1,0:T(8,128)(2,1)S(1)}, bf16[256,512]{1,0:T(8,128)(2,1)S(1)}, u32[]{:S(2)}, u32[]{:S(2)}) collective-permute-start(bf16[256,512]{1,0:T(8,128)(2,1)S(1)} %add.69), channel_id=1, source_target_pairs={{0,1},{2,3},{4,5},{6,7},{8,9},{10,11},{12,13},{14,15},{16,17},{18,... | collective-permute-start | bytes 786440 | tf_op jit(solution)/shard_map/ppermute | solution.py:678
  90.3 20.0 %collective-permute-start.9 = (bf16[16,16,4096]{2,1,0:T(8,128)(2,1)S(1)}, bf16[16,16,4096]{2,1,0:T(8,128)(2,1)S(1)}, u32[]{:S(2)}, u32[]{:S(2)}) collective-permute-start(bf16[16,16,4096]{2,1,0:T(8,128)(2,1)S(1)} %get-tuple-element.141), channel_id=1, source_target_pairs={{0,4},{4,0},{8,12},{12,8},{16,20},{20,16},{24,28},{28,24},{1,5},{5... | collective-permute-start | bytes 6291464 | tf_op jit(solution)/shard_map/ppermute | solution.py:688
  103.1 24.6 %collective-permute-start.13 = (bf16[256,512]{1,0:T(8,128)(2,1)S(1)}, bf16[256,512]{1,0:T(8,128)(2,1)S(1)}, u32[]{:S(2)}, u32[]{:S(2)}) collective-permute-start(bf16[256,512]{1,0:T(8,128)(2,1)S(1)} %get-tuple-element.150), channel_id=1, source_target_pairs={{0,2},{1,3},{2,0},{3,1},{4,6},{5,7},{6,4},{7,5},{8,10},{9,11},{10,... | collective-permute-start | bytes 786440 | tf_op jit(solution)/shard_map/ppermute | solution.py:646
  106.5 21.2 %collective-permute-start.14 = (bf16[256,512]{1,0:T(8,128)(2,1)S(1)}, bf16[256,512]{1,0:T(8,128)(2,1)S(1)}, u32[]{:S(2)}, u32[]{:S(2)}) collective-permute-start(bf16[256,512]{1,0:T(8,128)(2,1)S(1)} %get-tuple-element.151), channel_id=1, source_target_pairs={{0,1},{1,2},{2,3},{3,0},{4,5},{5,6},{6,7},{7,4},{8,9},{9,10},{10,1... | collective-permute-start | bytes 786440 | tf_op jit(solution)/shard_map/ppermute | solution.py:646
  106.5 24.0 %collective-permute-start.12 = (bf16[512,512]{1,0:T(8,128)(2,1)S(1)}, bf16[512,512]{1,0:T(8,128)(2,1)S(1)}, u32[]{:S(2)}, u32[]{:S(2)}) collective-permute-start(bf16[512,512]{1,0:T(8,128)(2,1)S(1)} %get-tuple-element.149.refs_6_), channel_id=1, source_target_pairs={{0,3},{1,0},{2,1},{3,2},{4,7},{5,4},{6,5},{7,6},{8,11},{9,8},{10,9... | collective-permute-start | bytes 1572872 | tf_op jit(solution)/shard_map/ppermute | solution.py:646
  110.6 19.9 %collective-permute-start.10 = (bf16[8,16,2048]{2,1,0:T(8,128)(2,1)S(1)}, bf16[8,16,2048]{2,1,0:T(8,128)(2,1)S(1)}, u32[]{:S(2)}, u32[]{:S(2)}) collective-permute-start(bf16[8,16,2048]{2,1,0:T(8,128)(2,1)S(1)} %get-tuple-element.145), channel_id=1, source_target_pairs={{0,8},{4,12},{8,0},{12,4},{16,24},{20,28},{24,16},{28,20},{1,9},{5... | collective-permute-start | bytes 1572872 | tf_op jit(solution)/shard_map/ppermute | solution.py:688
  112.1 18.4 %collective-permute-start.11 = (bf16[8,16,2048]{2,1,0:T(8,128)(2,1)S(1)}, bf16[8,16,2048]{2,1,0:T(8,128)(2,1)S(1)}, u32[]{:S(2)}, u32[]{:S(2)}) collective-permute-start(bf16[8,16,2048]{2,1,0:T(8,128)(2,1)S(1)} %get-tuple-element.147), channel_id=1, source_target_pairs={{0,16},{4,20},{8,24},{12,28},{16,0},{20,4},{24,8},{28,12},{1,17},{... | collective-permute-start | bytes 1572872 | tf_op jit(solution)/shard_map/ppermute | solution.py:688
  130.7 21.8 %collective-permute-start.17 = (bf16[16,16,4224]{2,1,0:T(8,128)(2,1)S(1)}, bf16[16,16,4224]{2,1,0:T(8,128)(2,1)S(1)}, u32[]{:S(2)}, u32[]{:S(2)}) collective-permute-start(bf16[16,16,4224]{2,1,0:T(8,128)(2,1)S(1)} %get-tuple-element.158), channel_id=1, source_target_pairs={{0,4},{4,0},{8,12},{12,8},{16,20},{20,16},{24,28},{28,24},{1,5},{5... | collective-permute-start | bytes 6488072 | tf_op jit(solution)/shard_map/ppermute | solution.py:688
  130.8 14.9 %collective-permute-start.18 = (bf16[256,512]{1,0:T(8,128)(2,1)S(1)}, bf16[256,512]{1,0:T(8,128)(2,1)S(1)}, u32[]{:S(2)}, u32[]{:S(2)}) collective-permute-start(bf16[256,512]{1,0:T(8,128)(2,1)S(1)} %get-tuple-element.161), channel_id=1, source_target_pairs={{1,0},{2,1},{3,2},{5,4},{6,5},{7,6},{9,8},{10,9},{11,10},{13,12},{... | collective-permute-start | bytes 786440 | tf_op jit(solution)/shard_map/ppermute | solution.py:646
  132.1 13.6 %collective-permute-start.16 = (bf16[4,16,2048]{2,1,0:T(8,128)(2,1)S(1)}, bf16[4,16,2048]{2,1,0:T(8,128)(2,1)S(1)}, u32[]{:S(2)}, u32[]{:S(2)}) collective-permute-start(bf16[4,16,2048]{2,1,0:T(8,128)(2,1)S(1)} %get-tuple-element.155), channel_id=1, source_target_pairs={{0,8},{4,12},{8,0},{12,4},{16,24},{20,28},{24,16},{28,20},{1,9},{5... | collective-permute-start | bytes 786440 | tf_op jit(solution)/shard_map/ppermute | solution.py:688
  133.7 18.9 %collective-permute-start.19 = (bf16[256,512]{1,0:T(8,128)(2,1)S(1)}, bf16[256,512]{1,0:T(8,128)(2,1)S(1)}, u32[]{:S(2)}, u32[]{:S(2)}) collective-permute-start(bf16[256,512]{1,0:T(8,128)(2,1)S(1)} %get-tuple-element.162.refs_10_), channel_id=1, source_target_pairs={{2,0},{6,4},{10,8},{14,12},{18,16},{22,20},{26,24},{30,28}} | collective-permute-start | bytes 786440 | tf_op jit(solution)/shard_map/ppermute | solution.py:651
  135.2 17.3 %collective-permute-start.15 = (bf16[4,16,2048]{2,1,0:T(8,128)(2,1)S(1)}, bf16[4,16,2048]{2,1,0:T(8,128)(2,1)S(1)}, u32[]{:S(2)}, u32[]{:S(2)}) collective-permute-start(bf16[4,16,2048]{2,1,0:T(8,128)(2,1)S(1)} %get-tuple-element.153), channel_id=1, source_target_pairs={{0,16},{4,20},{8,24},{12,28},{16,0},{20,4},{24,8},{28,12},{1,17},{... | collective-permute-start | bytes 786440 | tf_op jit(solution)/shard_map/ppermute | solution.py:688
  153.1 15.6 %collective-permute-start.21 = (bf16[8,16,2176]{2,1,0:T(8,128)(2,1)S(1)}, bf16[8,16,2176]{2,1,0:T(8,128)(2,1)S(1)}, u32[]{:S(2)}, u32[]{:S(2)}) collective-permute-start(bf16[8,16,2176]{2,1,0:T(8,128)(2,1)S(1)} %get-tuple-element.166), channel_id=1, source_target_pairs={{0,16},{4,20},{8,24},{12,28},{16,0},{20,4},{24,8},{28,12},{1,17},{... | collective-permute-start | bytes 1671176 | tf_op jit(solution)/shard_map/ppermute | solution.py:688
  154.6 14.0 %collective-permute-start.20 = (bf16[8,16,2048]{2,1,0:T(8,128)(2,1)S(1)}, bf16[8,16,2048]{2,1,0:T(8,128)(2,1)S(1)}, u32[]{:S(2)}, u32[]{:S(2)}) collective-permute-start(bf16[8,16,2048]{2,1,0:T(8,128)(2,1)S(1)} %get-tuple-element.164), channel_id=1, source_target_pairs={{0,8},{4,12},{8,0},{12,4},{16,24},{20,28},{24,16},{28,20},{1,9},{5... | collective-permute-start | bytes 1572872 | tf_op jit(solution)/shard_map/ppermute | solution.py:688
  156.1 7.0 %collective-permute-start.22 = (bf16[1,16,4096]{2,1,0:T(8,128)(2,1)S(1)}, bf16[1,16,4096]{2,1,0:T(8,128)(2,1)S(1)}, u32[]{:S(2)}, u32[]{:S(2)}) collective-permute-start(bf16[1,16,4096]{2,1,0:T(8,128)(2,1)S(1)} %get-tuple-element.168), channel_id=1, source_target_pairs={{0,1},{1,0},{2,3},{3,2},{4,5},{5,4},{6,7},{7,6},{8,9},{9,8},{10,11... | collective-permute-start | bytes 393224 | tf_op jit(solution)/shard_map/ppermute | solution.py:688
  156.1 12.5 %collective-permute-start.23 = (bf16[1,16,4096]{2,1,0:T(8,128)(2,1)S(1)}, bf16[1,16,4096]{2,1,0:T(8,128)(2,1)S(1)}, u32[]{:S(2)}, u32[]{:S(2)}) collective-permute-start(bf16[1,16,4096]{2,1,0:T(8,128)(2,1)S(1)} %get-tuple-element.169), channel_id=1, source_target_pairs={{0,2},{1,3},{2,0},{3,1},{4,6},{5,7},{6,4},{7,5},{8,10},{9,11},{10,... | collective-permute-start | bytes 393224 | tf_op jit(solution)/shard_map/ppermute | solution.py:688
  156.1 12.5 %collective-permute-start.24 = (bf16[1,16,4096]{2,1,0:T(8,128)(2,1)S(1)}, bf16[1,16,4096]{2,1,0:T(8,128)(2,1)S(1)}, u32[]{:S(2)}, u32[]{:S(2)}) collective-permute-start(bf16[1,16,4096]{2,1,0:T(8,128)(2,1)S(1)} %get-tuple-element.170), channel_id=1, source_target_pairs={{0,3},{1,2},{2,1},{3,0},{4,7},{5,6},{6,5},{7,4},{8,11},{9,10},{10,... | collective-permute-start | bytes 393224 | tf_op jit(solution)/shard_map/ppermute | solution.py:688
  168.9 14.2 %collective-permute-start.26 = (bf16[4,16,2176]{2,1,0:T(8,128)(2,1)S(1)}, bf16[4,16,2176]{2,1,0:T(8,128)(2,1)S(1)}, u32[]{:S(2)}, u32[]{:S(2)}) collective-permute-start(bf16[4,16,2176]{2,1,0:T(8,128)(2,1)S(1)} %get-tuple-element.174), channel_id=1, source_target_pairs={{0,8},{4,12},{8,0},{12,4},{16,24},{20,28},{24,16},{28,20},{1,9},{5... | collective-permute-start | bytes 835592 | tf_op jit(solution)/shard_map/ppermute | solution.py:688
  169.7 13.4 %collective-permute-start.25 = (bf16[4,16,2048]{2,1,0:T(8,128)(2,1)S(1)}, bf16[4,16,2048]{2,1,0:T(8,128)(2,1)S(1)}, u32[]{:S(2)}, u32[]{:S(2)}) collective-permute-start(bf16[4,16,2048]{2,1,0:T(8,128)(2,1)S(1)} %get-tuple-element.172), channel_id=1, source_target_pairs={{0,16},{4,20},{8,24},{12,28},{16,0},{20,4},{24,8},{28,12},{1,17},{... | collective-permute-start | bytes 786440 | tf_op jit(solution)/shard_map/ppermute | solution.py:688
  170.7 8.2 %collective-permute-start.29 = (bf16[1,16,4096]{2,1,0:T(8,128)(2,1)S(1)}, bf16[1,16,4096]{2,1,0:T(8,128)(2,1)S(1)}, u32[]{:S(2)}, u32[]{:S(2)}) collective-permute-start(bf16[1,16,4096]{2,1,0:T(8,128)(2,1)S(1)} %get-tuple-element.175.refs_4_), channel_id=1, source_target_pairs={{0,3},{1,2},{2,1},{3,0},{4,7},{5,6},{6,5},{7,4},{8,11},{9,10},{10,... | collective-permute-start | bytes 393224 | tf_op jit(solution)/shard_map/ppermute | solution.py:688
  171.4 11.6 %collective-permute-start.28 = (bf16[1,16,4096]{2,1,0:T(8,128)(2,1)S(1)}, bf16[1,16,4096]{2,1,0:T(8,128)(2,1)S(1)}, u32[]{:S(2)}, u32[]{:S(2)}) collective-permute-start(bf16[1,16,4096]{2,1,0:T(8,128)(2,1)S(1)} %get-tuple-element.175.refs_4_), channel_id=1, source_target_pairs={{0,2},{1,3},{2,0},{3,1},{4,6},{5,7},{6,4},{7,5},{8,10},{9,11},{10,... | collective-permute-start | bytes 393224 | tf_op jit(solution)/shard_map/ppermute | solution.py:688
  173.4 9.6 %collective-permute-start.27 = (bf16[1,16,4096]{2,1,0:T(8,128)(2,1)S(1)}, bf16[1,16,4096]{2,1,0:T(8,128)(2,1)S(1)}, u32[]{:S(2)}, u32[]{:S(2)}) collective-permute-start(bf16[1,16,4096]{2,1,0:T(8,128)(2,1)S(1)} %get-tuple-element.175.refs_4_), channel_id=1, source_target_pairs={{0,1},{1,0},{2,3},{3,2},{4,5},{5,4},{6,7},{7,6},{8,9},{9,8},{10,11... | collective-permute-start | bytes 393224 | tf_op jit(solution)/shard_map/ppermute | solution.py:688
  183.2 15.4 %collective-permute-start.33 = (bf16[4,16,2048]{2,1,0:T(8,128)(2,1)S(1)}, bf16[4,16,2048]{2,1,0:T(8,128)(2,1)S(1)}, u32[]{:S(2)}, u32[]{:S(2)}) collective-permute-start(bf16[4,16,2048]{2,1,0:T(8,128)(2,1)S(1)} %get-tuple-element.180.refs_5_), channel_id=1, source_target_pairs={{0,16},{4,20},{8,24},{12,28},{16,0},{20,4},{24,8},{28,12},{1,17},{... | collective-permute-start | bytes 786440 | tf_op jit(solution)/shard_map/ppermute | solution.py:688
  184.8 13.8 %collective-permute-start.34 = (bf16[4,16,2048]{2,1,0:T(8,128)(2,1)S(1)}, bf16[4,16,2048]{2,1,0:T(8,128)(2,1)S(1)}, u32[]{:S(2)}, u32[]{:S(2)}) collective-permute-start(bf16[4,16,2048]{2,1,0:T(8,128)(2,1)S(1)} %get-tuple-element.181.refs_7_), channel_id=1, source_target_pairs={{0,8},{4,12},{8,0},{12,4},{16,24},{20,28},{24,16},{28,20},{1,9},{5... | collective-permute-start | bytes 786440 | tf_op jit(solution)/shard_map/ppermute | solution.py:688
  186.0 12.6 %collective-permute-start.31 = (bf16[1,16,4224]{2,1,0:T(8,128)(2,1)S(1)}, bf16[1,16,4224]{2,1,0:T(8,128)(2,1)S(1)}, u32[]{:S(2)}, u32[]{:S(2)}) collective-permute-start(bf16[1,16,4224]{2,1,0:T(8,128)(2,1)S(1)} %get-tuple-element.178), channel_id=1, source_target_pairs={{0,2},{1,3},{2,0},{3,1},{4,6},{5,7},{6,4},{7,5},{8,10},{9,11},{10,... | collective-permute-start | bytes 405512 | tf_op jit(solution)/shard_map/ppermute | solution.py:688
  186.8 11.7 %collective-permute-start.32 = (bf16[1,16,4224]{2,1,0:T(8,128)(2,1)S(1)}, bf16[1,16,4224]{2,1,0:T(8,128)(2,1)S(1)}, u32[]{:S(2)}, u32[]{:S(2)}) collective-permute-start(bf16[1,16,4224]{2,1,0:T(8,128)(2,1)S(1)} %get-tuple-element.179), channel_id=1, source_target_pairs={{0,3},{1,2},{2,1},{3,0},{4,7},{5,6},{6,5},{7,4},{8,11},{9,10},{10,... | collective-permute-start | bytes 405512 | tf_op jit(solution)/shard_map/ppermute | solution.py:688
  198.7 12.9 %collective-permute-start.38 = (bf16[8,16,2048]{2,1,0:T(8,128)(2,1)S(1)}, bf16[8,16,2048]{2,1,0:T(8,128)(2,1)S(1)}, u32[]{:S(2)}, u32[]{:S(2)}) collective-permute-start(bf16[8,16,2048]{2,1,0:T(8,128)(2,1)S(1)} %get-tuple-element.183.refs_4_), channel_id=1, source_target_pairs={{0,8},{4,12},{8,0},{12,4},{16,24},{20,28},{24,16},{28,20},{1,9},{5... | collective-permute-start | bytes 1572872 | tf_op jit(solution)/shard_map/ppermute | solution.py:688
  199.3 12.3 %collective-permute-start.39 = (bf16[8,16,2048]{2,1,0:T(8,128)(2,1)S(1)}, bf16[8,16,2048]{2,1,0:T(8,128)(2,1)S(1)}, u32[]{:S(2)}, u32[]{:S(2)}) collective-permute-start(bf16[8,16,2048]{2,1,0:T(8,128)(2,1)S(1)} %get-tuple-element.184.refs_6_), channel_id=1, source_target_pairs={{0,16},{4,20},{8,24},{12,28},{16,0},{20,4},{24,8},{28,12},{1,17},{... | collective-permute-start | bytes 1572872 | tf_op jit(solution)/shard_map/ppermute | solution.py:688
  199.8 7.6 %collective-permute-start.37 = (bf16[1,16,4224]{2,1,0:T(8,128)(2,1)S(1)}, bf16[1,16,4224]{2,1,0:T(8,128)(2,1)S(1)}, u32[]{:S(2)}, u32[]{:S(2)}) collective-permute-start(bf16[1,16,4224]{2,1,0:T(8,128)(2,1)S(1)} %get-tuple-element.182.refs_0_), channel_id=1, source_target_pairs={{0,3},{1,2},{2,1},{3,0},{4,7},{5,6},{6,5},{7,4},{8,11},{9,10},{10,... | collective-permute-start | bytes 405512 | tf_op jit(solution)/shard_map/ppermute | solution.py:688
  201.4 10.2 %collective-permute-start.36 = (bf16[1,16,4224]{2,1,0:T(8,128)(2,1)S(1)}, bf16[1,16,4224]{2,1,0:T(8,128)(2,1)S(1)}, u32[]{:S(2)}, u32[]{:S(2)}) collective-permute-start(bf16[1,16,4224]{2,1,0:T(8,128)(2,1)S(1)} %get-tuple-element.182.refs_0_), channel_id=1, source_target_pairs={{0,2},{1,3},{2,0},{3,1},{4,6},{5,7},{6,4},{7,5},{8,10},{9,11},{10,... | collective-permute-start | bytes 405512 | tf_op jit(solution)/shard_map/ppermute | solution.py:688
  204.5 7.1 %collective-permute-start.35 = (bf16[1,16,4224]{2,1,0:T(8,128)(2,1)S(1)}, bf16[1,16,4224]{2,1,0:T(8,128)(2,1)S(1)}, u32[]{:S(2)}, u32[]{:S(2)}) collective-permute-start(bf16[1,16,4224]{2,1,0:T(8,128)(2,1)S(1)} %get-tuple-element.182.refs_0_), channel_id=1, source_target_pairs={{0,1},{1,0},{2,3},{3,2},{4,5},{5,4},{6,7},{7,6},{8,9},{9,8},{10,11... | collective-permute-start | bytes 405512 | tf_op jit(solution)/shard_map/ppermute | solution.py:688
  211.8 17.7 %collective-permute-start.42 = (bf16[16,16,4096]{2,1,0:T(8,128)(2,1)S(1)}, bf16[16,16,4096]{2,1,0:T(8,128)(2,1)S(1)}, u32[]{:S(2)}, u32[]{:S(2)}) collective-permute-start(bf16[16,16,4096]{2,1,0:T(8,128)(2,1)S(1)} %get-tuple-element.187.refs_0_), channel_id=1, source_target_pairs={{0,4},{4,0},{8,12},{12,8},{16,20},{20,16},{24,28},{28,24},{1,5},{5... | collective-permute-start | bytes 6291464 | tf_op jit(solution)/shard_map/ppermute | solution.py:688
  211.9 17.6 %collective-permute-start.41 = (bf16[4,16,2176]{2,1,0:T(8,128)(2,1)S(1)}, bf16[4,16,2176]{2,1,0:T(8,128)(2,1)S(1)}, u32[]{:S(2)}, u32[]{:S(2)}) collective-permute-start(bf16[4,16,2176]{2,1,0:T(8,128)(2,1)S(1)} %get-tuple-element.186.refs_2_), channel_id=1, source_target_pairs={{0,8},{4,12},{8,0},{12,4},{16,24},{20,28},{24,16},{28,20},{1,9},{5... | collective-permute-start | bytes 835592 | tf_op jit(solution)/shard_map/ppermute | solution.py:688
  213.6 11.0 %collective-permute-start.43 = (bf16[256,512]{1,0:T(8,128)(2,1)S(1)}, bf16[256,512]{1,0:T(8,128)(2,1)S(1)}, u32[]{:S(2)}, u32[]{:S(2)}) collective-permute-start(bf16[256,512]{1,0:T(8,128)(2,1)S(1)} %get-tuple-element.191), channel_id=1, source_target_pairs={{1,0},{2,1},{3,2},{5,4},{6,5},{7,6},{9,8},{10,9},{11,10},{13,12},{... | collective-permute-start | bytes 786440 | tf_op jit(solution)/shard_map/ppermute | solution.py:646
  214.9 14.6 %collective-permute-start.44 = (bf16[256,512]{1,0:T(8,128)(2,1)S(1)}, bf16[256,512]{1,0:T(8,128)(2,1)S(1)}, u32[]{:S(2)}, u32[]{:S(2)}) collective-permute-start(bf16[256,512]{1,0:T(8,128)(2,1)S(1)} %get-tuple-element.192.refs_9_), channel_id=1, source_target_pairs={{1,0},{3,2},{5,4},{7,6},{9,8},{11,10},{13,12},{15,14},{17,16},{19,... | collective-permute-start | bytes 786440 | tf_op jit(solution)/shard_map/ppermute | solution.py:651
  216.2 13.3 %collective-permute-start.40 = (bf16[4,16,2048]{2,1,0:T(8,128)(2,1)S(1)}, bf16[4,16,2048]{2,1,0:T(8,128)(2,1)S(1)}, u32[]{:S(2)}, u32[]{:S(2)}) collective-permute-start(bf16[4,16,2048]{2,1,0:T(8,128)(2,1)S(1)} %get-tuple-element.185.refs_0_), channel_id=1, source_target_pairs={{0,16},{4,20},{8,24},{12,28},{16,0},{20,4},{24,8},{28,12},{1,17},{... | collective-permute-start | bytes 786440 | tf_op jit(solution)/shard_map/ppermute | solution.py:688
  229.7 10.8 %collective-permute-start.45 = (bf16[256,512]{1,0:T(8,128)(2,1)S(1)}, bf16[256,512]{1,0:T(8,128)(2,1)S(1)}, u32[]{:S(2)}, u32[]{:S(2)}) collective-permute-start(bf16[256,512]{1,0:T(8,128)(2,1)S(1)} %get-tuple-element.193), channel_id=1, source_target_pairs={{1,0},{2,1},{3,2},{5,4},{6,5},{7,6},{9,8},{10,9},{11,10},{13,12},{... | collective-permute-start | bytes 786440 | tf_op jit(solution)/shard_map/ppermute | solution.py:646
  231.0 13.8 %collective-permute-start.48 = (bf16[256,512]{1,0:T(8,128)(2,1)S(1)}, bf16[256,512]{1,0:T(8,128)(2,1)S(1)}, u32[]{:S(2)}, u32[]{:S(2)}) collective-permute-start(bf16[256,512]{1,0:T(8,128)(2,1)S(1)} %get-tuple-element.198.refs_7_), channel_id=1, source_target_pairs={{2,0},{6,4},{10,8},{14,12},{18,16},{22,20},{26,24},{30,28}} | collective-permute-start | bytes 786440 | tf_op jit(solution)/shard_map/ppermute | solution.py:651
  232.3 13.2 %collective-permute-start.46 = (bf16[8,16,2048]{2,1,0:T(8,128)(2,1)S(1)}, bf16[8,16,2048]{2,1,0:T(8,128)(2,1)S(1)}, u32[]{:S(2)}, u32[]{:S(2)}) collective-permute-start(bf16[8,16,2048]{2,1,0:T(8,128)(2,1)S(1)} %get-tuple-element.195.refs_0_), channel_id=1, source_target_pairs={{0,8},{4,12},{8,0},{12,4},{16,24},{20,28},{24,16},{28,20},{1,9},{5... | collective-permute-start | bytes 1572872 | tf_op jit(solution)/shard_map/ppermute | solution.py:688
  232.7 13.6 %collective-permute-start.47 = (bf16[8,16,2176]{2,1,0:T(8,128)(2,1)S(1)}, bf16[8,16,2176]{2,1,0:T(8,128)(2,1)S(1)}, u32[]{:S(2)}, u32[]{:S(2)}) collective-permute-start(bf16[8,16,2176]{2,1,0:T(8,128)(2,1)S(1)} %get-tuple-element.196.refs_2_), channel_id=1, source_target_pairs={{0,16},{4,20},{8,24},{12,28},{16,0},{20,4},{24,8},{28,12},{1,17},{... | collective-permute-start | bytes 1671176 | tf_op jit(solution)/shard_map/ppermute | solution.py:688
  (21 other events, 409.2 us)

commit v2 on v1

--- a/solution.py
+++ b/solution.py
@@ -384,27 +384,30 @@
         parts[1][(b - n + 1) * rows : (b - n + 2) * rows, :] = value
 
 
-def cross_back_kernel(n, order, enc, *refs):
+def cross_back_kernel(n, grad, mixed, inverse, cq, kept, w_cm, w_cout, *refs):
+    parts, (dq, dkv, low, up, kv, p, sems) = refs[:-7], refs[-7:]
+    ready, done = loads(kept, kv, p, sems)
+    rows = parts[0].shape[0]
+    low[...] = grad[...].astype(LOW)
+    up[...] = nt(low[...], w_cout[...]).astype(LOW)
+    attend_back(up, mixed, inverse, cq, kv, p, dq, dkv, plan_of(n), ready, done)
+    for b in range(n + n // 4):
+        put_part(parts, n, b, nt(dkv[b * rows : (b + 1) * rows, :], w_cm[...]).astype(LOW))
+
+
+def cross_sums_kernel(n, order, enc, *refs):
     el, es, refs = refs[: n - 1], refs[n - 1], refs[n:]
-    (grad, mixed, inverse, cq, kept, after, n1, w_cm, w_cout, w_cq, gains) = refs[:11]
-    parts, (self_grad, g_cross, g_small, dq, up, dkv, kv, p, sems) = refs[11:-9], refs[-9:]
-    ready, done = loads(kept, kv, p, sems)
+    grad, low, mixed, dq, dkv, after, n1, w_cq, gains, self_grad, g_cross, g_small = refs
     rows, width = enc.shape[1:]
-    low = grad[...].astype(LOW)
-    g_cross[:, 3 * width :] = tn(mixed[...], low).astype(LOW)
-    up[...] = nt(low, w_cout[...]).astype(LOW)
-    attend_back(up, mixed, inverse, cq, kv, p, dq, dkv, plan_of(n), ready, done)
-    dq_low = dq[...]
-    g_cross[:, 2 * width : 3 * width] = tn(n1[...], dq_low).astype(LOW)
+    g_cross[:, 3 * width :] = tn(mixed[...], low[...]).astype(LOW)
+    g_cross[:, 2 * width : 3 * width] = tn(n1[...], dq[...]).astype(LOW)
     total = tn(enc[order[0]], dkv[0:rows, :])
     for d in range(1, n):
         total = total + tn(el[d - 1][...], dkv[d * rows : (d + 1) * rows, :])
     for j in range(n // 4):
         total = total + tn(es[j], dkv[(n + j) * rows : (n + j + 1) * rows, :])
     g_cross[:, : 2 * width] = total.astype(LOW)
-    for b in range(n + n // 4):
-        put_part(parts, n, b, nt(dkv[b * rows : (b + 1) * rows, :], w_cm[...]).astype(LOW))
-    inner, gain, shift = norm_back(after[...], gains[1:2], nt(dq_low, w_cq[...]))
+    inner, gain, shift = norm_back(after[...], gains[1:2], nt(dq[...], w_cq[...]))
     self_grad[...] = grad[...] + inner
     g_small[0, :] = gain
     g_small[1, :] = shift
@@ -646,6 +649,10 @@
     return lax.ppermute(block, "blk", pairs)
 
 
+def hand_down(held, n, distance):
+    return lax.ppermute(held, "blk", [(i, i - 1) for i in range(distance, n)])
+
+
 def return_short(held, n, root, distance):
     pairs = [((root + k + distance) % n, (root + k) % n) for k in range(0, n, 2 * distance)]
     return lax.ppermute(held, "blk", pairs)
@@ -811,17 +818,24 @@
     part_shapes[1] = (((n // 4 + 1) * rows, width), LOW)
     feed_core = trade(far, "batch", 1)
     feed_near = near
-    *e_parts, self_grad, g_cross, small_cross = call(
+    *e_parts, cross_dq, cross_dkv, cross_low = call(
         functools.partial(cross_back_kernel, n),
-        (order, encoder_output, *el, es, cross_grad, cmixed, cinverse,
-         cq, cross_kept, after, n1, cross_memory, cross_outward, cross_query, norm_gains),
-        part_shapes + [((both, width), WIDE), ((width, 4 * width), LOW), ((2, width), WIDE)],
-        14,
-        scratch=[low_rows, low_rows, pair_rows, *loaded],
+        (cross_grad, cmixed, cinverse, cq, cross_kept, cross_memory, cross_outward),
+        part_shapes + [low_rows, pair_rows, low_rows],
+        10,
+        scratch=[low_rows, *loaded],
+        room=room,
+        far_ins=(4,),
+        sems=3 * pairs,
+    )
+    self_grad, g_cross, small_cross = call(
+        functools.partial(cross_sums_kernel, n),
+        (order, encoder_output, *el, es, cross_grad, cross_low, cmixed, cross_dq, cross_dkv,
+         after, n1, cross_query, norm_gains),
+        [wide_rows, ((width, 4 * width), LOW), ((2, width), WIDE)],
+        4,
         smem=1,
         room=room,
-        far_ins=(n + 6,),
-        sems=3 * pairs,
     )
     (a, a_send, b, b_send), _ = small_steps(
         [(add_core, (feed_near, feed_core), [shape(8, w) for w in wide for _ in "ks"]),
@@ -836,7 +850,7 @@
         [((rows, width), LOW)] * blocks
         + [((both, width), WIDE), (shape(half, sum(wide_rest)), LOW),
            (shape(half, sum(wide_rest)), LOW)],
-        16,
+        14,
         scratch=[(shape(chunks, sum(wide_rest)), LOW), low_rows, low_rows, pair_rows, *loaded],
         smem=2,
         room=room,
@@ -854,8 +868,8 @@
     e_got = [return_short(e_short[k], n, k, 2) for k in roots]
     held = tied(parts[n - 1], a_send)
     for d in range(n - 2, 2, -1):
-        held = parts[d] + return_long(held, n, 1, False)
-    long_got = return_long(held, n, 1, False)
+        held = parts[d] + hand_down(held, n, d + 1)
+    long_got = hand_down(held, n, 3)
     feed, (a, a_send, b, b_send), (held,), *e_short = small_steps(
         [(add_to_pieces, (a, a_got, b, b_got), [shape(1, sum(wide))] * 4),
          (add_core, (near, trade(tied(far, a_send), "batch", 1)),
@@ -890,7 +904,7 @@
     ra_got, rb_got = trade(ra, "batch", 4), trade(rb, "batch", 2)
     feed_got = trade(feed, "batch", 1)
     held, *shorts = tied((held, *parts[n:]), ra)
-    long_got = return_long(held, n, 1, False)
+    long_got = hand_down(held, n, 2)
     got = [return_short(shorts[k], n, k, 1) for k in roots]
     (ra,), (rb,), _, (held,), *shorts = small_steps(
         [(join, (ra, ra_got), [shape(8, wide_rest[0])]),
@@ -900,7 +914,7 @@
         + [(add_all, (own, parts[n + k], got[k]), [(rows, width)]) for k in roots]
     )
     ra_got, rb_got = trade(ra, "batch", 2), trade(rb, "batch", 4)
-    long_got = return_long(held, n, 1, False)
+    long_got = hand_down(held, n, 1)
     got = [return_short(shorts[k][0], n, k, 2) for k in roots]
     s_up, s_down = call(
         functools.partial(unpack_feed_kernel, [(0, 2, 0, 0, 1), (0, 2, 1, hidden, hidden // width)]),

time: 255 us -> 246 us (0.965)
  waiting for transfers between devices: 82 us -> 75.9 us
  starting transfers between devices: 86.1 us -> 82.6 us
    ppermute x6 -> x3, waiting for transfers between devices: 19.9 us -> 0.01 us  [return_long(): return lax.ppermute(block, 'blk', pairs)]
    ppermute x3, waiting for transfers between devices: 15.8 us -> 25.3 us  [return_short(): return lax.ppermute(held, 'blk', pairs)]
    ppermute x32, waiting for transfers between devices: 34.6 us -> 38.9 us  [trade(): lax.ppermute(v, axis, [(i, i ^ distance) for i in range(lax.axis_size(axi...]
    ppermute x6 -> x3, starting transfers between devices: 11.1 us -> 7.25 us  [return_long(): return lax.ppermute(block, 'blk', pairs)]
    ppermute x0 -> x3, starting transfers between devices: none -> 2.63 us  [hand_down(): return lax.ppermute(held, 'blk', [(i, i - 1) for i in range(distance, n)])]
    pallas_call x18 -> x19, Pallas kernels: 77.8 us -> 78.1 us  [call(): pl.pallas_call(kernel, out_shape=[jax.ShapeDtypeStruct(s, t) for s, t in...]
  transfers between devices with their start and end apart: 50 -> 50, of which waited for: 21 -> 17; matrix products, arithmetic and copies ran while one was open for 1% -> 1% of each run, Pallas kernels for 18% -> 19%
where the time goes in v2:
time: 246 us; the launch traced here: 245 us
  starting transfers between devices  82.6 us (34%)
  Pallas kernels  78.1 us (32%)
  waiting for transfers between devices  75.9 us (31%)
  local copies, waits for them, and re-layouts  4.29 us (2%)
  between operations  2.49 us (1%)
    pallas_call x19, Pallas kernels, call(): pl.pallas_call(kernel, out_shape=[jax.ShapeDtypeStruct(s, t) for s, t in...  78.1 us
    ppermute x32, waiting for transfers between devices, trade(): lax.ppermute(v, axis, [(i, i ^ distance) for i in range(lax.axis_size(axi...  38.9 us
    ppermute x32, starting transfers between devices, trade(): lax.ppermute(v, axis, [(i, i ^ distance) for i in range(lax.axis_size(axi...  35.8 us
    ppermute x3, waiting for transfers between devices, return_short(): return lax.ppermute(held, 'blk', pairs)  25.3 us
    ppermute x6, starting transfers between devices, send_long(): got.append(lax.ppermute(block, 'blk', pairs))  16.1 us
    ppermute x2, starting transfers between devices, send_short_rest(): terms[root].append(lax.ppermute(held, 'blk', pairs))  10.4 us
    ppermute x3, starting transfers between devices, return_long(): return lax.ppermute(block, 'blk', pairs)  7.25 us
    ppermute x1, starting transfers between devices, send_short_first(): lax.ppermute(held, 'blk', [(root, (root + n // 2) % n)])  6.24 us
  transfers between devices with their start and end apart: 50, of which 17 were waited for; matrix products, arithmetic and copies ran while one was open for 1% of the time, Pallas kernels for 19%

profile of v2, /device:TPU:0, one launch (start us, length us, event | category | flops | bytes accessed | tf_op | source)
XLA Modules:
  0.0 245.4 jit_solution(11141775297236354573)
XLA Ops:
  0.7 2.2 shard_map.263
  2.9 6.2 %collective-permute-start = (bf16[512,512]{1,0:T(8,128)(2,1)}, bf16[512,512]{1,0:T(8,128)(2,1)S(1)}, u32[]{:S(2)}, u32[]{:S(2)}) collective-permute-start(bf16[512,512]{1,0:T(8,128)(2,1)} %get-tuple-element.118), channel_id=1, source_target_pairs={{0,2},{4,6},{8,10},{12,14},{16,18},{20,22},{24,26},{28,30}} | collective-permute-start | bytes 1572872 | tf_op jit(solution)/shard_map/ppermute | solution.py:674
  9.2 1.6 collective-permute-start.6
  10.8 2.0 collective-permute-start.5
  12.8 3.2 %collective-permute-start.4 = (bf16[256,512]{1,0:T(8,128)(2,1)}, bf16[256,512]{1,0:T(8,128)(2,1)}, u32[]{:S(2)}, u32[]{:S(2)}) collective-permute-start(bf16[256,512]{1,0:T(8,128)(2,1)} %get-tuple-element.120), channel_id=1, source_target_pairs={{0,1},{1,2},{2,3},{4,5},{5,6},{6,7},{8,9},{9,10},{10,11},{12,13},{... | collective-permute-start | bytes 786440 | tf_op jit(solution)/shard_map/ppermute | solution.py:643
  15.9 5.9 %collective-permute-done = bf16[512,512]{1,0:T(8,128)(2,1)S(1)} collective-permute-done((bf16[512,512]{1,0:T(8,128)(2,1)}, bf16[512,512]{1,0:T(8,128)(2,1)S(1)}, u32[]{:S(2)}, u32[]{:S(2)}) %collective-permute-start) | collective-permute-done | bytes 524320 | tf_op jit(solution)/shard_map/ppermute | solution.py:674
  21.8 1.9 slice_add_fusion
  23.7 2.0 collective-permute-start.8
  27.8 3.4 %collective-permute-start.2 = (bf16[256,512]{1,0:T(8,128)(2,1)}, bf16[256,512]{1,0:T(8,128)(2,1)S(1)}, u32[]{:S(2)}, u32[]{:S(2)}) collective-permute-start(bf16[256,512]{1,0:T(8,128)(2,1)} %get-tuple-element.119), channel_id=1, source_target_pairs={{0,2},{1,3},{2,0},{3,1},{4,6},{5,7},{6,4},{7,5},{8,10},{9,11},{10,... | collective-permute-start | bytes 786440 | tf_op jit(solution)/shard_map/ppermute | solution.py:643
  31.2 1.8 collective-permute-done.5.refs_1_
  33.1 6.0 %collective-permute-start.1 = (bf16[256,512]{1,0:T(8,128)(2,1)}, bf16[256,512]{1,0:T(8,128)(2,1)S(1)}, u32[]{:S(2)}, u32[]{:S(2)}) collective-permute-start(bf16[256,512]{1,0:T(8,128)(2,1)} %get-tuple-element.119), channel_id=1, source_target_pairs={{0,1},{1,2},{2,3},{3,0},{4,5},{5,6},{6,7},{7,4},{8,9},{9,10},{10,1... | collective-permute-start | bytes 786440 | tf_op jit(solution)/shard_map/ppermute | solution.py:643
  39.1 8.4 %collective-permute-start.7 = (bf16[256,512]{1,0:T(8,128)(2,1)S(1)}, bf16[256,512]{1,0:T(8,128)(2,1)S(1)}, u32[]{:S(2)}, u32[]{:S(2)}) collective-permute-start(bf16[256,512]{1,0:T(8,128)(2,1)S(1)} %add.69), channel_id=1, source_target_pairs={{0,1},{2,3},{4,5},{6,7},{8,9},{10,11},{12,13},{14,15},{16,17},{18,... | collective-permute-start | bytes 786440 | tf_op jit(solution)/shard_map/ppermute | solution.py:685
  50.5 11.2 %shard_map.264 = (bf16[512,512]{1,0:T(8,128)(2,1)S(1)}, bf16[11520,3072]{1,0:T(8,128)(2,1)}, bf16[512,512]{1,0:T(8,128)(2,1)S(1)}, f32[8,512]{1,0:T(8,128)S(1)},...) custom-call(s32[2]{0:T(128)S(1)} %pad_add_fusion.order, ...), custom_call_target="tpu_custom_call" | custom-call | flops 12000000000 | tf_op jit(solution)/shard_map/pallas_call | solution.py:613
  61.7 3.8 %collective-permute-done.7.refs_5_ = bf16[256,512]{1,0:T(8,128)(2,1)S(1)} collective-permute-done((bf16[256,512]{1,0:T(8,128)(2,1)S(1)}, bf16[256,512]{1,0:T(8,128)(2,1)S(1)}, u32[]{:S(2)}, u32[]{:S(2)}) %collective-permute-start.7) | collective-permute-done | bytes 262176 | tf_op jit(solution)/shard_map/ppermute | solution.py:685
  65.6 9.8 %shard_map.265 = (bf16[11520,3072]{1,0:T(8,128)(2,1)}, bf16[512,512]{1,0:T(8,128)(2,1)S(1)}, f32[8,512]{1,0:T(8,128)S(1)}, f32[512,512]{1,0:T(8,128)S(1)}, bf16[1,256,512]{2,1,0:T(8,128)(2,1)S(1)}) custom-call(s32[2]{0:T(128)S(1)} %pad_add_fusion.order, s32[1]{0:T(128)} %bitcast.2.rank, s32[2,4]{1,0:T(2,128)S(1)} %copy-done.15, ...), custom_call_target="tpu_custom_call" | custom-call | flops 11000000512 | tf_op jit(solution)/shard_map/pallas_call | solution.py:613
  75.5 14.7 %shard_map.266 = (bf16[2,256,512]{2,1,0:T(8,128)(2,1)}, f32[512,512]{1,0:T(8,128)S(1)}, bf16[16,16,4096]{2,1,0:T(8,128)(2,1)S(1)}, bf16[16,16,4096]{2,1,0:T(8,12...) custom-call(s32[2]{0:T(128)S(1)} %pad_add_fusion.order, s32[2]{0:T(128)S(1)} %pad_add_fusion.1.codes, ...), custom_call_target="tpu_custom_call" | custom-call | flops 14000000000 | tf_op jit(solution)/shard_map/pallas_call | solution.py:613
  90.3 9.8 %shard_map.267 = (bf16[256,512]{1,0:T(8,128)(2,1)S(1)}, bf16[512,512]{1,0:T(8,128)(2,1)S(1)}, bf16[256,512]{1,0:T(8,128)(2,1)S(1)}, bf16[256,512]{1,0:T(8,128)(2...) custom-call(f32[512,512]{1,0:T(8,128)S(1)} %get-tuple-element.128.grad.refs_4_, ...), custom_call_target="tpu_custom_call" | custom-call | flops 10000000000 | tf_op jit(solution)/shard_map/pallas_call | solution.py:613
  100.1 3.4 %collective-permute-start.13 = (bf16[256,512]{1,0:T(8,128)(2,1)S(1)}, bf16[256,512]{1,0:T(8,128)(2,1)S(1)}, u32[]{:S(2)}, u32[]{:S(2)}) collective-permute-start(bf16[256,512]{1,0:T(8,128)(2,1)S(1)} %get-tuple-element.156), channel_id=1, source_target_pairs={{0,2},{1,3},{2,0},{3,1},{4,6},{5,7},{6,4},{7,5},{8,10},{9,11},{10,... | collective-permute-start | bytes 786440 | tf_op jit(solution)/shard_map/ppermute | solution.py:649
  103.5 3.8 %collective-permute-start.12 = (bf16[512,512]{1,0:T(8,128)(2,1)S(1)}, bf16[512,512]{1,0:T(8,128)(2,1)S(1)}, u32[]{:S(2)}, u32[]{:S(2)}) collective-permute-start(bf16[512,512]{1,0:T(8,128)(2,1)S(1)} %get-tuple-element.155.refs_6_), channel_id=1, source_target_pairs={{0,3},{1,0},{2,1},{3,2},{4,7},{5,4},{6,5},{7,6},{8,11},{9,8},{10,9... | collective-permute-start | bytes 1572872 | tf_op jit(solution)/shard_map/ppermute | solution.py:649
  107.3 3.3 %shard_map.268 = (f32[512,512]{1,0:T(8,128)S(1)}, bf16[512,2048]{1,0:T(8,128)(2,1)S(1)}, f32[2,512]{1,0:T(2,128)S(1)}) custom-call(s32[2]{0:T(128)S(1)} %pad_add_fusion.order, bf16[2,256,512]{2,1,0:T(8,128)(2,1)S(1)} %copy-done.12, bf16[256,512]{1,0:T(8,128)(2,1)S(1)} %collective-permute-done.1.refs_0_, bf16[256,512]{1,0:T(8,128)(2,1)S(1)} %collective-permute-done.2.refs_1_, ...), custom_call_target="tpu_custom_call" | custom-call | flops 4000000000 | tf_op jit(solution)/shard_map/pallas_call | solution.py:613
  110.9 1.6 collective-permute-start.10
  112.5 1.5 collective-permute-start.11
  114.0 14.0 %shard_map.270 = (bf16[256,512]{1,0:T(8,128)(2,1)S(1)}, bf16[256,512]{1,0:T(8,128)(2,1)S(1)}, bf16[256,512]{1,0:T(8,128)(2,1)S(1)}, bf16[256,512]{1,0:T(8,128)(2...) custom-call(s32[2]{0:T(128)S(1)} %pad_add_fusion.order, ...), custom_call_target="tpu_custom_call" | custom-call | flops 14000000000 | tf_op jit(solution)/shard_map/pallas_call | solution.py:613
  130.0 1.5 collective-permute-start.19
  131.5 1.6 collective-permute-start.15
  133.2 4.7 %collective-permute-done.16.refs_3_ = bf16[4,16,2048]{2,1,0:T(8,128)(2,1)S(1)} collective-permute-done((bf16[4,16,2048]{2,1,0:T(8,128)(2,1)S(1)}, bf16[4,16,2048]{2,1,0:T(8,128)(2,1)S(1)}, u32[]{:S(2)}, u32[]{:S(2)}) %collective-permute-start.16) | collective-permute-done | bytes 262176 | tf_op jit(solution)/shard_map/ppermute | solution.py:695
  137.9 6.8 %collective-permute-done.19.refs_11_ = bf16[256,512]{1,0:T(8,128)(2,1)S(1)} collective-permute-done((bf16[256,512]{1,0:T(8,128)(2,1)S(1)}, bf16[256,512]{1,0:T(8,128)(2,1)S(1)}, u32[]{:S(2)}, u32[]{:S(2)}) %collective-permute-start.19) | collective-permute-done | bytes 262176 | tf_op jit(solution)/shard_map/ppermute | solution.py:658
  145.1 1.6 collective-permute-start.21
  148.1 3.0 %collective-permute-start.23 = (bf16[1,16,4096]{2,1,0:T(8,128)(2,1)S(1)}, bf16[1,16,4096]{2,1,0:T(8,128)(2,1)S(1)}, u32[]{:S(2)}, u32[]{:S(2)}) collective-permute-start(bf16[1,16,4096]{2,1,0:T(8,128)(2,1)S(1)} %get-tuple-element.175), channel_id=1, source_target_pairs={{0,2},{1,3},{2,0},{3,1},{4,6},{5,7},{6,4},{7,5},{8,10},{9,11},{10,... | collective-permute-start | bytes 393224 | tf_op jit(solution)/shard_map/ppermute | solution.py:695
  151.6 1.7 collective-permute-done.22.refs_6_
  153.3 6.7 %collective-permute-done.23.refs_7_ = bf16[1,16,4096]{2,1,0:T(8,128)(2,1)S(1)} collective-permute-done((bf16[1,16,4096]{2,1,0:T(8,128)(2,1)S(1)}, bf16[1,16,4096]{2,1,0:T(8,128)(2,1)S(1)}, u32[]{:S(2)}, u32[]{:S(2)}) %collective-permute-start.23) | collective-permute-done | bytes 131104 | tf_op jit(solution)/shard_map/ppermute | solution.py:695
  160.2 1.6 collective-permute-start.26
  162.3 2.6 %collective-permute-start.29 = (bf16[1,16,4096]{2,1,0:T(8,128)(2,1)S(1)}, bf16[1,16,4096]{2,1,0:T(8,128)(2,1)S(1)}, u32[]{:S(2)}, u32[]{:S(2)}) collective-permute-start(bf16[1,16,4096]{2,1,0:T(8,128)(2,1)S(1)} %get-tuple-element.181.refs_4_), channel_id=1, source_target_pairs={{0,3},{1,2},{2,1},{3,0},{4,7},{5,6},{6,5},{7,4},{8,11},{9,10},{10,... | collective-permute-start | bytes 393224 | tf_op jit(solution)/shard_map/ppermute | solution.py:695
  166.7 3.8 %collective-permute-done.29.refs_7_ = bf16[1,16,4096]{2,1,0:T(8,128)(2,1)S(1)} collective-permute-done((bf16[1,16,4096]{2,1,0:T(8,128)(2,1)S(1)}, bf16[1,16,4096]{2,1,0:T(8,128)(2,1)S(1)}, u32[]{:S(2)}, u32[]{:S(2)}) %collective-permute-start.29) | collective-permute-done | bytes 131104 | tf_op jit(solution)/shard_map/ppermute | solution.py:695
  170.5 4.8 %collective-permute-done.28.refs_6_ = bf16[1,16,4096]{2,1,0:T(8,128)(2,1)S(1)} collective-permute-done((bf16[1,16,4096]{2,1,0:T(8,128)(2,1)S(1)}, bf16[1,16,4096]{2,1,0:T(8,128)(2,1)S(1)}, u32[]{:S(2)}, u32[]{:S(2)}) %collective-permute-start.28) | collective-permute-done | bytes 131104 | tf_op jit(solution)/shard_map/ppermute | solution.py:695
  177.8 2.8 %collective-permute-start.31 = (bf16[1,16,4224]{2,1,0:T(8,128)(2,1)S(1)}, bf16[1,16,4224]{2,1,0:T(8,128)(2,1)S(1)}, u32[]{:S(2)}, u32[]{:S(2)}) collective-permute-start(bf16[1,16,4224]{2,1,0:T(8,128)(2,1)S(1)} %get-tuple-element.184), channel_id=1, source_target_pairs={{0,2},{1,3},{2,0},{3,1},{4,6},{5,7},{6,4},{7,5},{8,10},{9,11},{10,... | collective-permute-start | bytes 405512 | tf_op jit(solution)/shard_map/ppermute | solution.py:695
  180.6 1.6 collective-permute-start.32
  182.2 1.6 collective-permute-done.30.refs_2_
  183.8 6.5 %collective-permute-done.31.refs_3_ = bf16[1,16,4224]{2,1,0:T(8,128)(2,1)S(1)} collective-permute-done((bf16[1,16,4224]{2,1,0:T(8,128)(2,1)S(1)}, bf16[1,16,4224]{2,1,0:T(8,128)(2,1)S(1)}, u32[]{:S(2)}, u32[]{:S(2)}) %collective-permute-start.31) | collective-permute-done | bytes 135200 | tf_op jit(solution)/shard_map/ppermute | solution.py:695
  192.1 2.4 collective-permute-start.37
  196.4 3.7 %collective-permute-done.37.refs_3_ = bf16[1,16,4224]{2,1,0:T(8,128)(2,1)S(1)} collective-permute-done((bf16[1,16,4224]{2,1,0:T(8,128)(2,1)S(1)}, bf16[1,16,4224]{2,1,0:T(8,128)(2,1)S(1)}, u32[]{:S(2)}, u32[]{:S(2)}) %collective-permute-start.37) | collective-permute-done | bytes 135200 | tf_op jit(solution)/shard_map/ppermute | solution.py:695
  200.1 3.8 %collective-permute-done.36.refs_2_ = bf16[1,16,4224]{2,1,0:T(8,128)(2,1)S(1)} collective-permute-done((bf16[1,16,4224]{2,1,0:T(8,128)(2,1)S(1)}, bf16[1,16,4224]{2,1,0:T(8,128)(2,1)S(1)}, u32[]{:S(2)}, u32[]{:S(2)}) %collective-permute-start.36) | collective-permute-done | bytes 135200 | tf_op jit(solution)/shard_map/ppermute | solution.py:695
  208.9 7.8 %collective-permute-done.44.refs_10_ = bf16[256,512]{1,0:T(8,128)(2,1)S(1)} collective-permute-done((bf16[256,512]{1,0:T(8,128)(2,1)S(1)}, bf16[256,512]{1,0:T(8,128)(2,1)S(1)}, u32[]{:S(2)}, u32[]{:S(2)}) %collective-permute-start.44) | collective-permute-done | bytes 262176 | tf_op jit(solution)/shard_map/ppermute | solution.py:658
  221.0 4.5 %shard_map.278 = (f32[512,2048]{1,0:T(8,128)}, f32[2048,512]{1,0:T(8,128)}) custom-call(s32[2]{0:T(128)S(1)} %pad_add_fusion.1.codes, bf16[16,16,4096]{2,1,0:T(8,128)(2,1)S(1)} %get-tuple-element.193.refs_0_, bf16[16,16,4096]{2,1,0:T(8,128)(2,1)S(1)} %collective-permute-done.42.refs_4_.refs_1_), custom_call_target="tpu_custom_call" | custom-call | flops 6000000000 | tf_op jit(solution)/shard_map/pallas_call | solution.py:613
  226.3 10.6 %collective-permute-done.48.refs_8_ = bf16[256,512]{1,0:T(8,128)(2,1)S(1)} collective-permute-done((bf16[256,512]{1,0:T(8,128)(2,1)S(1)}, bf16[256,512]{1,0:T(8,128)(2,1)S(1)}, u32[]{:S(2)}, u32[]{:S(2)}) %collective-permute-start.48) | collective-permute-done | bytes 262176 | tf_op jit(solution)/shard_map/ppermute | solution.py:658
  237.2 2.7 %shard_map.280 = (f32[2,256,512]{2,1,0:T(8,128)}, f32[2,256,512]{2,1,0:T(8,128)}) custom-call(s32[2]{0:T(128)S(1)} %pad_add_fusion.order, s32[1]{0:T(128)} %bitcast.2.rank, bf16[2,256,512]{2,1,0:T(8,128)(2,1)S(1)} %copy-done.4, f32[512,512]{1,0:T(8,128)S(1)} %get-tuple-element.136.refs_4_.self_grad, ...), custom_call_target="tpu_custom_call" | custom-call | flops 3000000000 | tf_op jit(solution)/shard_map/pallas_call | solution.py:613
  239.9 1.5 collective-permute-done.49.refs_1_
  241.5 3.9 %shard_map.281 = (f32[512,1024]{1,0:T(8,128)}, f32[512,512]{1,0:T(8,128)}, f32[512,512]{1,0:T(8,128)}, f32[512,1536]{1,0:T(8,128)}, f32[512,512]{1,0:T(8,128)}, ...) custom-call(s32[2]{0:T(128)S(1)} %pad_add_fusion.1.codes, ...), custom_call_target="tpu_custom_call" | custom-call | flops 5000000000 | tf_op jit(solution)/shard_map/pallas_call | solution.py:613
  (117 shorter events, 27.5 us)
Async XLA Ops:
  2.9 18.9 %collective-permute-start = (bf16[512,512]{1,0:T(8,128)(2,1)}, bf16[512,512]{1,0:T(8,128)(2,1)S(1)}, u32[]{:S(2)}, u32[]{:S(2)}) collective-permute-start(bf16[512,512]{1,0:T(8,128)(2,1)} %get-tuple-element.118), channel_id=1, source_target_pairs={{0,2},{4,6},{8,10},{12,14},{16,18},{20,22},{24,26},{28,30}} | collective-permute-start | bytes 1572872 | tf_op jit(solution)/shard_map/ppermute | solution.py:674
  9.2 18.6 %collective-permute-start.6 = (bf16[256,512]{1,0:T(8,128)(2,1)}, bf16[256,512]{1,0:T(8,128)(2,1)S(1)}, u32[]{:S(2)}, u32[]{:S(2)}) collective-permute-start(bf16[256,512]{1,0:T(8,128)(2,1)} %get-tuple-element.120), channel_id=1, source_target_pairs={{0,3},{4,7},{8,11},{12,15},{16,19},{20,23},{24,27},{28,31}} | collective-permute-start | bytes 786440 | tf_op jit(solution)/shard_map/ppermute | solution.py:643
  10.8 22.3 %collective-permute-start.5 = (bf16[256,512]{1,0:T(8,128)(2,1)}, bf16[256,512]{1,0:T(8,128)(2,1)}, u32[]{:S(2)}, u32[]{:S(2)}) collective-permute-start(bf16[256,512]{1,0:T(8,128)(2,1)} %get-tuple-element.120), channel_id=1, source_target_pairs={{0,2},{1,3},{4,6},{5,7},{8,10},{9,11},{12,14},{13,15},{16,18},{17,... | collective-permute-start | bytes 786440 | tf_op jit(solution)/shard_map/ppermute | solution.py:643
  12.8 26.3 %collective-permute-start.4 = (bf16[256,512]{1,0:T(8,128)(2,1)}, bf16[256,512]{1,0:T(8,128)(2,1)}, u32[]{:S(2)}, u32[]{:S(2)}) collective-permute-start(bf16[256,512]{1,0:T(8,128)(2,1)} %get-tuple-element.120), channel_id=1, source_target_pairs={{0,1},{1,2},{2,3},{4,5},{5,6},{6,7},{8,9},{9,10},{10,11},{12,13},{... | collective-permute-start | bytes 786440 | tf_op jit(solution)/shard_map/ppermute | solution.py:643
  23.7 23.8 %collective-permute-start.8 = (bf16[256,512]{1,0:T(8,128)(2,1)}, bf16[256,512]{1,0:T(8,128)(2,1)}, u32[]{:S(2)}, u32[]{:S(2)}) collective-permute-start(bf16[256,512]{1,0:T(8,128)(2,1)} %get-tuple-element.220), channel_id=1, source_target_pairs={{0,1},{2,3},{4,5},{6,7},{8,9},{10,11},{12,13},{14,15},{16,17},{18,... | collective-permute-start | bytes 786440 | tf_op jit(solution)/shard_map/ppermute | solution.py:685
  27.8 33.9 %collective-permute-start.3 = (bf16[256,512]{1,0:T(8,128)(2,1)}, bf16[256,512]{1,0:T(8,128)(2,1)S(1)}, u32[]{:S(2)}, u32[]{:S(2)}) collective-permute-start(bf16[256,512]{1,0:T(8,128)(2,1)} %get-tuple-element.119), channel_id=1, source_target_pairs={{0,3},{1,0},{2,1},{3,2},{4,7},{5,4},{6,5},{7,6},{8,11},{9,8},{10,9... | collective-permute-start | bytes 786440 | tf_op jit(solution)/shard_map/ppermute | solution.py:643
  27.8 33.9 %collective-permute-start.2 = (bf16[256,512]{1,0:T(8,128)(2,1)}, bf16[256,512]{1,0:T(8,128)(2,1)S(1)}, u32[]{:S(2)}, u32[]{:S(2)}) collective-permute-start(bf16[256,512]{1,0:T(8,128)(2,1)} %get-tuple-element.119), channel_id=1, source_target_pairs={{0,2},{1,3},{2,0},{3,1},{4,6},{5,7},{6,4},{7,5},{8,10},{9,11},{10,... | collective-permute-start | bytes 786440 | tf_op jit(solution)/shard_map/ppermute | solution.py:643
  33.1 28.7 %collective-permute-start.1 = (bf16[256,512]{1,0:T(8,128)(2,1)}, bf16[256,512]{1,0:T(8,128)(2,1)S(1)}, u32[]{:S(2)}, u32[]{:S(2)}) collective-permute-start(bf16[256,512]{1,0:T(8,128)(2,1)} %get-tuple-element.119), channel_id=1, source_target_pairs={{0,1},{1,2},{2,3},{3,0},{4,5},{5,6},{6,7},{7,4},{8,9},{9,10},{10,1... | collective-permute-start | bytes 786440 | tf_op jit(solution)/shard_map/ppermute | solution.py:643
  39.1 26.4 %collective-permute-start.7 = (bf16[256,512]{1,0:T(8,128)(2,1)S(1)}, bf16[256,512]{1,0:T(8,128)(2,1)S(1)}, u32[]{:S(2)}, u32[]{:S(2)}) collective-permute-start(bf16[256,512]{1,0:T(8,128)(2,1)S(1)} %add.69), channel_id=1, source_target_pairs={{0,1},{2,3},{4,5},{6,7},{8,9},{10,11},{12,13},{14,15},{16,17},{18,... | collective-permute-start | bytes 786440 | tf_op jit(solution)/shard_map/ppermute | solution.py:685
  90.2 20.5 %collective-permute-start.9 = (bf16[16,16,4096]{2,1,0:T(8,128)(2,1)S(1)}, bf16[16,16,4096]{2,1,0:T(8,128)(2,1)S(1)}, u32[]{:S(2)}, u32[]{:S(2)}) collective-permute-start(bf16[16,16,4096]{2,1,0:T(8,128)(2,1)S(1)} %get-tuple-element.147), channel_id=1, source_target_pairs={{0,4},{4,0},{8,12},{12,8},{16,20},{20,16},{24,28},{28,24},{1,5},{5... | collective-permute-start | bytes 6291464 | tf_op jit(solution)/shard_map/ppermute | solution.py:695
  100.1 28.0 %collective-permute-start.13 = (bf16[256,512]{1,0:T(8,128)(2,1)S(1)}, bf16[256,512]{1,0:T(8,128)(2,1)S(1)}, u32[]{:S(2)}, u32[]{:S(2)}) collective-permute-start(bf16[256,512]{1,0:T(8,128)(2,1)S(1)} %get-tuple-element.156), channel_id=1, source_target_pairs={{0,2},{1,3},{2,0},{3,1},{4,6},{5,7},{6,4},{7,5},{8,10},{9,11},{10,... | collective-permute-start | bytes 786440 | tf_op jit(solution)/shard_map/ppermute | solution.py:649
  103.5 24.5 %collective-permute-start.14 = (bf16[256,512]{1,0:T(8,128)(2,1)S(1)}, bf16[256,512]{1,0:T(8,128)(2,1)S(1)}, u32[]{:S(2)}, u32[]{:S(2)}) collective-permute-start(bf16[256,512]{1,0:T(8,128)(2,1)S(1)} %get-tuple-element.157), channel_id=1, source_target_pairs={{0,1},{1,2},{2,3},{3,0},{4,5},{5,6},{6,7},{7,4},{8,9},{9,10},{10,1... | collective-permute-start | bytes 786440 | tf_op jit(solution)/shard_map/ppermute | solution.py:649
  103.5 24.5 %collective-permute-start.12 = (bf16[512,512]{1,0:T(8,128)(2,1)S(1)}, bf16[512,512]{1,0:T(8,128)(2,1)S(1)}, u32[]{:S(2)}, u32[]{:S(2)}) collective-permute-start(bf16[512,512]{1,0:T(8,128)(2,1)S(1)} %get-tuple-element.155.refs_6_), channel_id=1, source_target_pairs={{0,3},{1,0},{2,1},{3,2},{4,7},{5,4},{6,5},{7,6},{8,11},{9,8},{10,9... | collective-permute-start | bytes 1572872 | tf_op jit(solution)/shard_map/ppermute | solution.py:649
  110.9 17.1 %collective-permute-start.10 = (bf16[8,16,2048]{2,1,0:T(8,128)(2,1)S(1)}, bf16[8,16,2048]{2,1,0:T(8,128)(2,1)S(1)}, u32[]{:S(2)}, u32[]{:S(2)}) collective-permute-start(bf16[8,16,2048]{2,1,0:T(8,128)(2,1)S(1)} %get-tuple-element.151), channel_id=1, source_target_pairs={{0,8},{4,12},{8,0},{12,4},{16,24},{20,28},{24,16},{28,20},{1,9},{5... | collective-permute-start | bytes 1572872 | tf_op jit(solution)/shard_map/ppermute | solution.py:695
  112.5 15.6 %collective-permute-start.11 = (bf16[8,16,2048]{2,1,0:T(8,128)(2,1)S(1)}, bf16[8,16,2048]{2,1,0:T(8,128)(2,1)S(1)}, u32[]{:S(2)}, u32[]{:S(2)}) collective-permute-start(bf16[8,16,2048]{2,1,0:T(8,128)(2,1)S(1)} %get-tuple-element.153), channel_id=1, source_target_pairs={{0,16},{4,20},{8,24},{12,28},{16,0},{20,4},{24,8},{28,12},{1,17},{... | collective-permute-start | bytes 1572872 | tf_op jit(solution)/shard_map/ppermute | solution.py:695
  128.3 16.4 %collective-permute-start.17 = (bf16[16,16,4224]{2,1,0:T(8,128)(2,1)S(1)}, bf16[16,16,4224]{2,1,0:T(8,128)(2,1)S(1)}, u32[]{:S(2)}, u32[]{:S(2)}) collective-permute-start(bf16[16,16,4224]{2,1,0:T(8,128)(2,1)S(1)} %get-tuple-element.164), channel_id=1, source_target_pairs={{0,4},{4,0},{8,12},{12,8},{16,20},{20,16},{24,28},{28,24},{1,5},{5... | collective-permute-start | bytes 6488072 | tf_op jit(solution)/shard_map/ppermute | solution.py:695
  128.4 4.8 %collective-permute-start.18 = (bf16[256,512]{1,0:T(8,128)(2,1)S(1)}, bf16[256,512]{1,0:T(8,128)(2,1)S(1)}, u32[]{:S(2)}, u32[]{:S(2)}) collective-permute-start(bf16[256,512]{1,0:T(8,128)(2,1)S(1)} %get-tuple-element.167), channel_id=1, source_target_pairs={{3,2},{7,6},{11,10},{15,14},{19,18},{23,22},{27,26},{31,30}} | collective-permute-start | bytes 786440 | tf_op jit(solution)/shard_map/ppermute | solution.py:653
  129.1 8.8 %collective-permute-start.16 = (bf16[4,16,2048]{2,1,0:T(8,128)(2,1)S(1)}, bf16[4,16,2048]{2,1,0:T(8,128)(2,1)S(1)}, u32[]{:S(2)}, u32[]{:S(2)}) collective-permute-start(bf16[4,16,2048]{2,1,0:T(8,128)(2,1)S(1)} %get-tuple-element.161), channel_id=1, source_target_pairs={{0,8},{4,12},{8,0},{12,4},{16,24},{20,28},{24,16},{28,20},{1,9},{5... | collective-permute-start | bytes 786440 | tf_op jit(solution)/shard_map/ppermute | solution.py:695
  130.0 14.7 %collective-permute-start.19 = (bf16[256,512]{1,0:T(8,128)(2,1)S(1)}, bf16[256,512]{1,0:T(8,128)(2,1)S(1)}, u32[]{:S(2)}, u32[]{:S(2)}) collective-permute-start(bf16[256,512]{1,0:T(8,128)(2,1)S(1)} %get-tuple-element.168.refs_10_), channel_id=1, source_target_pairs={{2,0},{6,4},{10,8},{14,12},{18,16},{22,20},{26,24},{30,28}} | collective-permute-start | bytes 786440 | tf_op jit(solution)/shard_map/ppermute | solution.py:658
  131.5 13.2 %collective-permute-start.15 = (bf16[4,16,2048]{2,1,0:T(8,128)(2,1)S(1)}, bf16[4,16,2048]{2,1,0:T(8,128)(2,1)S(1)}, u32[]{:S(2)}, u32[]{:S(2)}) collective-permute-start(bf16[4,16,2048]{2,1,0:T(8,128)(2,1)S(1)} %get-tuple-element.159), channel_id=1, source_target_pairs={{0,16},{4,20},{8,24},{12,28},{16,0},{20,4},{24,8},{28,12},{1,17},{... | collective-permute-start | bytes 786440 | tf_op jit(solution)/shard_map/ppermute | solution.py:695
  145.1 14.9 %collective-permute-start.21 = (bf16[8,16,2176]{2,1,0:T(8,128)(2,1)S(1)}, bf16[8,16,2176]{2,1,0:T(8,128)(2,1)S(1)}, u32[]{:S(2)}, u32[]{:S(2)}) collective-permute-start(bf16[8,16,2176]{2,1,0:T(8,128)(2,1)S(1)} %get-tuple-element.172), channel_id=1, source_target_pairs={{0,16},{4,20},{8,24},{12,28},{16,0},{20,4},{24,8},{28,12},{1,17},{... | collective-permute-start | bytes 1671176 | tf_op jit(solution)/shard_map/ppermute | solution.py:695
  146.7 13.3 %collective-permute-start.20 = (bf16[8,16,2048]{2,1,0:T(8,128)(2,1)S(1)}, bf16[8,16,2048]{2,1,0:T(8,128)(2,1)S(1)}, u32[]{:S(2)}, u32[]{:S(2)}) collective-permute-start(bf16[8,16,2048]{2,1,0:T(8,128)(2,1)S(1)} %get-tuple-element.170), channel_id=1, source_target_pairs={{0,8},{4,12},{8,0},{12,4},{16,24},{20,28},{24,16},{28,20},{1,9},{5... | collective-permute-start | bytes 1572872 | tf_op jit(solution)/shard_map/ppermute | solution.py:695
  147.2 6.1 %collective-permute-start.22 = (bf16[1,16,4096]{2,1,0:T(8,128)(2,1)S(1)}, bf16[1,16,4096]{2,1,0:T(8,128)(2,1)S(1)}, u32[]{:S(2)}, u32[]{:S(2)}) collective-permute-start(bf16[1,16,4096]{2,1,0:T(8,128)(2,1)S(1)} %get-tuple-element.174), channel_id=1, source_target_pairs={{0,1},{1,0},{2,3},{3,2},{4,5},{5,4},{6,7},{7,6},{8,9},{9,8},{10,11... | collective-permute-start | bytes 393224 | tf_op jit(solution)/shard_map/ppermute | solution.py:695
  148.1 11.9 %collective-permute-start.23 = (bf16[1,16,4096]{2,1,0:T(8,128)(2,1)S(1)}, bf16[1,16,4096]{2,1,0:T(8,128)(2,1)S(1)}, u32[]{:S(2)}, u32[]{:S(2)}) collective-permute-start(bf16[1,16,4096]{2,1,0:T(8,128)(2,1)S(1)} %get-tuple-element.175), channel_id=1, source_target_pairs={{0,2},{1,3},{2,0},{3,1},{4,6},{5,7},{6,4},{7,5},{8,10},{9,11},{10,... | collective-permute-start | bytes 393224 | tf_op jit(solution)/shard_map/ppermute | solution.py:695
  151.1 9.0 %collective-permute-start.24 = (bf16[1,16,4096]{2,1,0:T(8,128)(2,1)S(1)}, bf16[1,16,4096]{2,1,0:T(8,128)(2,1)S(1)}, u32[]{:S(2)}, u32[]{:S(2)}) collective-permute-start(bf16[1,16,4096]{2,1,0:T(8,128)(2,1)S(1)} %get-tuple-element.176), channel_id=1, source_target_pairs={{0,3},{1,2},{2,1},{3,0},{4,7},{5,6},{6,5},{7,4},{8,11},{9,10},{10,... | collective-permute-start | bytes 393224 | tf_op jit(solution)/shard_map/ppermute | solution.py:695
  160.2 15.1 %collective-permute-start.26 = (bf16[4,16,2176]{2,1,0:T(8,128)(2,1)S(1)}, bf16[4,16,2176]{2,1,0:T(8,128)(2,1)S(1)}, u32[]{:S(2)}, u32[]{:S(2)}) collective-permute-start(bf16[4,16,2176]{2,1,0:T(8,128)(2,1)S(1)} %get-tuple-element.180), channel_id=1, source_target_pairs={{0,8},{4,12},{8,0},{12,4},{16,24},{20,28},{24,16},{28,20},{1,9},{5... | collective-permute-start | bytes 835592 | tf_op jit(solution)/shard_map/ppermute | solution.py:695
  161.8 13.5 %collective-permute-start.25 = (bf16[4,16,2048]{2,1,0:T(8,128)(2,1)S(1)}, bf16[4,16,2048]{2,1,0:T(8,128)(2,1)S(1)}, u32[]{:S(2)}, u32[]{:S(2)}) collective-permute-start(bf16[4,16,2048]{2,1,0:T(8,128)(2,1)S(1)} %get-tuple-element.178), channel_id=1, source_target_pairs={{0,16},{4,20},{8,24},{12,28},{16,0},{20,4},{24,8},{28,12},{1,17},{... | collective-permute-start | bytes 786440 | tf_op jit(solution)/shard_map/ppermute | solution.py:695
  162.3 8.2 %collective-permute-start.29 = (bf16[1,16,4096]{2,1,0:T(8,128)(2,1)S(1)}, bf16[1,16,4096]{2,1,0:T(8,128)(2,1)S(1)}, u32[]{:S(2)}, u32[]{:S(2)}) collective-permute-start(bf16[1,16,4096]{2,1,0:T(8,128)(2,1)S(1)} %get-tuple-element.181.refs_4_), channel_id=1, source_target_pairs={{0,3},{1,2},{2,1},{3,0},{4,7},{5,6},{6,5},{7,4},{8,11},{9,10},{10,... | collective-permute-start | bytes 393224 | tf_op jit(solution)/shard_map/ppermute | solution.py:695
  164.9 10.4 %collective-permute-start.28 = (bf16[1,16,4096]{2,1,0:T(8,128)(2,1)S(1)}, bf16[1,16,4096]{2,1,0:T(8,128)(2,1)S(1)}, u32[]{:S(2)}, u32[]{:S(2)}) collective-permute-start(bf16[1,16,4096]{2,1,0:T(8,128)(2,1)S(1)} %get-tuple-element.181.refs_4_), channel_id=1, source_target_pairs={{0,2},{1,3},{2,0},{3,1},{4,6},{5,7},{6,4},{7,5},{8,10},{9,11},{10,... | collective-permute-start | bytes 393224 | tf_op jit(solution)/shard_map/ppermute | solution.py:695
  165.7 9.6 %collective-permute-start.27 = (bf16[1,16,4096]{2,1,0:T(8,128)(2,1)S(1)}, bf16[1,16,4096]{2,1,0:T(8,128)(2,1)S(1)}, u32[]{:S(2)}, u32[]{:S(2)}) collective-permute-start(bf16[1,16,4096]{2,1,0:T(8,128)(2,1)S(1)} %get-tuple-element.181.refs_4_), channel_id=1, source_target_pairs={{0,1},{1,0},{2,3},{3,2},{4,5},{5,4},{6,7},{7,6},{8,9},{9,8},{10,11... | collective-permute-start | bytes 393224 | tf_op jit(solution)/shard_map/ppermute | solution.py:695
  175.4 14.9 %collective-permute-start.33 = (bf16[4,16,2048]{2,1,0:T(8,128)(2,1)S(1)}, bf16[4,16,2048]{2,1,0:T(8,128)(2,1)S(1)}, u32[]{:S(2)}, u32[]{:S(2)}) collective-permute-start(bf16[4,16,2048]{2,1,0:T(8,128)(2,1)S(1)} %get-tuple-element.186.refs_5_), channel_id=1, source_target_pairs={{0,16},{4,20},{8,24},{12,28},{16,0},{20,4},{24,8},{28,12},{1,17},{... | collective-permute-start | bytes 786440 | tf_op jit(solution)/shard_map/ppermute | solution.py:695
  176.5 13.8 %collective-permute-start.34 = (bf16[4,16,2048]{2,1,0:T(8,128)(2,1)S(1)}, bf16[4,16,2048]{2,1,0:T(8,128)(2,1)S(1)}, u32[]{:S(2)}, u32[]{:S(2)}) collective-permute-start(bf16[4,16,2048]{2,1,0:T(8,128)(2,1)S(1)} %get-tuple-element.187.refs_7_), channel_id=1, source_target_pairs={{0,8},{4,12},{8,0},{12,4},{16,24},{20,28},{24,16},{28,20},{1,9},{5... | collective-permute-start | bytes 786440 | tf_op jit(solution)/shard_map/ppermute | solution.py:695
  177.8 6.0 %collective-permute-start.30 = (bf16[1,16,4224]{2,1,0:T(8,128)(2,1)S(1)}, bf16[1,16,4224]{2,1,0:T(8,128)(2,1)S(1)}, u32[]{:S(2)}, u32[]{:S(2)}) collective-permute-start(bf16[1,16,4224]{2,1,0:T(8,128)(2,1)S(1)} %get-tuple-element.183), channel_id=1, source_target_pairs={{0,1},{1,0},{2,3},{3,2},{4,5},{5,4},{6,7},{7,6},{8,9},{9,8},{10,11... | collective-permute-start | bytes 405512 | tf_op jit(solution)/shard_map/ppermute | solution.py:695
  177.8 12.5 %collective-permute-start.31 = (bf16[1,16,4224]{2,1,0:T(8,128)(2,1)S(1)}, bf16[1,16,4224]{2,1,0:T(8,128)(2,1)S(1)}, u32[]{:S(2)}, u32[]{:S(2)}) collective-permute-start(bf16[1,16,4224]{2,1,0:T(8,128)(2,1)S(1)} %get-tuple-element.184), channel_id=1, source_target_pairs={{0,2},{1,3},{2,0},{3,1},{4,6},{5,7},{6,4},{7,5},{8,10},{9,11},{10,... | collective-permute-start | bytes 405512 | tf_op jit(solution)/shard_map/ppermute | solution.py:695
  180.6 9.7 %collective-permute-start.32 = (bf16[1,16,4224]{2,1,0:T(8,128)(2,1)S(1)}, bf16[1,16,4224]{2,1,0:T(8,128)(2,1)S(1)}, u32[]{:S(2)}, u32[]{:S(2)}) collective-permute-start(bf16[1,16,4224]{2,1,0:T(8,128)(2,1)S(1)} %get-tuple-element.185), channel_id=1, source_target_pairs={{0,3},{1,2},{2,1},{3,0},{4,7},{5,6},{6,5},{7,4},{8,11},{9,10},{10,... | collective-permute-start | bytes 405512 | tf_op jit(solution)/shard_map/ppermute | solution.py:695
  190.4 13.5 %collective-permute-start.38 = (bf16[8,16,2048]{2,1,0:T(8,128)(2,1)S(1)}, bf16[8,16,2048]{2,1,0:T(8,128)(2,1)S(1)}, u32[]{:S(2)}, u32[]{:S(2)}) collective-permute-start(bf16[8,16,2048]{2,1,0:T(8,128)(2,1)S(1)} %get-tuple-element.189.refs_4_), channel_id=1, source_target_pairs={{0,8},{4,12},{8,0},{12,4},{16,24},{20,28},{24,16},{28,20},{1,9},{5... | collective-permute-start | bytes 1572872 | tf_op jit(solution)/shard_map/ppermute | solution.py:695
  190.8 13.2 %collective-permute-start.39 = (bf16[8,16,2048]{2,1,0:T(8,128)(2,1)S(1)}, bf16[8,16,2048]{2,1,0:T(8,128)(2,1)S(1)}, u32[]{:S(2)}, u32[]{:S(2)}) collective-permute-start(bf16[8,16,2048]{2,1,0:T(8,128)(2,1)S(1)} %get-tuple-element.190.refs_6_), channel_id=1, source_target_pairs={{0,16},{4,20},{8,24},{12,28},{16,0},{20,4},{24,8},{28,12},{1,17},{... | collective-permute-start | bytes 1572872 | tf_op jit(solution)/shard_map/ppermute | solution.py:695
  192.1 8.1 %collective-permute-start.37 = (bf16[1,16,4224]{2,1,0:T(8,128)(2,1)S(1)}, bf16[1,16,4224]{2,1,0:T(8,128)(2,1)S(1)}, u32[]{:S(2)}, u32[]{:S(2)}) collective-permute-start(bf16[1,16,4224]{2,1,0:T(8,128)(2,1)S(1)} %get-tuple-element.188.refs_0_), channel_id=1, source_target_pairs={{0,3},{1,2},{2,1},{3,0},{4,7},{5,6},{6,5},{7,4},{8,11},{9,10},{10,... | collective-permute-start | bytes 405512 | tf_op jit(solution)/shard_map/ppermute | solution.py:695
  194.4 9.5 %collective-permute-start.36 = (bf16[1,16,4224]{2,1,0:T(8,128)(2,1)S(1)}, bf16[1,16,4224]{2,1,0:T(8,128)(2,1)S(1)}, u32[]{:S(2)}, u32[]{:S(2)}) collective-permute-start(bf16[1,16,4224]{2,1,0:T(8,128)(2,1)S(1)} %get-tuple-element.188.refs_0_), channel_id=1, source_target_pairs={{0,2},{1,3},{2,0},{3,1},{4,6},{5,7},{6,4},{7,5},{8,10},{9,11},{10,... | collective-permute-start | bytes 405512 | tf_op jit(solution)/shard_map/ppermute | solution.py:695
  195.5 8.4 %collective-permute-start.35 = (bf16[1,16,4224]{2,1,0:T(8,128)(2,1)S(1)}, bf16[1,16,4224]{2,1,0:T(8,128)(2,1)S(1)}, u32[]{:S(2)}, u32[]{:S(2)}) collective-permute-start(bf16[1,16,4224]{2,1,0:T(8,128)(2,1)S(1)} %get-tuple-element.188.refs_0_), channel_id=1, source_target_pairs={{0,1},{1,0},{2,3},{3,2},{4,5},{5,4},{6,7},{7,6},{8,9},{9,8},{10,11... | collective-permute-start | bytes 405512 | tf_op jit(solution)/shard_map/ppermute | solution.py:695
  204.1 12.5 %collective-permute-start.42 = (bf16[16,16,4096]{2,1,0:T(8,128)(2,1)S(1)}, bf16[16,16,4096]{2,1,0:T(8,128)(2,1)S(1)}, u32[]{:S(2)}, u32[]{:S(2)}) collective-permute-start(bf16[16,16,4096]{2,1,0:T(8,128)(2,1)S(1)} %get-tuple-element.193.refs_0_), channel_id=1, source_target_pairs={{0,4},{4,0},{8,12},{12,8},{16,20},{20,16},{24,28},{28,24},{1,5},{5... | collective-permute-start | bytes 6291464 | tf_op jit(solution)/shard_map/ppermute | solution.py:695
  204.2 12.5 %collective-permute-start.41 = (bf16[4,16,2176]{2,1,0:T(8,128)(2,1)S(1)}, bf16[4,16,2176]{2,1,0:T(8,128)(2,1)S(1)}, u32[]{:S(2)}, u32[]{:S(2)}) collective-permute-start(bf16[4,16,2176]{2,1,0:T(8,128)(2,1)S(1)} %get-tuple-element.192.refs_2_), channel_id=1, source_target_pairs={{0,8},{4,12},{8,0},{12,4},{16,24},{20,28},{24,16},{28,20},{1,9},{5... | collective-permute-start | bytes 835592 | tf_op jit(solution)/shard_map/ppermute | solution.py:695
  206.4 10.3 %collective-permute-start.44 = (bf16[256,512]{1,0:T(8,128)(2,1)S(1)}, bf16[256,512]{1,0:T(8,128)(2,1)S(1)}, u32[]{:S(2)}, u32[]{:S(2)}) collective-permute-start(bf16[256,512]{1,0:T(8,128)(2,1)S(1)} %get-tuple-element.198.refs_9_), channel_id=1, source_target_pairs={{1,0},{3,2},{5,4},{7,6},{9,8},{11,10},{13,12},{15,14},{17,16},{19,... | collective-permute-start | bytes 786440 | tf_op jit(solution)/shard_map/ppermute | solution.py:658
  207.7 9.0 %collective-permute-start.40 = (bf16[4,16,2048]{2,1,0:T(8,128)(2,1)S(1)}, bf16[4,16,2048]{2,1,0:T(8,128)(2,1)S(1)}, u32[]{:S(2)}, u32[]{:S(2)}) collective-permute-start(bf16[4,16,2048]{2,1,0:T(8,128)(2,1)S(1)} %get-tuple-element.191.refs_0_), channel_id=1, source_target_pairs={{0,16},{4,20},{8,24},{12,28},{16,0},{20,4},{24,8},{28,12},{1,17},{... | collective-permute-start | bytes 786440 | tf_op jit(solution)/shard_map/ppermute | solution.py:695
  216.9 9.4 %collective-permute-start.45 = (bf16[256,512]{1,0:T(8,128)(2,1)S(1)}, bf16[256,512]{1,0:T(8,128)(2,1)S(1)}, u32[]{:S(2)}, u32[]{:S(2)}) collective-permute-start(bf16[256,512]{1,0:T(8,128)(2,1)S(1)} %get-tuple-element.199), channel_id=1, source_target_pairs={{1,0},{2,1},{3,2},{5,4},{6,5},{7,6},{9,8},{10,9},{11,10},{13,12},{... | collective-permute-start | bytes 786440 | tf_op jit(solution)/shard_map/ppermute | solution.py:653
  218.2 18.8 %collective-permute-start.48 = (bf16[256,512]{1,0:T(8,128)(2,1)S(1)}, bf16[256,512]{1,0:T(8,128)(2,1)S(1)}, u32[]{:S(2)}, u32[]{:S(2)}) collective-permute-start(bf16[256,512]{1,0:T(8,128)(2,1)S(1)} %get-tuple-element.204.refs_7_), channel_id=1, source_target_pairs={{2,0},{6,4},{10,8},{14,12},{18,16},{22,20},{26,24},{30,28}} | collective-permute-start | bytes 786440 | tf_op jit(solution)/shard_map/ppermute | solution.py:658
  219.5 17.5 %collective-permute-start.46 = (bf16[8,16,2048]{2,1,0:T(8,128)(2,1)S(1)}, bf16[8,16,2048]{2,1,0:T(8,128)(2,1)S(1)}, u32[]{:S(2)}, u32[]{:S(2)}) collective-permute-start(bf16[8,16,2048]{2,1,0:T(8,128)(2,1)S(1)} %get-tuple-element.201.refs_0_), channel_id=1, source_target_pairs={{0,8},{4,12},{8,0},{12,4},{16,24},{20,28},{24,16},{28,20},{1,9},{5... | collective-permute-start | bytes 1572872 | tf_op jit(solution)/shard_map/ppermute | solution.py:695
  220.1 16.8 %collective-permute-start.47 = (bf16[8,16,2176]{2,1,0:T(8,128)(2,1)S(1)}, bf16[8,16,2176]{2,1,0:T(8,128)(2,1)S(1)}, u32[]{:S(2)}, u32[]{:S(2)}) collective-permute-start(bf16[8,16,2176]{2,1,0:T(8,128)(2,1)S(1)} %get-tuple-element.202.refs_2_), channel_id=1, source_target_pairs={{0,16},{4,20},{8,24},{12,28},{16,0},{20,4},{24,8},{28,12},{1,17},{... | collective-permute-start | bytes 1671176 | tf_op jit(solution)/shard_map/ppermute | solution.py:695
  (21 other events, 419.3 us)

commit v3 on v2

--- a/solution.py
+++ b/solution.py
@@ -858,26 +858,25 @@
         far_outs=(blocks + 1, blocks + 2),
         sems=3 * pairs,
     )
-    (a, a_send), (b, b_send), (e_long, *e_short) = small_steps(
+    (a, a_send), (b, b_send) = small_steps(
         [(add_halves, (a, a_got, own), [shape(4, wide[0])] * 2),
-         (add_halves, (b, b_got), [shape(4, wide[1])] * 2),
-         (add_returns, (e_parts[0], e_parts[1], *e_got),
+         (add_halves, (b, b_got), [shape(4, wide[1])] * 2)]
+    )
+    a_got, b_got = trade(a_send, "batch", 4), trade(b_send, "batch", 2)
+    ((e_long, *e_short),) = small_steps(
+        [(add_returns, (tied(e_parts[0], a_send), e_parts[1], *e_got),
           [((rows, width), WIDE)] + [(rows, width)] * (n // 4))]
     )
-    a_got, b_got = trade(a_send, "batch", 4), trade(b_send, "batch", 2)
-    e_got = [return_short(e_short[k], n, k, 2) for k in roots]
-    held = tied(parts[n - 1], a_send)
+    held = tied(parts[n - 1], e_short[0])
     for d in range(n - 2, 2, -1):
         held = parts[d] + hand_down(held, n, d + 1)
     long_got = hand_down(held, n, 3)
-    feed, (a, a_send, b, b_send), (held,), *e_short = small_steps(
+    feed, (a, a_send, b, b_send), (held,) = small_steps(
         [(add_to_pieces, (a, a_got, b, b_got), [shape(1, sum(wide))] * 4),
-         (add_core, (near, trade(tied(far, a_send), "batch", 1)),
+         (add_core, (near, trade(tied(far, e_short[0]), "batch", 1)),
           [shape(8, w) for w in wide_rest for _ in "ks"]),
          (add_all, (own, parts[2], long_got), [(rows, width)])]
-        + [(add_all, (own, e_short[k], e_got[k]), [(rows, width)]) for k in roots]
-    )
-    e_short = return_short_rest([v for v, in e_short], n)
+    )
     a_got, b_got = trade(a_send, "batch", 2), trade(b_send, "batch", 4)
     (a, a_send), (b, b_send), (feed,) = small_steps(
         [(add_halves, (a, a_got), [shape(4, wide_rest[0])] * 2),
@@ -902,18 +901,20 @@
           [shape(16, sum(wide))])]
     )
     ra_got, rb_got = trade(ra, "batch", 4), trade(rb, "batch", 2)
-    feed_got = trade(feed, "batch", 1)
     held, *shorts = tied((held, *parts[n:]), ra)
     long_got = hand_down(held, n, 2)
     got = [return_short(shorts[k], n, k, 1) for k in roots]
-    (ra,), (rb,), _, (held,), *shorts = small_steps(
+    e_got = [return_short(tied(e_short[k], ra), n, k, 2) for k in roots]
+    (ra,), (rb,), (held,), *shorts = small_steps(
         [(join, (ra, ra_got), [shape(8, wide_rest[0])]),
          (join, (rb, rb_got), [shape(8, wide_rest[1])]),
-         (note, (feed_got,), []),
          (add_all, (own, parts[1], long_got), [(rows, width)])]
         + [(add_all, (own, parts[n + k], got[k]), [(rows, width)]) for k in roots]
-    )
+        + [(add_all, (own, e_short[k], e_got[k]), [(rows, width)]) for k in roots]
+    )
+    shorts, e_short = shorts[: n // 4], return_short_rest([v for v, in shorts[n // 4 :]], n)
     ra_got, rb_got = trade(ra, "batch", 2), trade(rb, "batch", 4)
+    feed_got = trade(tied(feed, ra), "batch", 1)
     long_got = hand_down(held, n, 1)
     got = [return_short(shorts[k][0], n, k, 2) for k in roots]
     s_up, s_down = call(

time: 246 us -> 245 us (level)
  waiting for transfers between devices: 75.9 us -> 68.8 us
  starting transfers between devices: 82.6 us -> 88.3 us
    ppermute x3, waiting for transfers between devices: 25.3 us -> 8.05 us  [return_short(): return lax.ppermute(held, 'blk', pairs)]
    ppermute x3, waiting for transfers between devices: 0.16 us -> 6.51 us  [hand_down(): return lax.ppermute(held, 'blk', [(i, i - 1) for i in range(distance, n)])]
    ppermute x32, starting transfers between devices: 35.8 us -> 41.5 us  [trade(): lax.ppermute(v, axis, [(i, i ^ distance) for i in range(lax.axis_size(axi...]
    ppermute x32, waiting for transfers between devices: 38.9 us -> 42.7 us  [trade(): lax.ppermute(v, axis, [(i, i ^ distance) for i in range(lax.axis_size(axi...]
    pallas_call x19 -> x20, Pallas kernels: 78.1 us -> 78.1 us  [call(): pl.pallas_call(kernel, out_shape=[jax.ShapeDtypeStruct(s, t) for s, t in...]
  transfers between devices with their start and end apart: 50 -> 50, of which waited for: 17 -> 18; matrix products, arithmetic and copies ran while one was open for 1% -> 1% of each run, Pallas kernels for 19% -> 19%
where the time goes in v3:
time: 245 us; the launch traced here: 244 us
  starting transfers between devices  88.3 us (36%)
  Pallas kernels  78.1 us (32%)
  waiting for transfers between devices  68.8 us (28%)
  local copies, waits for them, and re-layouts  4.29 us (2%)
  between operations  2.49 us (1%)
    pallas_call x20, Pallas kernels, call(): pl.pallas_call(kernel, out_shape=[jax.ShapeDtypeStruct(s, t) for s, t in...  78.1 us
    ppermute x32, waiting for transfers between devices, trade(): lax.ppermute(v, axis, [(i, i ^ distance) for i in range(lax.axis_size(axi...  42.7 us
    ppermute x32, starting transfers between devices, trade(): lax.ppermute(v, axis, [(i, i ^ distance) for i in range(lax.axis_size(axi...  41.5 us
    ppermute x6, starting transfers between devices, send_long(): got.append(lax.ppermute(block, 'blk', pairs))  16.1 us
    ppermute x2, starting transfers between devices, send_short_rest(): terms[root].append(lax.ppermute(held, 'blk', pairs))  10.4 us
    ppermute x3, waiting for transfers between devices, return_short(): return lax.ppermute(held, 'blk', pairs)  8.05 us
    ppermute x3, starting transfers between devices, return_long(): return lax.ppermute(block, 'blk', pairs)  7.25 us
    ppermute x3, waiting for transfers between devices, hand_down(): return lax.ppermute(held, 'blk', [(i, i - 1) for i in range(distance, n)])  6.51 us
  transfers between devices with their start and end apart: 50, of which 18 were waited for; matrix products, arithmetic and copies ran while one was open for 1% of the time, Pallas kernels for 19%

profile of v3, /device:TPU:0, one launch (start us, length us, event | category | flops | bytes accessed | tf_op | source)
XLA Modules:
  0.0 244.2 jit_solution(12335563585712588769)
XLA Ops:
  0.7 2.2 shard_map.263
  2.9 6.2 %collective-permute-start = (bf16[512,512]{1,0:T(8,128)(2,1)}, bf16[512,512]{1,0:T(8,128)(2,1)S(1)}, u32[]{:S(2)}, u32[]{:S(2)}) collective-permute-start(bf16[512,512]{1,0:T(8,128)(2,1)} %get-tuple-element.121), channel_id=1, source_target_pairs={{0,2},{4,6},{8,10},{12,14},{16,18},{20,22},{24,26},{28,30}} | collective-permute-start | bytes 1572872 | tf_op jit(solution)/shard_map/ppermute | solution.py:674
  9.2 1.6 collective-permute-start.6
  10.8 2.0 collective-permute-start.5
  12.8 3.2 %collective-permute-start.4 = (bf16[256,512]{1,0:T(8,128)(2,1)}, bf16[256,512]{1,0:T(8,128)(2,1)}, u32[]{:S(2)}, u32[]{:S(2)}) collective-permute-start(bf16[256,512]{1,0:T(8,128)(2,1)} %get-tuple-element.123), channel_id=1, source_target_pairs={{0,1},{1,2},{2,3},{4,5},{5,6},{6,7},{8,9},{9,10},{10,11},{12,13},{... | collective-permute-start | bytes 786440 | tf_op jit(solution)/shard_map/ppermute | solution.py:643
  16.0 5.9 %collective-permute-done = bf16[512,512]{1,0:T(8,128)(2,1)S(1)} collective-permute-done((bf16[512,512]{1,0:T(8,128)(2,1)}, bf16[512,512]{1,0:T(8,128)(2,1)S(1)}, u32[]{:S(2)}, u32[]{:S(2)}) %collective-permute-start) | collective-permute-done | bytes 524320 | tf_op jit(solution)/shard_map/ppermute | solution.py:674
  21.8 1.9 slice_add_fusion
  23.7 2.0 collective-permute-start.8
  27.8 3.4 %collective-permute-start.2 = (bf16[256,512]{1,0:T(8,128)(2,1)}, bf16[256,512]{1,0:T(8,128)(2,1)S(1)}, u32[]{:S(2)}, u32[]{:S(2)}) collective-permute-start(bf16[256,512]{1,0:T(8,128)(2,1)} %get-tuple-element.122), channel_id=1, source_target_pairs={{0,2},{1,3},{2,0},{3,1},{4,6},{5,7},{6,4},{7,5},{8,10},{9,11},{10,... | collective-permute-start | bytes 786440 | tf_op jit(solution)/shard_map/ppermute | solution.py:643
  31.2 1.8 collective-permute-done.5.refs_1_
  33.1 6.0 %collective-permute-start.1 = (bf16[256,512]{1,0:T(8,128)(2,1)}, bf16[256,512]{1,0:T(8,128)(2,1)S(1)}, u32[]{:S(2)}, u32[]{:S(2)}) collective-permute-start(bf16[256,512]{1,0:T(8,128)(2,1)} %get-tuple-element.122), channel_id=1, source_target_pairs={{0,1},{1,2},{2,3},{3,0},{4,5},{5,6},{6,7},{7,4},{8,9},{9,10},{10,1... | collective-permute-start | bytes 786440 | tf_op jit(solution)/shard_map/ppermute | solution.py:643
  39.1 8.4 %collective-permute-start.7 = (bf16[256,512]{1,0:T(8,128)(2,1)S(1)}, bf16[256,512]{1,0:T(8,128)(2,1)S(1)}, u32[]{:S(2)}, u32[]{:S(2)}) collective-permute-start(bf16[256,512]{1,0:T(8,128)(2,1)S(1)} %add.69), channel_id=1, source_target_pairs={{0,1},{2,3},{4,5},{6,7},{8,9},{10,11},{12,13},{14,15},{16,17},{18,... | collective-permute-start | bytes 786440 | tf_op jit(solution)/shard_map/ppermute | solution.py:685
  50.5 11.2 %shard_map.264 = (bf16[512,512]{1,0:T(8,128)(2,1)S(1)}, bf16[11520,3072]{1,0:T(8,128)(2,1)}, bf16[512,512]{1,0:T(8,128)(2,1)S(1)}, f32[8,512]{1,0:T(8,128)S(1)},...) custom-call(s32[2]{0:T(128)S(1)} %pad_add_fusion.order, ...), custom_call_target="tpu_custom_call" | custom-call | flops 12000000000 | tf_op jit(solution)/shard_map/pallas_call | solution.py:613
  61.7 3.8 %collective-permute-done.7.refs_5_ = bf16[256,512]{1,0:T(8,128)(2,1)S(1)} collective-permute-done((bf16[256,512]{1,0:T(8,128)(2,1)S(1)}, bf16[256,512]{1,0:T(8,128)(2,1)S(1)}, u32[]{:S(2)}, u32[]{:S(2)}) %collective-permute-start.7) | collective-permute-done | bytes 262176 | tf_op jit(solution)/shard_map/ppermute | solution.py:685
  65.6 9.9 %shard_map.265 = (bf16[11520,3072]{1,0:T(8,128)(2,1)}, bf16[512,512]{1,0:T(8,128)(2,1)S(1)}, f32[8,512]{1,0:T(8,128)S(1)}, f32[512,512]{1,0:T(8,128)S(1)}, bf16[1,256,512]{2,1,0:T(8,128)(2,1)S(1)}) custom-call(s32[2]{0:T(128)S(1)} %pad_add_fusion.order, s32[1]{0:T(128)} %bitcast.2.rank, s32[2,4]{1,0:T(2,128)S(1)} %copy-done.15, ...), custom_call_target="tpu_custom_call" | custom-call | flops 11000000512 | tf_op jit(solution)/shard_map/pallas_call | solution.py:613
  75.5 14.7 %shard_map.266 = (bf16[2,256,512]{2,1,0:T(8,128)(2,1)}, f32[512,512]{1,0:T(8,128)S(1)}, bf16[16,16,4096]{2,1,0:T(8,128)(2,1)S(1)}, bf16[16,16,4096]{2,1,0:T(8,12...) custom-call(s32[2]{0:T(128)S(1)} %pad_add_fusion.order, s32[2]{0:T(128)S(1)} %pad_add_fusion.1.codes, ...), custom_call_target="tpu_custom_call" | custom-call | flops 14000000000 | tf_op jit(solution)/shard_map/pallas_call | solution.py:613
  90.3 9.8 %shard_map.267 = (bf16[256,512]{1,0:T(8,128)(2,1)S(1)}, bf16[512,512]{1,0:T(8,128)(2,1)S(1)}, bf16[256,512]{1,0:T(8,128)(2,1)S(1)}, bf16[256,512]{1,0:T(8,128)(2...) custom-call(f32[512,512]{1,0:T(8,128)S(1)} %get-tuple-element.131.grad.refs_4_, ...), custom_call_target="tpu_custom_call" | custom-call | flops 10000000000 | tf_op jit(solution)/shard_map/pallas_call | solution.py:613
  100.1 3.4 %collective-permute-start.15 = (bf16[256,512]{1,0:T(8,128)(2,1)S(1)}, bf16[256,512]{1,0:T(8,128)(2,1)S(1)}, u32[]{:S(2)}, u32[]{:S(2)}) collective-permute-start(bf16[256,512]{1,0:T(8,128)(2,1)S(1)} %get-tuple-element.166), channel_id=1, source_target_pairs={{0,2},{1,3},{2,0},{3,1},{4,6},{5,7},{6,4},{7,5},{8,10},{9,11},{10,... | collective-permute-start | bytes 786440 | tf_op jit(solution)/shard_map/ppermute | solution.py:649
  103.6 3.8 %collective-permute-start.14 = (bf16[512,512]{1,0:T(8,128)(2,1)S(1)}, bf16[512,512]{1,0:T(8,128)(2,1)S(1)}, u32[]{:S(2)}, u32[]{:S(2)}) collective-permute-start(bf16[512,512]{1,0:T(8,128)(2,1)S(1)} %get-tuple-element.165.refs_1_), channel_id=1, source_target_pairs={{0,3},{1,0},{2,1},{3,2},{4,7},{5,4},{6,5},{7,6},{8,11},{9,8},{10,9... | collective-permute-start | bytes 1572872 | tf_op jit(solution)/shard_map/ppermute | solution.py:649
  107.4 3.4 %shard_map.268 = (f32[512,512]{1,0:T(8,128)S(1)}, bf16[512,2048]{1,0:T(8,128)(2,1)S(1)}, f32[2,512]{1,0:T(2,128)S(1)}) custom-call(s32[2]{0:T(128)S(1)} %pad_add_fusion.order, bf16[2,256,512]{2,1,0:T(8,128)(2,1)S(1)} %copy-done.12, bf16[256,512]{1,0:T(8,128)(2,1)S(1)} %collective-permute-done.1.refs_0_, bf16[256,512]{1,0:T(8,128)(2,1)S(1)} %collective-permute-done.2.refs_1_, ...), custom_call_target="tpu_custom_call" | custom-call | flops 4000000000 | tf_op jit(solution)/shard_map/pallas_call | solution.py:613
  111.0 1.5 collective-permute-start.10
  114.1 14.0 %shard_map.270 = (bf16[256,512]{1,0:T(8,128)(2,1)S(1)}, bf16[256,512]{1,0:T(8,128)(2,1)S(1)}, bf16[256,512]{1,0:T(8,128)(2,1)S(1)}, bf16[256,512]{1,0:T(8,128)(2...) custom-call(s32[2]{0:T(128)S(1)} %pad_add_fusion.order, ...), custom_call_target="tpu_custom_call" | custom-call | flops 14000000000 | tf_op jit(solution)/shard_map/pallas_call | solution.py:613
  131.8 6.4 %collective-permute-done.13.refs_3_ = bf16[4,16,2048]{2,1,0:T(8,128)(2,1)S(1)} collective-permute-done((bf16[4,16,2048]{2,1,0:T(8,128)(2,1)S(1)}, bf16[4,16,2048]{2,1,0:T(8,128)(2,1)S(1)}, u32[]{:S(2)}, u32[]{:S(2)}) %collective-permute-start.13) | collective-permute-done | bytes 262176 | tf_op jit(solution)/shard_map/ppermute | solution.py:695
  139.0 1.6 collective-permute-start.20
  141.1 6.1 %collective-permute-start.21 = (bf16[1,16,4096]{2,1,0:T(8,128)(2,1)S(1)}, bf16[1,16,4096]{2,1,0:T(8,128)(2,1)S(1)}, u32[]{:S(2)}, u32[]{:S(2)}) collective-permute-start(bf16[1,16,4096]{2,1,0:T(8,128)(2,1)S(1)} %get-tuple-element.178), channel_id=1, source_target_pairs={{0,1},{1,0},{2,3},{3,2},{4,5},{5,4},{6,7},{7,6},{8,9},{9,8},{10,11... | collective-permute-start | bytes 393224 | tf_op jit(solution)/shard_map/ppermute | solution.py:695
  147.2 3.0 %collective-permute-start.22 = (bf16[1,16,4096]{2,1,0:T(8,128)(2,1)S(1)}, bf16[1,16,4096]{2,1,0:T(8,128)(2,1)S(1)}, u32[]{:S(2)}, u32[]{:S(2)}) collective-permute-start(bf16[1,16,4096]{2,1,0:T(8,128)(2,1)S(1)} %get-tuple-element.179), channel_id=1, source_target_pairs={{0,2},{1,3},{2,0},{3,1},{4,6},{5,7},{6,4},{7,5},{8,10},{9,11},{10,... | collective-permute-start | bytes 393224 | tf_op jit(solution)/shard_map/ppermute | solution.py:695
  151.3 7.9 %collective-permute-done.22.refs_7_ = bf16[1,16,4096]{2,1,0:T(8,128)(2,1)S(1)} collective-permute-done((bf16[1,16,4096]{2,1,0:T(8,128)(2,1)S(1)}, bf16[1,16,4096]{2,1,0:T(8,128)(2,1)S(1)}, u32[]{:S(2)}, u32[]{:S(2)}) %collective-permute-start.22) | collective-permute-done | bytes 131104 | tf_op jit(solution)/shard_map/ppermute | solution.py:695
  161.4 2.4 collective-permute-start.28
  165.8 3.6 %collective-permute-done.28.refs_7_ = bf16[1,16,4096]{2,1,0:T(8,128)(2,1)S(1)} collective-permute-done((bf16[1,16,4096]{2,1,0:T(8,128)(2,1)S(1)}, bf16[1,16,4096]{2,1,0:T(8,128)(2,1)S(1)}, u32[]{:S(2)}, u32[]{:S(2)}) %collective-permute-start.28) | collective-permute-done | bytes 131104 | tf_op jit(solution)/shard_map/ppermute | solution.py:695
  169.4 4.0 %collective-permute-done.27.refs_6_ = bf16[1,16,4096]{2,1,0:T(8,128)(2,1)S(1)} collective-permute-done((bf16[1,16,4096]{2,1,0:T(8,128)(2,1)S(1)}, bf16[1,16,4096]{2,1,0:T(8,128)(2,1)S(1)}, u32[]{:S(2)}, u32[]{:S(2)}) %collective-permute-start.27) | collective-permute-done | bytes 131104 | tf_op jit(solution)/shard_map/ppermute | solution.py:695
  173.5 1.6 collective-permute-start.32
  176.2 3.4 %collective-permute-start.30 = (bf16[1,16,4224]{2,1,0:T(8,128)(2,1)S(1)}, bf16[1,16,4224]{2,1,0:T(8,128)(2,1)S(1)}, u32[]{:S(2)}, u32[]{:S(2)}) collective-permute-start(bf16[1,16,4224]{2,1,0:T(8,128)(2,1)S(1)} %get-tuple-element.188), channel_id=1, source_target_pairs={{0,2},{1,3},{2,0},{3,1},{4,6},{5,7},{6,4},{7,5},{8,10},{9,11},{10,... | collective-permute-start | bytes 405512 | tf_op jit(solution)/shard_map/ppermute | solution.py:695
  180.1 2.2 collective-permute-done.29.refs_2_
  182.3 7.0 %collective-permute-done.30.refs_3_ = bf16[1,16,4224]{2,1,0:T(8,128)(2,1)S(1)} collective-permute-done((bf16[1,16,4224]{2,1,0:T(8,128)(2,1)S(1)}, bf16[1,16,4224]{2,1,0:T(8,128)(2,1)S(1)}, u32[]{:S(2)}, u32[]{:S(2)}) %collective-permute-start.30) | collective-permute-done | bytes 135200 | tf_op jit(solution)/shard_map/ppermute | solution.py:695
  189.8 1.5 collective-permute-start.38
  191.3 2.4 collective-permute-start.36
  193.7 2.0 collective-permute-start.35
  196.3 3.3 %collective-permute-done.36.refs_3_ = bf16[1,16,4224]{2,1,0:T(8,128)(2,1)S(1)} collective-permute-done((bf16[1,16,4224]{2,1,0:T(8,128)(2,1)S(1)}, bf16[1,16,4224]{2,1,0:T(8,128)(2,1)S(1)}, u32[]{:S(2)}, u32[]{:S(2)}) %collective-permute-start.36) | collective-permute-done | bytes 135200 | tf_op jit(solution)/shard_map/ppermute | solution.py:695
  199.6 3.7 %collective-permute-done.35.refs_2_ = bf16[1,16,4224]{2,1,0:T(8,128)(2,1)S(1)} collective-permute-done((bf16[1,16,4224]{2,1,0:T(8,128)(2,1)S(1)}, bf16[1,16,4224]{2,1,0:T(8,128)(2,1)S(1)}, u32[]{:S(2)}, u32[]{:S(2)}) %collective-permute-start.35) | collective-permute-done | bytes 135200 | tf_op jit(solution)/shard_map/ppermute | solution.py:695
  207.4 1.7 collective-permute-start.39
  209.1 5.2 %collective-permute-done.42.refs_9_ = bf16[256,512]{1,0:T(8,128)(2,1)S(1)} collective-permute-done((bf16[256,512]{1,0:T(8,128)(2,1)S(1)}, bf16[256,512]{1,0:T(8,128)(2,1)S(1)}, u32[]{:S(2)}, u32[]{:S(2)}) %collective-permute-start.42) | collective-permute-done | bytes 262176 | tf_op jit(solution)/shard_map/ppermute | solution.py:658
  214.4 2.8 %collective-permute-done.43.refs_12_ = bf16[256,512]{1,0:T(8,128)(2,1)S(1)} collective-permute-done((bf16[256,512]{1,0:T(8,128)(2,1)S(1)}, bf16[256,512]{1,0:T(8,128)(2,1)S(1)}, u32[]{:S(2)}, u32[]{:S(2)}) %collective-permute-start.43) | collective-permute-done | bytes 262176 | tf_op jit(solution)/shard_map/ppermute | solution.py:658
  221.0 1.6 collective-permute-start.46
  222.6 4.5 %shard_map.279 = (f32[512,2048]{1,0:T(8,128)}, f32[2048,512]{1,0:T(8,128)}) custom-call(s32[2]{0:T(128)S(1)} %pad_add_fusion.1.codes, bf16[16,16,4096]{2,1,0:T(8,128)(2,1)S(1)} %get-tuple-element.208.refs_0_, bf16[16,16,4096]{2,1,0:T(8,128)(2,1)S(1)} %collective-permute-done.47.refs_1_), custom_call_target="tpu_custom_call" | custom-call | flops 6000000000 | tf_op jit(solution)/shard_map/pallas_call | solution.py:613
  227.7 6.5 %collective-permute-done.44.refs_5_.part_got = bf16[256,512]{1,0:T(8,128)(2,1)S(1)} collective-permute-done((bf16[256,512]{1,0:T(8,128)(2,1)S(1)}, bf16[256,512]{1,0:T(8,128)(2,1)S(1)}, u32[]{:S(2)}, u32[]{:S(2)}) %collective-permute-start.44) | collective-permute-done | bytes 262176 | tf_op jit(solution)/shard_map/ppermute | solution.py:653
  236.0 2.7 %shard_map.281 = (f32[2,256,512]{2,1,0:T(8,128)}, f32[2,256,512]{2,1,0:T(8,128)}) custom-call(s32[2]{0:T(128)S(1)} %pad_add_fusion.order, s32[1]{0:T(128)} %bitcast.2.rank, bf16[2,256,512]{2,1,0:T(8,128)(2,1)S(1)} %copy-done.4, f32[512,512]{1,0:T(8,128)S(1)} %get-tuple-element.139.refs_4_.self_grad, ...), custom_call_target="tpu_custom_call" | custom-call | flops 3000000000 | tf_op jit(solution)/shard_map/pallas_call | solution.py:613
  238.7 1.5 collective-permute-done.49.refs_1_
  240.2 3.9 %shard_map.282 = (f32[512,1024]{1,0:T(8,128)}, f32[512,512]{1,0:T(8,128)}, f32[512,512]{1,0:T(8,128)}, f32[512,1536]{1,0:T(8,128)}, f32[512,512]{1,0:T(8,128)}, ...) custom-call(s32[2]{0:T(128)S(1)} %pad_add_fusion.1.codes, ...), custom_call_target="tpu_custom_call" | custom-call | flops 5000000000 | tf_op jit(solution)/shard_map/pallas_call | solution.py:613
  (118 shorter events, 29.0 us)
Async XLA Ops:
  2.9 18.9 %collective-permute-start = (bf16[512,512]{1,0:T(8,128)(2,1)}, bf16[512,512]{1,0:T(8,128)(2,1)S(1)}, u32[]{:S(2)}, u32[]{:S(2)}) collective-permute-start(bf16[512,512]{1,0:T(8,128)(2,1)} %get-tuple-element.121), channel_id=1, source_target_pairs={{0,2},{4,6},{8,10},{12,14},{16,18},{20,22},{24,26},{28,30}} | collective-permute-start | bytes 1572872 | tf_op jit(solution)/shard_map/ppermute | solution.py:674
  9.2 18.6 %collective-permute-start.6 = (bf16[256,512]{1,0:T(8,128)(2,1)}, bf16[256,512]{1,0:T(8,128)(2,1)S(1)}, u32[]{:S(2)}, u32[]{:S(2)}) collective-permute-start(bf16[256,512]{1,0:T(8,128)(2,1)} %get-tuple-element.123), channel_id=1, source_target_pairs={{0,3},{4,7},{8,11},{12,15},{16,19},{20,23},{24,27},{28,31}} | collective-permute-start | bytes 786440 | tf_op jit(solution)/shard_map/ppermute | solution.py:643
  10.8 22.3 %collective-permute-start.5 = (bf16[256,512]{1,0:T(8,128)(2,1)}, bf16[256,512]{1,0:T(8,128)(2,1)}, u32[]{:S(2)}, u32[]{:S(2)}) collective-permute-start(bf16[256,512]{1,0:T(8,128)(2,1)} %get-tuple-element.123), channel_id=1, source_target_pairs={{0,2},{1,3},{4,6},{5,7},{8,10},{9,11},{12,14},{13,15},{16,18},{17,... | collective-permute-start | bytes 786440 | tf_op jit(solution)/shard_map/ppermute | solution.py:643
  12.8 26.3 %collective-permute-start.4 = (bf16[256,512]{1,0:T(8,128)(2,1)}, bf16[256,512]{1,0:T(8,128)(2,1)}, u32[]{:S(2)}, u32[]{:S(2)}) collective-permute-start(bf16[256,512]{1,0:T(8,128)(2,1)} %get-tuple-element.123), channel_id=1, source_target_pairs={{0,1},{1,2},{2,3},{4,5},{5,6},{6,7},{8,9},{9,10},{10,11},{12,13},{... | collective-permute-start | bytes 786440 | tf_op jit(solution)/shard_map/ppermute | solution.py:643
  23.7 23.8 %collective-permute-start.8 = (bf16[256,512]{1,0:T(8,128)(2,1)}, bf16[256,512]{1,0:T(8,128)(2,1)}, u32[]{:S(2)}, u32[]{:S(2)}) collective-permute-start(bf16[256,512]{1,0:T(8,128)(2,1)} %get-tuple-element.226), channel_id=1, source_target_pairs={{0,1},{2,3},{4,5},{6,7},{8,9},{10,11},{12,13},{14,15},{16,17},{18,... | collective-permute-start | bytes 786440 | tf_op jit(solution)/shard_map/ppermute | solution.py:685
  27.8 33.9 %collective-permute-start.3 = (bf16[256,512]{1,0:T(8,128)(2,1)}, bf16[256,512]{1,0:T(8,128)(2,1)S(1)}, u32[]{:S(2)}, u32[]{:S(2)}) collective-permute-start(bf16[256,512]{1,0:T(8,128)(2,1)} %get-tuple-element.122), channel_id=1, source_target_pairs={{0,3},{1,0},{2,1},{3,2},{4,7},{5,4},{6,5},{7,6},{8,11},{9,8},{10,9... | collective-permute-start | bytes 786440 | tf_op jit(solution)/shard_map/ppermute | solution.py:643
  27.8 33.9 %collective-permute-start.2 = (bf16[256,512]{1,0:T(8,128)(2,1)}, bf16[256,512]{1,0:T(8,128)(2,1)S(1)}, u32[]{:S(2)}, u32[]{:S(2)}) collective-permute-start(bf16[256,512]{1,0:T(8,128)(2,1)} %get-tuple-element.122), channel_id=1, source_target_pairs={{0,2},{1,3},{2,0},{3,1},{4,6},{5,7},{6,4},{7,5},{8,10},{9,11},{10,... | collective-permute-start | bytes 786440 | tf_op jit(solution)/shard_map/ppermute | solution.py:643
  33.1 28.7 %collective-permute-start.1 = (bf16[256,512]{1,0:T(8,128)(2,1)}, bf16[256,512]{1,0:T(8,128)(2,1)S(1)}, u32[]{:S(2)}, u32[]{:S(2)}) collective-permute-start(bf16[256,512]{1,0:T(8,128)(2,1)} %get-tuple-element.122), channel_id=1, source_target_pairs={{0,1},{1,2},{2,3},{3,0},{4,5},{5,6},{6,7},{7,4},{8,9},{9,10},{10,1... | collective-permute-start | bytes 786440 | tf_op jit(solution)/shard_map/ppermute | solution.py:643
  39.1 26.4 %collective-permute-start.7 = (bf16[256,512]{1,0:T(8,128)(2,1)S(1)}, bf16[256,512]{1,0:T(8,128)(2,1)S(1)}, u32[]{:S(2)}, u32[]{:S(2)}) collective-permute-start(bf16[256,512]{1,0:T(8,128)(2,1)S(1)} %add.69), channel_id=1, source_target_pairs={{0,1},{2,3},{4,5},{6,7},{8,9},{10,11},{12,13},{14,15},{16,17},{18,... | collective-permute-start | bytes 786440 | tf_op jit(solution)/shard_map/ppermute | solution.py:685
  90.2 20.5 %collective-permute-start.9 = (bf16[16,16,4096]{2,1,0:T(8,128)(2,1)S(1)}, bf16[16,16,4096]{2,1,0:T(8,128)(2,1)S(1)}, u32[]{:S(2)}, u32[]{:S(2)}) collective-permute-start(bf16[16,16,4096]{2,1,0:T(8,128)(2,1)S(1)} %get-tuple-element.150), channel_id=1, source_target_pairs={{0,4},{4,0},{8,12},{12,8},{16,20},{20,16},{24,28},{28,24},{1,5},{5... | collective-permute-start | bytes 6291464 | tf_op jit(solution)/shard_map/ppermute | solution.py:695
  100.1 28.1 %collective-permute-start.15 = (bf16[256,512]{1,0:T(8,128)(2,1)S(1)}, bf16[256,512]{1,0:T(8,128)(2,1)S(1)}, u32[]{:S(2)}, u32[]{:S(2)}) collective-permute-start(bf16[256,512]{1,0:T(8,128)(2,1)S(1)} %get-tuple-element.166), channel_id=1, source_target_pairs={{0,2},{1,3},{2,0},{3,1},{4,6},{5,7},{6,4},{7,5},{8,10},{9,11},{10,... | collective-permute-start | bytes 786440 | tf_op jit(solution)/shard_map/ppermute | solution.py:649
  103.6 24.7 %collective-permute-start.16 = (bf16[256,512]{1,0:T(8,128)(2,1)S(1)}, bf16[256,512]{1,0:T(8,128)(2,1)S(1)}, u32[]{:S(2)}, u32[]{:S(2)}) collective-permute-start(bf16[256,512]{1,0:T(8,128)(2,1)S(1)} %get-tuple-element.167), channel_id=1, source_target_pairs={{0,1},{1,2},{2,3},{3,0},{4,5},{5,6},{6,7},{7,4},{8,9},{9,10},{10,1... | collective-permute-start | bytes 786440 | tf_op jit(solution)/shard_map/ppermute | solution.py:649
  103.6 24.7 %collective-permute-start.14 = (bf16[512,512]{1,0:T(8,128)(2,1)S(1)}, bf16[512,512]{1,0:T(8,128)(2,1)S(1)}, u32[]{:S(2)}, u32[]{:S(2)}) collective-permute-start(bf16[512,512]{1,0:T(8,128)(2,1)S(1)} %get-tuple-element.165.refs_1_), channel_id=1, source_target_pairs={{0,3},{1,0},{2,1},{3,2},{4,7},{5,4},{6,5},{7,6},{8,11},{9,8},{10,9... | collective-permute-start | bytes 1572872 | tf_op jit(solution)/shard_map/ppermute | solution.py:649
  111.0 17.1 %collective-permute-start.10 = (bf16[8,16,2048]{2,1,0:T(8,128)(2,1)S(1)}, bf16[8,16,2048]{2,1,0:T(8,128)(2,1)S(1)}, u32[]{:S(2)}, u32[]{:S(2)}) collective-permute-start(bf16[8,16,2048]{2,1,0:T(8,128)(2,1)S(1)} %get-tuple-element.154), channel_id=1, source_target_pairs={{0,8},{4,12},{8,0},{12,4},{16,24},{20,28},{24,16},{28,20},{1,9},{5... | collective-permute-start | bytes 1572872 | tf_op jit(solution)/shard_map/ppermute | solution.py:695
  112.5 15.6 %collective-permute-start.11 = (bf16[8,16,2048]{2,1,0:T(8,128)(2,1)S(1)}, bf16[8,16,2048]{2,1,0:T(8,128)(2,1)S(1)}, u32[]{:S(2)}, u32[]{:S(2)}) collective-permute-start(bf16[8,16,2048]{2,1,0:T(8,128)(2,1)S(1)} %get-tuple-element.156), channel_id=1, source_target_pairs={{0,16},{4,20},{8,24},{12,28},{16,0},{20,4},{24,8},{28,12},{1,17},{... | collective-permute-start | bytes 1572872 | tf_op jit(solution)/shard_map/ppermute | solution.py:695
  128.4 10.3 %collective-permute-start.17 = (bf16[16,16,4224]{2,1,0:T(8,128)(2,1)S(1)}, bf16[16,16,4224]{2,1,0:T(8,128)(2,1)S(1)}, u32[]{:S(2)}, u32[]{:S(2)}) collective-permute-start(bf16[16,16,4224]{2,1,0:T(8,128)(2,1)S(1)} %get-tuple-element.169), channel_id=1, source_target_pairs={{0,4},{4,0},{8,12},{12,8},{16,20},{20,16},{24,28},{28,24},{1,5},{5... | collective-permute-start | bytes 6488072 | tf_op jit(solution)/shard_map/ppermute | solution.py:695
  129.4 8.8 %collective-permute-start.13 = (bf16[4,16,2048]{2,1,0:T(8,128)(2,1)S(1)}, bf16[4,16,2048]{2,1,0:T(8,128)(2,1)S(1)}, u32[]{:S(2)}, u32[]{:S(2)}) collective-permute-start(bf16[4,16,2048]{2,1,0:T(8,128)(2,1)S(1)} %get-tuple-element.160), channel_id=1, source_target_pairs={{0,8},{4,12},{8,0},{12,4},{16,24},{20,28},{24,16},{28,20},{1,9},{5... | collective-permute-start | bytes 786440 | tf_op jit(solution)/shard_map/ppermute | solution.py:695
  130.3 8.4 %collective-permute-start.12 = (bf16[4,16,2048]{2,1,0:T(8,128)(2,1)S(1)}, bf16[4,16,2048]{2,1,0:T(8,128)(2,1)S(1)}, u32[]{:S(2)}, u32[]{:S(2)}) collective-permute-start(bf16[4,16,2048]{2,1,0:T(8,128)(2,1)S(1)} %get-tuple-element.158), channel_id=1, source_target_pairs={{0,16},{4,20},{8,24},{12,28},{16,0},{20,4},{24,8},{28,12},{1,17},{... | collective-permute-start | bytes 786440 | tf_op jit(solution)/shard_map/ppermute | solution.py:695
  139.0 20.2 %collective-permute-start.20 = (bf16[8,16,2176]{2,1,0:T(8,128)(2,1)S(1)}, bf16[8,16,2176]{2,1,0:T(8,128)(2,1)S(1)}, u32[]{:S(2)}, u32[]{:S(2)}) collective-permute-start(bf16[8,16,2176]{2,1,0:T(8,128)(2,1)S(1)} %get-tuple-element.176), channel_id=1, source_target_pairs={{0,16},{4,20},{8,24},{12,28},{16,0},{20,4},{24,8},{28,12},{1,17},{... | collective-permute-start | bytes 1671176 | tf_op jit(solution)/shard_map/ppermute | solution.py:695
  140.6 18.6 %collective-permute-start.19 = (bf16[8,16,2048]{2,1,0:T(8,128)(2,1)S(1)}, bf16[8,16,2048]{2,1,0:T(8,128)(2,1)S(1)}, u32[]{:S(2)}, u32[]{:S(2)}) collective-permute-start(bf16[8,16,2048]{2,1,0:T(8,128)(2,1)S(1)} %get-tuple-element.174), channel_id=1, source_target_pairs={{0,8},{4,12},{8,0},{12,4},{16,24},{20,28},{24,16},{28,20},{1,9},{5... | collective-permute-start | bytes 1572872 | tf_op jit(solution)/shard_map/ppermute | solution.py:695
  141.1 10.2 %collective-permute-start.21 = (bf16[1,16,4096]{2,1,0:T(8,128)(2,1)S(1)}, bf16[1,16,4096]{2,1,0:T(8,128)(2,1)S(1)}, u32[]{:S(2)}, u32[]{:S(2)}) collective-permute-start(bf16[1,16,4096]{2,1,0:T(8,128)(2,1)S(1)} %get-tuple-element.178), channel_id=1, source_target_pairs={{0,1},{1,0},{2,3},{3,2},{4,5},{5,4},{6,7},{7,6},{8,9},{9,8},{10,11... | collective-permute-start | bytes 393224 | tf_op jit(solution)/shard_map/ppermute | solution.py:695
  147.2 12.0 %collective-permute-start.22 = (bf16[1,16,4096]{2,1,0:T(8,128)(2,1)S(1)}, bf16[1,16,4096]{2,1,0:T(8,128)(2,1)S(1)}, u32[]{:S(2)}, u32[]{:S(2)}) collective-permute-start(bf16[1,16,4096]{2,1,0:T(8,128)(2,1)S(1)} %get-tuple-element.179), channel_id=1, source_target_pairs={{0,2},{1,3},{2,0},{3,1},{4,6},{5,7},{6,4},{7,5},{8,10},{9,11},{10,... | collective-permute-start | bytes 393224 | tf_op jit(solution)/shard_map/ppermute | solution.py:695
  150.2 9.0 %collective-permute-start.23 = (bf16[1,16,4096]{2,1,0:T(8,128)(2,1)S(1)}, bf16[1,16,4096]{2,1,0:T(8,128)(2,1)S(1)}, u32[]{:S(2)}, u32[]{:S(2)}) collective-permute-start(bf16[1,16,4096]{2,1,0:T(8,128)(2,1)S(1)} %get-tuple-element.180), channel_id=1, source_target_pairs={{0,3},{1,2},{2,1},{3,0},{4,7},{5,6},{6,5},{7,4},{8,11},{9,10},{10,... | collective-permute-start | bytes 393224 | tf_op jit(solution)/shard_map/ppermute | solution.py:695
  159.4 14.0 %collective-permute-start.25 = (bf16[4,16,2176]{2,1,0:T(8,128)(2,1)S(1)}, bf16[4,16,2176]{2,1,0:T(8,128)(2,1)S(1)}, u32[]{:S(2)}, u32[]{:S(2)}) collective-permute-start(bf16[4,16,2176]{2,1,0:T(8,128)(2,1)S(1)} %get-tuple-element.184), channel_id=1, source_target_pairs={{0,8},{4,12},{8,0},{12,4},{16,24},{20,28},{24,16},{28,20},{1,9},{5... | collective-permute-start | bytes 835592 | tf_op jit(solution)/shard_map/ppermute | solution.py:695
  160.9 12.5 %collective-permute-start.24 = (bf16[4,16,2048]{2,1,0:T(8,128)(2,1)S(1)}, bf16[4,16,2048]{2,1,0:T(8,128)(2,1)S(1)}, u32[]{:S(2)}, u32[]{:S(2)}) collective-permute-start(bf16[4,16,2048]{2,1,0:T(8,128)(2,1)S(1)} %get-tuple-element.182), channel_id=1, source_target_pairs={{0,16},{4,20},{8,24},{12,28},{16,0},{20,4},{24,8},{28,12},{1,17},{... | collective-permute-start | bytes 786440 | tf_op jit(solution)/shard_map/ppermute | solution.py:695
  161.4 8.0 %collective-permute-start.28 = (bf16[1,16,4096]{2,1,0:T(8,128)(2,1)S(1)}, bf16[1,16,4096]{2,1,0:T(8,128)(2,1)S(1)}, u32[]{:S(2)}, u32[]{:S(2)}) collective-permute-start(bf16[1,16,4096]{2,1,0:T(8,128)(2,1)S(1)} %get-tuple-element.185.refs_4_), channel_id=1, source_target_pairs={{0,3},{1,2},{2,1},{3,0},{4,7},{5,6},{6,5},{7,4},{8,11},{9,10},{10,... | collective-permute-start | bytes 393224 | tf_op jit(solution)/shard_map/ppermute | solution.py:695
  163.8 9.6 %collective-permute-start.27 = (bf16[1,16,4096]{2,1,0:T(8,128)(2,1)S(1)}, bf16[1,16,4096]{2,1,0:T(8,128)(2,1)S(1)}, u32[]{:S(2)}, u32[]{:S(2)}) collective-permute-start(bf16[1,16,4096]{2,1,0:T(8,128)(2,1)S(1)} %get-tuple-element.185.refs_4_), channel_id=1, source_target_pairs={{0,2},{1,3},{2,0},{3,1},{4,6},{5,7},{6,4},{7,5},{8,10},{9,11},{10,... | collective-permute-start | bytes 393224 | tf_op jit(solution)/shard_map/ppermute | solution.py:695
  164.9 8.6 %collective-permute-start.26 = (bf16[1,16,4096]{2,1,0:T(8,128)(2,1)S(1)}, bf16[1,16,4096]{2,1,0:T(8,128)(2,1)S(1)}, u32[]{:S(2)}, u32[]{:S(2)}) collective-permute-start(bf16[1,16,4096]{2,1,0:T(8,128)(2,1)S(1)} %get-tuple-element.185.refs_4_), channel_id=1, source_target_pairs={{0,1},{1,0},{2,3},{3,2},{4,5},{5,4},{6,7},{7,6},{8,9},{9,8},{10,11... | collective-permute-start | bytes 393224 | tf_op jit(solution)/shard_map/ppermute | solution.py:695
  173.5 15.8 %collective-permute-start.32 = (bf16[4,16,2048]{2,1,0:T(8,128)(2,1)S(1)}, bf16[4,16,2048]{2,1,0:T(8,128)(2,1)S(1)}, u32[]{:S(2)}, u32[]{:S(2)}) collective-permute-start(bf16[4,16,2048]{2,1,0:T(8,128)(2,1)S(1)} %get-tuple-element.190.refs_5_), channel_id=1, source_target_pairs={{0,16},{4,20},{8,24},{12,28},{16,0},{20,4},{24,8},{28,12},{1,17},{... | collective-permute-start | bytes 786440 | tf_op jit(solution)/shard_map/ppermute | solution.py:695
  175.1 14.2 %collective-permute-start.33 = (bf16[4,16,2048]{2,1,0:T(8,128)(2,1)S(1)}, bf16[4,16,2048]{2,1,0:T(8,128)(2,1)S(1)}, u32[]{:S(2)}, u32[]{:S(2)}) collective-permute-start(bf16[4,16,2048]{2,1,0:T(8,128)(2,1)S(1)} %get-tuple-element.191.refs_7_), channel_id=1, source_target_pairs={{0,8},{4,12},{8,0},{12,4},{16,24},{20,28},{24,16},{28,20},{1,9},{5... | collective-permute-start | bytes 786440 | tf_op jit(solution)/shard_map/ppermute | solution.py:695
  175.7 6.6 %collective-permute-start.29 = (bf16[1,16,4224]{2,1,0:T(8,128)(2,1)S(1)}, bf16[1,16,4224]{2,1,0:T(8,128)(2,1)S(1)}, u32[]{:S(2)}, u32[]{:S(2)}) collective-permute-start(bf16[1,16,4224]{2,1,0:T(8,128)(2,1)S(1)} %get-tuple-element.187), channel_id=1, source_target_pairs={{0,1},{1,0},{2,3},{3,2},{4,5},{5,4},{6,7},{7,6},{8,9},{9,8},{10,11... | collective-permute-start | bytes 405512 | tf_op jit(solution)/shard_map/ppermute | solution.py:695
  176.2 13.1 %collective-permute-start.30 = (bf16[1,16,4224]{2,1,0:T(8,128)(2,1)S(1)}, bf16[1,16,4224]{2,1,0:T(8,128)(2,1)S(1)}, u32[]{:S(2)}, u32[]{:S(2)}) collective-permute-start(bf16[1,16,4224]{2,1,0:T(8,128)(2,1)S(1)} %get-tuple-element.188), channel_id=1, source_target_pairs={{0,2},{1,3},{2,0},{3,1},{4,6},{5,7},{6,4},{7,5},{8,10},{9,11},{10,... | collective-permute-start | bytes 405512 | tf_op jit(solution)/shard_map/ppermute | solution.py:695
  179.6 9.7 %collective-permute-start.31 = (bf16[1,16,4224]{2,1,0:T(8,128)(2,1)S(1)}, bf16[1,16,4224]{2,1,0:T(8,128)(2,1)S(1)}, u32[]{:S(2)}, u32[]{:S(2)}) collective-permute-start(bf16[1,16,4224]{2,1,0:T(8,128)(2,1)S(1)} %get-tuple-element.189), channel_id=1, source_target_pairs={{0,3},{1,2},{2,1},{3,0},{4,7},{5,6},{6,5},{7,4},{8,11},{9,10},{10,... | collective-permute-start | bytes 405512 | tf_op jit(solution)/shard_map/ppermute | solution.py:695
  189.5 13.8 %collective-permute-start.37 = (bf16[8,16,2048]{2,1,0:T(8,128)(2,1)S(1)}, bf16[8,16,2048]{2,1,0:T(8,128)(2,1)S(1)}, u32[]{:S(2)}, u32[]{:S(2)}) collective-permute-start(bf16[8,16,2048]{2,1,0:T(8,128)(2,1)S(1)} %get-tuple-element.193.refs_4_), channel_id=1, source_target_pairs={{0,8},{4,12},{8,0},{12,4},{16,24},{20,28},{24,16},{28,20},{1,9},{5... | collective-permute-start | bytes 1572872 | tf_op jit(solution)/shard_map/ppermute | solution.py:695
  189.8 13.5 %collective-permute-start.38 = (bf16[8,16,2048]{2,1,0:T(8,128)(2,1)S(1)}, bf16[8,16,2048]{2,1,0:T(8,128)(2,1)S(1)}, u32[]{:S(2)}, u32[]{:S(2)}) collective-permute-start(bf16[8,16,2048]{2,1,0:T(8,128)(2,1)S(1)} %get-tuple-element.194.refs_6_), channel_id=1, source_target_pairs={{0,16},{4,20},{8,24},{12,28},{16,0},{20,4},{24,8},{28,12},{1,17},{... | collective-permute-start | bytes 1572872 | tf_op jit(solution)/shard_map/ppermute | solution.py:695
  191.3 8.3 %collective-permute-start.36 = (bf16[1,16,4224]{2,1,0:T(8,128)(2,1)S(1)}, bf16[1,16,4224]{2,1,0:T(8,128)(2,1)S(1)}, u32[]{:S(2)}, u32[]{:S(2)}) collective-permute-start(bf16[1,16,4224]{2,1,0:T(8,128)(2,1)S(1)} %get-tuple-element.192.refs_0_), channel_id=1, source_target_pairs={{0,3},{1,2},{2,1},{3,0},{4,7},{5,6},{6,5},{7,4},{8,11},{9,10},{10,... | collective-permute-start | bytes 405512 | tf_op jit(solution)/shard_map/ppermute | solution.py:695
  193.7 9.5 %collective-permute-start.35 = (bf16[1,16,4224]{2,1,0:T(8,128)(2,1)S(1)}, bf16[1,16,4224]{2,1,0:T(8,128)(2,1)S(1)}, u32[]{:S(2)}, u32[]{:S(2)}) collective-permute-start(bf16[1,16,4224]{2,1,0:T(8,128)(2,1)S(1)} %get-tuple-element.192.refs_0_), channel_id=1, source_target_pairs={{0,2},{1,3},{2,0},{3,1},{4,6},{5,7},{6,4},{7,5},{8,10},{9,11},{10,... | collective-permute-start | bytes 405512 | tf_op jit(solution)/shard_map/ppermute | solution.py:695
  195.7 7.6 %collective-permute-start.34 = (bf16[1,16,4224]{2,1,0:T(8,128)(2,1)S(1)}, bf16[1,16,4224]{2,1,0:T(8,128)(2,1)S(1)}, u32[]{:S(2)}, u32[]{:S(2)}) collective-permute-start(bf16[1,16,4224]{2,1,0:T(8,128)(2,1)S(1)} %get-tuple-element.192.refs_0_), channel_id=1, source_target_pairs={{0,1},{1,0},{2,3},{3,2},{4,5},{5,4},{6,7},{7,6},{8,9},{9,8},{10,11... | collective-permute-start | bytes 405512 | tf_op jit(solution)/shard_map/ppermute | solution.py:695
  203.5 13.7 %collective-permute-start.40 = (bf16[4,16,2176]{2,1,0:T(8,128)(2,1)S(1)}, bf16[4,16,2176]{2,1,0:T(8,128)(2,1)S(1)}, u32[]{:S(2)}, u32[]{:S(2)}) collective-permute-start(bf16[4,16,2176]{2,1,0:T(8,128)(2,1)S(1)} %get-tuple-element.196.refs_2_), channel_id=1, source_target_pairs={{0,8},{4,12},{8,0},{12,4},{16,24},{20,28},{24,16},{28,20},{1,9},{5... | collective-permute-start | bytes 835592 | tf_op jit(solution)/shard_map/ppermute | solution.py:695
  204.1 5.0 %collective-permute-start.41 = (bf16[256,512]{1,0:T(8,128)(2,1)S(1)}, bf16[256,512]{1,0:T(8,128)(2,1)S(1)}, u32[]{:S(2)}, u32[]{:S(2)}) collective-permute-start(bf16[256,512]{1,0:T(8,128)(2,1)S(1)} %get-tuple-element.200), channel_id=1, source_target_pairs={{2,1},{3,2},{6,5},{7,6},{10,9},{11,10},{14,13},{15,14},{18,17},{19... | collective-permute-start | bytes 786440 | tf_op jit(solution)/shard_map/ppermute | solution.py:653
  204.8 9.6 %collective-permute-start.42 = (bf16[256,512]{1,0:T(8,128)(2,1)S(1)}, bf16[256,512]{1,0:T(8,128)(2,1)S(1)}, u32[]{:S(2)}, u32[]{:S(2)}) collective-permute-start(bf16[256,512]{1,0:T(8,128)(2,1)S(1)} %get-tuple-element.201.refs_8_), channel_id=1, source_target_pairs={{1,0},{3,2},{5,4},{7,6},{9,8},{11,10},{13,12},{15,14},{17,16},{19,... | collective-permute-start | bytes 786440 | tf_op jit(solution)/shard_map/ppermute | solution.py:658
  206.1 11.1 %collective-permute-start.43 = (bf16[256,512]{1,0:T(8,128)(2,1)S(1)}, bf16[256,512]{1,0:T(8,128)(2,1)S(1)}, u32[]{:S(2)}, u32[]{:S(2)}) collective-permute-start(bf16[256,512]{1,0:T(8,128)(2,1)S(1)} %get-tuple-element.202.refs_11_), channel_id=1, source_target_pairs={{2,0},{6,4},{10,8},{14,12},{18,16},{22,20},{26,24},{30,28}} | collective-permute-start | bytes 786440 | tf_op jit(solution)/shard_map/ppermute | solution.py:658
  207.4 9.8 %collective-permute-start.39 = (bf16[4,16,2048]{2,1,0:T(8,128)(2,1)S(1)}, bf16[4,16,2048]{2,1,0:T(8,128)(2,1)S(1)}, u32[]{:S(2)}, u32[]{:S(2)}) collective-permute-start(bf16[4,16,2048]{2,1,0:T(8,128)(2,1)S(1)} %get-tuple-element.195.refs_0_), channel_id=1, source_target_pairs={{0,16},{4,20},{8,24},{12,28},{16,0},{20,4},{24,8},{28,12},{1,17},{... | collective-permute-start | bytes 786440 | tf_op jit(solution)/shard_map/ppermute | solution.py:695
  217.4 5.1 %collective-permute-start.47 = (bf16[16,16,4096]{2,1,0:T(8,128)(2,1)S(1)}, bf16[16,16,4096]{2,1,0:T(8,128)(2,1)S(1)}, u32[]{:S(2)}, u32[]{:S(2)}) collective-permute-start(bf16[16,16,4096]{2,1,0:T(8,128)(2,1)S(1)} %get-tuple-element.208.refs_0_), channel_id=1, source_target_pairs={{0,4},{4,0},{8,12},{12,8},{16,20},{20,16},{24,28},{28,24},{1,5},{5... | collective-permute-start | bytes 6291464 | tf_op jit(solution)/shard_map/ppermute | solution.py:695
  217.5 16.7 %collective-permute-start.45 = (bf16[8,16,2048]{2,1,0:T(8,128)(2,1)S(1)}, bf16[8,16,2048]{2,1,0:T(8,128)(2,1)S(1)}, u32[]{:S(2)}, u32[]{:S(2)}) collective-permute-start(bf16[8,16,2048]{2,1,0:T(8,128)(2,1)S(1)} %get-tuple-element.205.refs_0_), channel_id=1, source_target_pairs={{0,8},{4,12},{8,0},{12,4},{16,24},{20,28},{24,16},{28,20},{1,9},{5... | collective-permute-start | bytes 1572872 | tf_op jit(solution)/shard_map/ppermute | solution.py:695
  218.4 15.9 %collective-permute-start.44 = (bf16[256,512]{1,0:T(8,128)(2,1)S(1)}, bf16[256,512]{1,0:T(8,128)(2,1)S(1)}, u32[]{:S(2)}, u32[]{:S(2)}) collective-permute-start(bf16[256,512]{1,0:T(8,128)(2,1)S(1)} %get-tuple-element.203), channel_id=1, source_target_pairs={{1,0},{2,1},{3,2},{5,4},{6,5},{7,6},{9,8},{10,9},{11,10},{13,12},{... | collective-permute-start | bytes 786440 | tf_op jit(solution)/shard_map/ppermute | solution.py:653
  219.7 14.6 %collective-permute-start.48 = (bf16[256,512]{1,0:T(8,128)(2,1)S(1)}, bf16[256,512]{1,0:T(8,128)(2,1)S(1)}, u32[]{:S(2)}, u32[]{:S(2)}) collective-permute-start(bf16[256,512]{1,0:T(8,128)(2,1)S(1)} %get-tuple-element.210.refs_7_), channel_id=1, source_target_pairs={{2,0},{6,4},{10,8},{14,12},{18,16},{22,20},{26,24},{30,28}} | collective-permute-start | bytes 786440 | tf_op jit(solution)/shard_map/ppermute | solution.py:658
  221.0 14.8 %collective-permute-start.46 = (bf16[8,16,2176]{2,1,0:T(8,128)(2,1)S(1)}, bf16[8,16,2176]{2,1,0:T(8,128)(2,1)S(1)}, u32[]{:S(2)}, u32[]{:S(2)}) collective-permute-start(bf16[8,16,2176]{2,1,0:T(8,128)(2,1)S(1)} %get-tuple-element.206.refs_2_), channel_id=1, source_target_pairs={{0,16},{4,20},{8,24},{12,28},{16,0},{20,4},{24,8},{28,12},{1,17},{... | collective-permute-start | bytes 1671176 | tf_op jit(solution)/shard_map/ppermute | solution.py:695
  (21 other events, 419.7 us)

commit v4 on v3

--- a/solution.py
+++ b/solution.py
@@ -878,16 +878,19 @@
          (add_all, (own, parts[2], long_got), [(rows, width)])]
     )
     a_got, b_got = trade(a_send, "batch", 2), trade(b_send, "batch", 4)
-    (a, a_send), (b, b_send), (feed,) = small_steps(
-        [(add_halves, (a, a_got), [shape(4, wide_rest[0])] * 2),
-         (add_halves, (b, b_got), [shape(4, wide_rest[1])] * 2),
-         (add_all, (own, feed[0], *to_tall(feed)), [shape(1, sum(wide))])]
+    ((feed,),) = small_steps(
+        [(add_all, (own, feed[0], *to_tall(feed)), [shape(1, sum(wide))])]
+    )
+    (a, a_send), (b, b_send) = small_steps(
+        [(add_halves, (tied(a, feed), a_got), [shape(4, wide_rest[0])] * 2),
+         (add_halves, (b, b_got), [shape(4, wide_rest[1])] * 2)]
     )
     feed = sharing.doubled(feed)
     a_got, b_got = trade(a_send, "batch", 4), trade(b_send, "batch", 2)
-    rest, (fa, fb) = small_steps(
-        [(add_to_pieces, (a, a_got, b, b_got), [shape(1, sum(wide_rest))] * 4),
-         (lay, (feed, *to_tall([feed] * 4)), [shape(4, w) for w in wide])]
+    feed_got = to_tall([feed] * 4)
+    (rest,) = small_steps([(add_to_pieces, (a, a_got, b, b_got), [shape(1, sum(wide_rest))] * 4)])
+    ((fa, fb),) = small_steps(
+        [(lay, (tied(feed, rest[0]), *feed_got), [shape(4, w) for w in wide])]
     )
     (rest,), (fa,), (fb,) = small_steps(
         [(add_all, (own, rest[0], *to_tall(rest)), [shape(1, sum(wide_rest))]),

time: 245 us -> 245 us (level)
    pallas_call x20 -> x22, Pallas kernels: 78.1 us -> 77.9 us  [call(): pl.pallas_call(kernel, out_shape=[jax.ShapeDtypeStruct(s, t) for s, t in...]
  transfers between devices with their start and end apart: 50 -> 50, of which waited for: 18 -> 19; matrix products, arithmetic and copies ran while one was open for 1% -> 1% of each run, Pallas kernels for 19% -> 19%
where the time goes in v4:
time: 245 us; the launch traced here: 244 us
  starting transfers between devices  88.3 us (36%)
  Pallas kernels  77.9 us (32%)
  waiting for transfers between devices  68.8 us (28%)
  local copies, waits for them, and re-layouts  4.29 us (2%)
  between operations  2.5 us (1%)
    pallas_call x22, Pallas kernels, call(): pl.pallas_call(kernel, out_shape=[jax.ShapeDtypeStruct(s, t) for s, t in...  77.9 us
    ppermute x32, waiting for transfers between devices, trade(): lax.ppermute(v, axis, [(i, i ^ distance) for i in range(lax.axis_size(axi...  42.7 us
    ppermute x32, starting transfers between devices, trade(): lax.ppermute(v, axis, [(i, i ^ distance) for i in range(lax.axis_size(axi...  41.5 us
    ppermute x6, starting transfers between devices, send_long(): got.append(lax.ppermute(block, 'blk', pairs))  16.1 us
    ppermute x2, starting transfers between devices, send_short_rest(): terms[root].append(lax.ppermute(held, 'blk', pairs))  10.4 us
    ppermute x3, waiting for transfers between devices, return_short(): return lax.ppermute(held, 'blk', pairs)  8.05 us
    ppermute x3, starting transfers between devices, return_long(): return lax.ppermute(block, 'blk', pairs)  7.25 us
    ppermute x3, waiting for transfers between devices, hand_down(): return lax.ppermute(held, 'blk', [(i, i - 1) for i in range(distance, n)])  6.46 us
  transfers between devices with their start and end apart: 50, of which 19 were waited for; matrix products, arithmetic and copies ran while one was open for 1% of the time, Pallas kernels for 19%

profile of v4, /device:TPU:0, one launch (start us, length us, event | category | flops | bytes accessed | tf_op | source)
XLA Modules:
  0.0 243.9 jit_solution(3047213069396064907)
XLA Ops:
  0.7 2.2 shard_map.263
  2.9 6.2 %collective-permute-start = (bf16[512,512]{1,0:T(8,128)(2,1)}, bf16[512,512]{1,0:T(8,128)(2,1)S(1)}, u32[]{:S(2)}, u32[]{:S(2)}) collective-permute-start(bf16[512,512]{1,0:T(8,128)(2,1)} %get-tuple-element.122), channel_id=1, source_target_pairs={{0,2},{4,6},{8,10},{12,14},{16,18},{20,22},{24,26},{28,30}} | collective-permute-start | bytes 1572872 | tf_op jit(solution)/shard_map/ppermute | solution.py:674
  9.2 1.6 collective-permute-start.6
  10.8 2.0 collective-permute-start.5
  12.8 3.2 %collective-permute-start.4 = (bf16[256,512]{1,0:T(8,128)(2,1)}, bf16[256,512]{1,0:T(8,128)(2,1)}, u32[]{:S(2)}, u32[]{:S(2)}) collective-permute-start(bf16[256,512]{1,0:T(8,128)(2,1)} %get-tuple-element.124), channel_id=1, source_target_pairs={{0,1},{1,2},{2,3},{4,5},{5,6},{6,7},{8,9},{9,10},{10,11},{12,13},{... | collective-permute-start | bytes 786440 | tf_op jit(solution)/shard_map/ppermute | solution.py:643
  15.9 5.9 %collective-permute-done = bf16[512,512]{1,0:T(8,128)(2,1)S(1)} collective-permute-done((bf16[512,512]{1,0:T(8,128)(2,1)}, bf16[512,512]{1,0:T(8,128)(2,1)S(1)}, u32[]{:S(2)}, u32[]{:S(2)}) %collective-permute-start) | collective-permute-done | bytes 524320 | tf_op jit(solution)/shard_map/ppermute | solution.py:674
  21.8 1.9 slice_add_fusion
  23.7 2.0 collective-permute-start.8
  27.8 3.4 %collective-permute-start.2 = (bf16[256,512]{1,0:T(8,128)(2,1)}, bf16[256,512]{1,0:T(8,128)(2,1)S(1)}, u32[]{:S(2)}, u32[]{:S(2)}) collective-permute-start(bf16[256,512]{1,0:T(8,128)(2,1)} %get-tuple-element.123), channel_id=1, source_target_pairs={{0,2},{1,3},{2,0},{3,1},{4,6},{5,7},{6,4},{7,5},{8,10},{9,11},{10,... | collective-permute-start | bytes 786440 | tf_op jit(solution)/shard_map/ppermute | solution.py:643
  31.2 1.8 collective-permute-done.5.refs_1_
  33.1 6.0 %collective-permute-start.1 = (bf16[256,512]{1,0:T(8,128)(2,1)}, bf16[256,512]{1,0:T(8,128)(2,1)S(1)}, u32[]{:S(2)}, u32[]{:S(2)}) collective-permute-start(bf16[256,512]{1,0:T(8,128)(2,1)} %get-tuple-element.123), channel_id=1, source_target_pairs={{0,1},{1,2},{2,3},{3,0},{4,5},{5,6},{6,7},{7,4},{8,9},{9,10},{10,1... | collective-permute-start | bytes 786440 | tf_op jit(solution)/shard_map/ppermute | solution.py:643
  39.1 8.4 %collective-permute-start.7 = (bf16[256,512]{1,0:T(8,128)(2,1)S(1)}, bf16[256,512]{1,0:T(8,128)(2,1)S(1)}, u32[]{:S(2)}, u32[]{:S(2)}) collective-permute-start(bf16[256,512]{1,0:T(8,128)(2,1)S(1)} %add.69), channel_id=1, source_target_pairs={{0,1},{2,3},{4,5},{6,7},{8,9},{10,11},{12,13},{14,15},{16,17},{18,... | collective-permute-start | bytes 786440 | tf_op jit(solution)/shard_map/ppermute | solution.py:685
  50.5 11.1 %shard_map.264 = (bf16[512,512]{1,0:T(8,128)(2,1)S(1)}, bf16[11520,3072]{1,0:T(8,128)(2,1)}, bf16[512,512]{1,0:T(8,128)(2,1)S(1)}, f32[8,512]{1,0:T(8,128)S(1)},...) custom-call(s32[2]{0:T(128)S(1)} %pad_add_fusion.order, ...), custom_call_target="tpu_custom_call" | custom-call | flops 12000000000 | tf_op jit(solution)/shard_map/pallas_call | solution.py:613
  61.7 3.8 %collective-permute-done.7.refs_5_ = bf16[256,512]{1,0:T(8,128)(2,1)S(1)} collective-permute-done((bf16[256,512]{1,0:T(8,128)(2,1)S(1)}, bf16[256,512]{1,0:T(8,128)(2,1)S(1)}, u32[]{:S(2)}, u32[]{:S(2)}) %collective-permute-start.7) | collective-permute-done | bytes 262176 | tf_op jit(solution)/shard_map/ppermute | solution.py:685
  65.6 9.8 %shard_map.265 = (bf16[11520,3072]{1,0:T(8,128)(2,1)}, bf16[512,512]{1,0:T(8,128)(2,1)S(1)}, f32[8,512]{1,0:T(8,128)S(1)}, f32[512,512]{1,0:T(8,128)S(1)}, bf16[1,256,512]{2,1,0:T(8,128)(2,1)S(1)}) custom-call(s32[2]{0:T(128)S(1)} %pad_add_fusion.order, s32[1]{0:T(128)} %bitcast.2.rank, s32[2,4]{1,0:T(2,128)S(1)} %copy-done.15, ...), custom_call_target="tpu_custom_call" | custom-call | flops 11000000512 | tf_op jit(solution)/shard_map/pallas_call | solution.py:613
  75.5 14.7 %shard_map.266 = (bf16[2,256,512]{2,1,0:T(8,128)(2,1)}, f32[512,512]{1,0:T(8,128)S(1)}, bf16[16,16,4096]{2,1,0:T(8,128)(2,1)S(1)}, bf16[16,16,4096]{2,1,0:T(8,12...) custom-call(s32[2]{0:T(128)S(1)} %pad_add_fusion.order, s32[2]{0:T(128)S(1)} %pad_add_fusion.1.codes, ...), custom_call_target="tpu_custom_call" | custom-call | flops 14000000000 | tf_op jit(solution)/shard_map/pallas_call | solution.py:613
  90.3 9.8 %shard_map.267 = (bf16[256,512]{1,0:T(8,128)(2,1)S(1)}, bf16[512,512]{1,0:T(8,128)(2,1)S(1)}, bf16[256,512]{1,0:T(8,128)(2,1)S(1)}, bf16[256,512]{1,0:T(8,128)(2...) custom-call(f32[512,512]{1,0:T(8,128)S(1)} %get-tuple-element.132.grad.refs_4_, ...), custom_call_target="tpu_custom_call" | custom-call | flops 10000000000 | tf_op jit(solution)/shard_map/pallas_call | solution.py:613
  100.0 3.4 %collective-permute-start.15 = (bf16[256,512]{1,0:T(8,128)(2,1)S(1)}, bf16[256,512]{1,0:T(8,128)(2,1)S(1)}, u32[]{:S(2)}, u32[]{:S(2)}) collective-permute-start(bf16[256,512]{1,0:T(8,128)(2,1)S(1)} %get-tuple-element.167), channel_id=1, source_target_pairs={{0,2},{1,3},{2,0},{3,1},{4,6},{5,7},{6,4},{7,5},{8,10},{9,11},{10,... | collective-permute-start | bytes 786440 | tf_op jit(solution)/shard_map/ppermute | solution.py:649
  103.5 3.8 %collective-permute-start.14 = (bf16[512,512]{1,0:T(8,128)(2,1)S(1)}, bf16[512,512]{1,0:T(8,128)(2,1)S(1)}, u32[]{:S(2)}, u32[]{:S(2)}) collective-permute-start(bf16[512,512]{1,0:T(8,128)(2,1)S(1)} %get-tuple-element.166.refs_1_), channel_id=1, source_target_pairs={{0,3},{1,0},{2,1},{3,2},{4,7},{5,4},{6,5},{7,6},{8,11},{9,8},{10,9... | collective-permute-start | bytes 1572872 | tf_op jit(solution)/shard_map/ppermute | solution.py:649
  107.3 3.3 %shard_map.268 = (f32[512,512]{1,0:T(8,128)S(1)}, bf16[512,2048]{1,0:T(8,128)(2,1)S(1)}, f32[2,512]{1,0:T(2,128)S(1)}) custom-call(s32[2]{0:T(128)S(1)} %pad_add_fusion.order, bf16[2,256,512]{2,1,0:T(8,128)(2,1)S(1)} %copy-done.12, bf16[256,512]{1,0:T(8,128)(2,1)S(1)} %collective-permute-done.1.refs_0_, bf16[256,512]{1,0:T(8,128)(2,1)S(1)} %collective-permute-done.2.refs_1_, ...), custom_call_target="tpu_custom_call" | custom-call | flops 4000000000 | tf_op jit(solution)/shard_map/pallas_call | solution.py:613
  110.9 1.5 collective-permute-start.10
  113.9 14.0 %shard_map.270 = (bf16[256,512]{1,0:T(8,128)(2,1)S(1)}, bf16[256,512]{1,0:T(8,128)(2,1)S(1)}, bf16[256,512]{1,0:T(8,128)(2,1)S(1)}, bf16[256,512]{1,0:T(8,128)(2...) custom-call(s32[2]{0:T(128)S(1)} %pad_add_fusion.order, ...), custom_call_target="tpu_custom_call" | custom-call | flops 14000000000 | tf_op jit(solution)/shard_map/pallas_call | solution.py:613
  130.1 1.5 collective-permute-start.12
  131.7 6.4 %collective-permute-done.13.refs_3_ = bf16[4,16,2048]{2,1,0:T(8,128)(2,1)S(1)} collective-permute-done((bf16[4,16,2048]{2,1,0:T(8,128)(2,1)S(1)}, bf16[4,16,2048]{2,1,0:T(8,128)(2,1)S(1)}, u32[]{:S(2)}, u32[]{:S(2)}) %collective-permute-start.13) | collective-permute-done | bytes 262176 | tf_op jit(solution)/shard_map/ppermute | solution.py:695
  138.9 1.6 collective-permute-start.23
  141.0 6.1 %collective-permute-start.19 = (bf16[1,16,4096]{2,1,0:T(8,128)(2,1)S(1)}, bf16[1,16,4096]{2,1,0:T(8,128)(2,1)S(1)}, u32[]{:S(2)}, u32[]{:S(2)}) collective-permute-start(bf16[1,16,4096]{2,1,0:T(8,128)(2,1)S(1)} %get-tuple-element.176), channel_id=1, source_target_pairs={{0,1},{1,0},{2,3},{3,2},{4,5},{5,4},{6,7},{7,6},{8,9},{9,8},{10,11... | collective-permute-start | bytes 393224 | tf_op jit(solution)/shard_map/ppermute | solution.py:695
  147.1 3.0 %collective-permute-start.20 = (bf16[1,16,4096]{2,1,0:T(8,128)(2,1)S(1)}, bf16[1,16,4096]{2,1,0:T(8,128)(2,1)S(1)}, u32[]{:S(2)}, u32[]{:S(2)}) collective-permute-start(bf16[1,16,4096]{2,1,0:T(8,128)(2,1)S(1)} %get-tuple-element.177), channel_id=1, source_target_pairs={{0,2},{1,3},{2,0},{3,1},{4,6},{5,7},{6,4},{7,5},{8,10},{9,11},{10,... | collective-permute-start | bytes 393224 | tf_op jit(solution)/shard_map/ppermute | solution.py:695
  151.2 7.8 %collective-permute-done.20.refs_3_ = bf16[1,16,4096]{2,1,0:T(8,128)(2,1)S(1)} collective-permute-done((bf16[1,16,4096]{2,1,0:T(8,128)(2,1)S(1)}, bf16[1,16,4096]{2,1,0:T(8,128)(2,1)S(1)}, u32[]{:S(2)}, u32[]{:S(2)}) %collective-permute-start.20) | collective-permute-done | bytes 131104 | tf_op jit(solution)/shard_map/ppermute | solution.py:695
  161.3 2.4 collective-permute-start.31
  167.3 2.1 collective-permute-done.31.refs_3_
  169.3 4.0 %collective-permute-done.30.refs_2_ = bf16[1,16,4096]{2,1,0:T(8,128)(2,1)S(1)} collective-permute-done((bf16[1,16,4096]{2,1,0:T(8,128)(2,1)S(1)}, bf16[1,16,4096]{2,1,0:T(8,128)(2,1)S(1)}, u32[]{:S(2)}, u32[]{:S(2)}) %collective-permute-start.30) | collective-permute-done | bytes 131104 | tf_op jit(solution)/shard_map/ppermute | solution.py:695
  173.4 1.6 collective-permute-start.32
  176.0 3.4 %collective-permute-start.27 = (bf16[1,16,4224]{2,1,0:T(8,128)(2,1)S(1)}, bf16[1,16,4224]{2,1,0:T(8,128)(2,1)S(1)}, u32[]{:S(2)}, u32[]{:S(2)}) collective-permute-start(bf16[1,16,4224]{2,1,0:T(8,128)(2,1)S(1)} %get-tuple-element.189), channel_id=1, source_target_pairs={{0,2},{1,3},{2,0},{3,1},{4,6},{5,7},{6,4},{7,5},{8,10},{9,11},{10,... | collective-permute-start | bytes 405512 | tf_op jit(solution)/shard_map/ppermute | solution.py:695
  179.9 2.2 collective-permute-done.26.refs_2_
  182.2 7.0 %collective-permute-done.27.refs_3_ = bf16[1,16,4224]{2,1,0:T(8,128)(2,1)S(1)} collective-permute-done((bf16[1,16,4224]{2,1,0:T(8,128)(2,1)S(1)}, bf16[1,16,4224]{2,1,0:T(8,128)(2,1)S(1)}, u32[]{:S(2)}, u32[]{:S(2)}) %collective-permute-start.27) | collective-permute-done | bytes 135200 | tf_op jit(solution)/shard_map/ppermute | solution.py:695
  191.2 2.4 collective-permute-start.36
  193.6 2.0 collective-permute-start.35
  196.1 3.3 %collective-permute-done.36.refs_3_ = bf16[1,16,4224]{2,1,0:T(8,128)(2,1)S(1)} collective-permute-done((bf16[1,16,4224]{2,1,0:T(8,128)(2,1)S(1)}, bf16[1,16,4224]{2,1,0:T(8,128)(2,1)S(1)}, u32[]{:S(2)}, u32[]{:S(2)}) %collective-permute-start.36) | collective-permute-done | bytes 135200 | tf_op jit(solution)/shard_map/ppermute | solution.py:695
  199.4 3.7 %collective-permute-done.35.refs_2_ = bf16[1,16,4224]{2,1,0:T(8,128)(2,1)S(1)} collective-permute-done((bf16[1,16,4224]{2,1,0:T(8,128)(2,1)S(1)}, bf16[1,16,4224]{2,1,0:T(8,128)(2,1)S(1)}, u32[]{:S(2)}, u32[]{:S(2)}) %collective-permute-start.35) | collective-permute-done | bytes 135200 | tf_op jit(solution)/shard_map/ppermute | solution.py:695
  207.2 1.7 collective-permute-start.39
  209.0 5.2 %collective-permute-done.42.refs_9_ = bf16[256,512]{1,0:T(8,128)(2,1)S(1)} collective-permute-done((bf16[256,512]{1,0:T(8,128)(2,1)S(1)}, bf16[256,512]{1,0:T(8,128)(2,1)S(1)}, u32[]{:S(2)}, u32[]{:S(2)}) %collective-permute-start.42) | collective-permute-done | bytes 262176 | tf_op jit(solution)/shard_map/ppermute | solution.py:658
  214.2 2.8 %collective-permute-done.43.refs_12_ = bf16[256,512]{1,0:T(8,128)(2,1)S(1)} collective-permute-done((bf16[256,512]{1,0:T(8,128)(2,1)S(1)}, bf16[256,512]{1,0:T(8,128)(2,1)S(1)}, u32[]{:S(2)}, u32[]{:S(2)}) %collective-permute-start.43) | collective-permute-done | bytes 262176 | tf_op jit(solution)/shard_map/ppermute | solution.py:658
  220.7 1.7 collective-permute-start.46
  222.4 4.5 %shard_map.281 = (f32[512,2048]{1,0:T(8,128)}, f32[2048,512]{1,0:T(8,128)}) custom-call(s32[2]{0:T(128)S(1)} %pad_add_fusion.1.codes, bf16[16,16,4096]{2,1,0:T(8,128)(2,1)S(1)} %get-tuple-element.210.refs_0_, bf16[16,16,4096]{2,1,0:T(8,128)(2,1)S(1)} %collective-permute-done.47.refs_1_), custom_call_target="tpu_custom_call" | custom-call | flops 6000000000 | tf_op jit(solution)/shard_map/pallas_call | solution.py:613
  227.6 6.5 %collective-permute-done.44.refs_5_.part_got = bf16[256,512]{1,0:T(8,128)(2,1)S(1)} collective-permute-done((bf16[256,512]{1,0:T(8,128)(2,1)S(1)}, bf16[256,512]{1,0:T(8,128)(2,1)S(1)}, u32[]{:S(2)}, u32[]{:S(2)}) %collective-permute-start.44) | collective-permute-done | bytes 262176 | tf_op jit(solution)/shard_map/ppermute | solution.py:653
  235.8 2.6 %shard_map.283 = (f32[2,256,512]{2,1,0:T(8,128)}, f32[2,256,512]{2,1,0:T(8,128)}) custom-call(s32[2]{0:T(128)S(1)} %pad_add_fusion.order, s32[1]{0:T(128)} %bitcast.2.rank, bf16[2,256,512]{2,1,0:T(8,128)(2,1)S(1)} %copy-done.4, f32[512,512]{1,0:T(8,128)S(1)} %get-tuple-element.140.refs_4_.self_grad, ...), custom_call_target="tpu_custom_call" | custom-call | flops 3000000000 | tf_op jit(solution)/shard_map/pallas_call | solution.py:613
  238.4 1.6 collective-permute-done.49.refs_1_
  240.0 3.9 %shard_map.284 = (f32[512,1024]{1,0:T(8,128)}, f32[512,512]{1,0:T(8,128)}, f32[512,512]{1,0:T(8,128)}, f32[512,1536]{1,0:T(8,128)}, f32[512,512]{1,0:T(8,128)}, ...) custom-call(s32[2]{0:T(128)S(1)} %pad_add_fusion.1.codes, ...), custom_call_target="tpu_custom_call" | custom-call | flops 5000000000 | tf_op jit(solution)/shard_map/pallas_call | solution.py:613
  (120 shorter events, 30.5 us)
Async XLA Ops:
  2.9 18.9 %collective-permute-start = (bf16[512,512]{1,0:T(8,128)(2,1)}, bf16[512,512]{1,0:T(8,128)(2,1)S(1)}, u32[]{:S(2)}, u32[]{:S(2)}) collective-permute-start(bf16[512,512]{1,0:T(8,128)(2,1)} %get-tuple-element.122), channel_id=1, source_target_pairs={{0,2},{4,6},{8,10},{12,14},{16,18},{20,22},{24,26},{28,30}} | collective-permute-start | bytes 1572872 | tf_op jit(solution)/shard_map/ppermute | solution.py:674
  9.2 18.6 %collective-permute-start.6 = (bf16[256,512]{1,0:T(8,128)(2,1)}, bf16[256,512]{1,0:T(8,128)(2,1)S(1)}, u32[]{:S(2)}, u32[]{:S(2)}) collective-permute-start(bf16[256,512]{1,0:T(8,128)(2,1)} %get-tuple-element.124), channel_id=1, source_target_pairs={{0,3},{4,7},{8,11},{12,15},{16,19},{20,23},{24,27},{28,31}} | collective-permute-start | bytes 786440 | tf_op jit(solution)/shard_map/ppermute | solution.py:643
  10.8 22.3 %collective-permute-start.5 = (bf16[256,512]{1,0:T(8,128)(2,1)}, bf16[256,512]{1,0:T(8,128)(2,1)}, u32[]{:S(2)}, u32[]{:S(2)}) collective-permute-start(bf16[256,512]{1,0:T(8,128)(2,1)} %get-tuple-element.124), channel_id=1, source_target_pairs={{0,2},{1,3},{4,6},{5,7},{8,10},{9,11},{12,14},{13,15},{16,18},{17,... | collective-permute-start | bytes 786440 | tf_op jit(solution)/shard_map/ppermute | solution.py:643
  12.8 26.3 %collective-permute-start.4 = (bf16[256,512]{1,0:T(8,128)(2,1)}, bf16[256,512]{1,0:T(8,128)(2,1)}, u32[]{:S(2)}, u32[]{:S(2)}) collective-permute-start(bf16[256,512]{1,0:T(8,128)(2,1)} %get-tuple-element.124), channel_id=1, source_target_pairs={{0,1},{1,2},{2,3},{4,5},{5,6},{6,7},{8,9},{9,10},{10,11},{12,13},{... | collective-permute-start | bytes 786440 | tf_op jit(solution)/shard_map/ppermute | solution.py:643
  23.7 23.8 %collective-permute-start.8 = (bf16[256,512]{1,0:T(8,128)(2,1)}, bf16[256,512]{1,0:T(8,128)(2,1)}, u32[]{:S(2)}, u32[]{:S(2)}) collective-permute-start(bf16[256,512]{1,0:T(8,128)(2,1)} %get-tuple-element.228), channel_id=1, source_target_pairs={{0,1},{2,3},{4,5},{6,7},{8,9},{10,11},{12,13},{14,15},{16,17},{18,... | collective-permute-start | bytes 786440 | tf_op jit(solution)/shard_map/ppermute | solution.py:685
  27.8 33.9 %collective-permute-start.3 = (bf16[256,512]{1,0:T(8,128)(2,1)}, bf16[256,512]{1,0:T(8,128)(2,1)S(1)}, u32[]{:S(2)}, u32[]{:S(2)}) collective-permute-start(bf16[256,512]{1,0:T(8,128)(2,1)} %get-tuple-element.123), channel_id=1, source_target_pairs={{0,3},{1,0},{2,1},{3,2},{4,7},{5,4},{6,5},{7,6},{8,11},{9,8},{10,9... | collective-permute-start | bytes 786440 | tf_op jit(solution)/shard_map/ppermute | solution.py:643
  27.8 33.9 %collective-permute-start.2 = (bf16[256,512]{1,0:T(8,128)(2,1)}, bf16[256,512]{1,0:T(8,128)(2,1)S(1)}, u32[]{:S(2)}, u32[]{:S(2)}) collective-permute-start(bf16[256,512]{1,0:T(8,128)(2,1)} %get-tuple-element.123), channel_id=1, source_target_pairs={{0,2},{1,3},{2,0},{3,1},{4,6},{5,7},{6,4},{7,5},{8,10},{9,11},{10,... | collective-permute-start | bytes 786440 | tf_op jit(solution)/shard_map/ppermute | solution.py:643
  33.1 28.7 %collective-permute-start.1 = (bf16[256,512]{1,0:T(8,128)(2,1)}, bf16[256,512]{1,0:T(8,128)(2,1)S(1)}, u32[]{:S(2)}, u32[]{:S(2)}) collective-permute-start(bf16[256,512]{1,0:T(8,128)(2,1)} %get-tuple-element.123), channel_id=1, source_target_pairs={{0,1},{1,2},{2,3},{3,0},{4,5},{5,6},{6,7},{7,4},{8,9},{9,10},{10,1... | collective-permute-start | bytes 786440 | tf_op jit(solution)/shard_map/ppermute | solution.py:643
  39.1 26.4 %collective-permute-start.7 = (bf16[256,512]{1,0:T(8,128)(2,1)S(1)}, bf16[256,512]{1,0:T(8,128)(2,1)S(1)}, u32[]{:S(2)}, u32[]{:S(2)}) collective-permute-start(bf16[256,512]{1,0:T(8,128)(2,1)S(1)} %add.69), channel_id=1, source_target_pairs={{0,1},{2,3},{4,5},{6,7},{8,9},{10,11},{12,13},{14,15},{16,17},{18,... | collective-permute-start | bytes 786440 | tf_op jit(solution)/shard_map/ppermute | solution.py:685
  90.2 20.4 %collective-permute-start.9 = (bf16[16,16,4096]{2,1,0:T(8,128)(2,1)S(1)}, bf16[16,16,4096]{2,1,0:T(8,128)(2,1)S(1)}, u32[]{:S(2)}, u32[]{:S(2)}) collective-permute-start(bf16[16,16,4096]{2,1,0:T(8,128)(2,1)S(1)} %get-tuple-element.151), channel_id=1, source_target_pairs={{0,4},{4,0},{8,12},{12,8},{16,20},{20,16},{24,28},{28,24},{1,5},{5... | collective-permute-start | bytes 6291464 | tf_op jit(solution)/shard_map/ppermute | solution.py:695
  100.0 28.1 %collective-permute-start.15 = (bf16[256,512]{1,0:T(8,128)(2,1)S(1)}, bf16[256,512]{1,0:T(8,128)(2,1)S(1)}, u32[]{:S(2)}, u32[]{:S(2)}) collective-permute-start(bf16[256,512]{1,0:T(8,128)(2,1)S(1)} %get-tuple-element.167), channel_id=1, source_target_pairs={{0,2},{1,3},{2,0},{3,1},{4,6},{5,7},{6,4},{7,5},{8,10},{9,11},{10,... | collective-permute-start | bytes 786440 | tf_op jit(solution)/shard_map/ppermute | solution.py:649
  103.5 24.6 %collective-permute-start.16 = (bf16[256,512]{1,0:T(8,128)(2,1)S(1)}, bf16[256,512]{1,0:T(8,128)(2,1)S(1)}, u32[]{:S(2)}, u32[]{:S(2)}) collective-permute-start(bf16[256,512]{1,0:T(8,128)(2,1)S(1)} %get-tuple-element.168), channel_id=1, source_target_pairs={{0,1},{1,2},{2,3},{3,0},{4,5},{5,6},{6,7},{7,4},{8,9},{9,10},{10,1... | collective-permute-start | bytes 786440 | tf_op jit(solution)/shard_map/ppermute | solution.py:649
  103.5 24.6 %collective-permute-start.14 = (bf16[512,512]{1,0:T(8,128)(2,1)S(1)}, bf16[512,512]{1,0:T(8,128)(2,1)S(1)}, u32[]{:S(2)}, u32[]{:S(2)}) collective-permute-start(bf16[512,512]{1,0:T(8,128)(2,1)S(1)} %get-tuple-element.166.refs_1_), channel_id=1, source_target_pairs={{0,3},{1,0},{2,1},{3,2},{4,7},{5,4},{6,5},{7,6},{8,11},{9,8},{10,9... | collective-permute-start | bytes 1572872 | tf_op jit(solution)/shard_map/ppermute | solution.py:649
  110.9 17.1 %collective-permute-start.10 = (bf16[8,16,2048]{2,1,0:T(8,128)(2,1)S(1)}, bf16[8,16,2048]{2,1,0:T(8,128)(2,1)S(1)}, u32[]{:S(2)}, u32[]{:S(2)}) collective-permute-start(bf16[8,16,2048]{2,1,0:T(8,128)(2,1)S(1)} %get-tuple-element.155), channel_id=1, source_target_pairs={{0,8},{4,12},{8,0},{12,4},{16,24},{20,28},{24,16},{28,20},{1,9},{5... | collective-permute-start | bytes 1572872 | tf_op jit(solution)/shard_map/ppermute | solution.py:695
  112.4 15.6 %collective-permute-start.11 = (bf16[8,16,2048]{2,1,0:T(8,128)(2,1)S(1)}, bf16[8,16,2048]{2,1,0:T(8,128)(2,1)S(1)}, u32[]{:S(2)}, u32[]{:S(2)}) collective-permute-start(bf16[8,16,2048]{2,1,0:T(8,128)(2,1)S(1)} %get-tuple-element.157), channel_id=1, source_target_pairs={{0,16},{4,20},{8,24},{12,28},{16,0},{20,4},{24,8},{28,12},{1,17},{... | collective-permute-start | bytes 1572872 | tf_op jit(solution)/shard_map/ppermute | solution.py:695
  128.3 10.3 %collective-permute-start.17 = (bf16[16,16,4224]{2,1,0:T(8,128)(2,1)S(1)}, bf16[16,16,4224]{2,1,0:T(8,128)(2,1)S(1)}, u32[]{:S(2)}, u32[]{:S(2)}) collective-permute-start(bf16[16,16,4224]{2,1,0:T(8,128)(2,1)S(1)} %get-tuple-element.170), channel_id=1, source_target_pairs={{0,4},{4,0},{8,12},{12,8},{16,20},{20,16},{24,28},{28,24},{1,5},{5... | collective-permute-start | bytes 6488072 | tf_op jit(solution)/shard_map/ppermute | solution.py:695
  129.3 8.8 %collective-permute-start.13 = (bf16[4,16,2048]{2,1,0:T(8,128)(2,1)S(1)}, bf16[4,16,2048]{2,1,0:T(8,128)(2,1)S(1)}, u32[]{:S(2)}, u32[]{:S(2)}) collective-permute-start(bf16[4,16,2048]{2,1,0:T(8,128)(2,1)S(1)} %get-tuple-element.161), channel_id=1, source_target_pairs={{0,8},{4,12},{8,0},{12,4},{16,24},{20,28},{24,16},{28,20},{1,9},{5... | collective-permute-start | bytes 786440 | tf_op jit(solution)/shard_map/ppermute | solution.py:695
  130.1 8.4 %collective-permute-start.12 = (bf16[4,16,2048]{2,1,0:T(8,128)(2,1)S(1)}, bf16[4,16,2048]{2,1,0:T(8,128)(2,1)S(1)}, u32[]{:S(2)}, u32[]{:S(2)}) collective-permute-start(bf16[4,16,2048]{2,1,0:T(8,128)(2,1)S(1)} %get-tuple-element.159), channel_id=1, source_target_pairs={{0,16},{4,20},{8,24},{12,28},{16,0},{20,4},{24,8},{28,12},{1,17},{... | collective-permute-start | bytes 786440 | tf_op jit(solution)/shard_map/ppermute | solution.py:695
  138.9 20.2 %collective-permute-start.23 = (bf16[8,16,2176]{2,1,0:T(8,128)(2,1)S(1)}, bf16[8,16,2176]{2,1,0:T(8,128)(2,1)S(1)}, u32[]{:S(2)}, u32[]{:S(2)}) collective-permute-start(bf16[8,16,2176]{2,1,0:T(8,128)(2,1)S(1)} %get-tuple-element.182), channel_id=1, source_target_pairs={{0,16},{4,20},{8,24},{12,28},{16,0},{20,4},{24,8},{28,12},{1,17},{... | collective-permute-start | bytes 1671176 | tf_op jit(solution)/shard_map/ppermute | solution.py:695
  140.5 18.6 %collective-permute-start.22 = (bf16[8,16,2048]{2,1,0:T(8,128)(2,1)S(1)}, bf16[8,16,2048]{2,1,0:T(8,128)(2,1)S(1)}, u32[]{:S(2)}, u32[]{:S(2)}) collective-permute-start(bf16[8,16,2048]{2,1,0:T(8,128)(2,1)S(1)} %get-tuple-element.180), channel_id=1, source_target_pairs={{0,8},{4,12},{8,0},{12,4},{16,24},{20,28},{24,16},{28,20},{1,9},{5... | collective-permute-start | bytes 1572872 | tf_op jit(solution)/shard_map/ppermute | solution.py:695
  141.0 10.2 %collective-permute-start.19 = (bf16[1,16,4096]{2,1,0:T(8,128)(2,1)S(1)}, bf16[1,16,4096]{2,1,0:T(8,128)(2,1)S(1)}, u32[]{:S(2)}, u32[]{:S(2)}) collective-permute-start(bf16[1,16,4096]{2,1,0:T(8,128)(2,1)S(1)} %get-tuple-element.176), channel_id=1, source_target_pairs={{0,1},{1,0},{2,3},{3,2},{4,5},{5,4},{6,7},{7,6},{8,9},{9,8},{10,11... | collective-permute-start | bytes 393224 | tf_op jit(solution)/shard_map/ppermute | solution.py:695
  147.1 12.0 %collective-permute-start.20 = (bf16[1,16,4096]{2,1,0:T(8,128)(2,1)S(1)}, bf16[1,16,4096]{2,1,0:T(8,128)(2,1)S(1)}, u32[]{:S(2)}, u32[]{:S(2)}) collective-permute-start(bf16[1,16,4096]{2,1,0:T(8,128)(2,1)S(1)} %get-tuple-element.177), channel_id=1, source_target_pairs={{0,2},{1,3},{2,0},{3,1},{4,6},{5,7},{6,4},{7,5},{8,10},{9,11},{10,... | collective-permute-start | bytes 393224 | tf_op jit(solution)/shard_map/ppermute | solution.py:695
  150.1 9.0 %collective-permute-start.21 = (bf16[1,16,4096]{2,1,0:T(8,128)(2,1)S(1)}, bf16[1,16,4096]{2,1,0:T(8,128)(2,1)S(1)}, u32[]{:S(2)}, u32[]{:S(2)}) collective-permute-start(bf16[1,16,4096]{2,1,0:T(8,128)(2,1)S(1)} %get-tuple-element.178), channel_id=1, source_target_pairs={{0,3},{1,2},{2,1},{3,0},{4,7},{5,6},{6,5},{7,4},{8,11},{9,10},{10,... | collective-permute-start | bytes 393224 | tf_op jit(solution)/shard_map/ppermute | solution.py:695
  159.3 7.9 %collective-permute-start.25 = (bf16[4,16,2176]{2,1,0:T(8,128)(2,1)S(1)}, bf16[4,16,2176]{2,1,0:T(8,128)(2,1)S(1)}, u32[]{:S(2)}, u32[]{:S(2)}) collective-permute-start(bf16[4,16,2176]{2,1,0:T(8,128)(2,1)S(1)} %get-tuple-element.186), channel_id=1, source_target_pairs={{0,8},{4,12},{8,0},{12,4},{16,24},{20,28},{24,16},{28,20},{1,9},{5... | collective-permute-start | bytes 835592 | tf_op jit(solution)/shard_map/ppermute | solution.py:695
  160.8 6.4 %collective-permute-start.24 = (bf16[4,16,2048]{2,1,0:T(8,128)(2,1)S(1)}, bf16[4,16,2048]{2,1,0:T(8,128)(2,1)S(1)}, u32[]{:S(2)}, u32[]{:S(2)}) collective-permute-start(bf16[4,16,2048]{2,1,0:T(8,128)(2,1)S(1)} %get-tuple-element.184), channel_id=1, source_target_pairs={{0,16},{4,20},{8,24},{12,28},{16,0},{20,4},{24,8},{28,12},{1,17},{... | collective-permute-start | bytes 786440 | tf_op jit(solution)/shard_map/ppermute | solution.py:695
  161.3 8.0 %collective-permute-start.31 = (bf16[1,16,4096]{2,1,0:T(8,128)(2,1)S(1)}, bf16[1,16,4096]{2,1,0:T(8,128)(2,1)S(1)}, u32[]{:S(2)}, u32[]{:S(2)}) collective-permute-start(bf16[1,16,4096]{2,1,0:T(8,128)(2,1)S(1)} %shard_map.274.refs_0_), channel_id=1, source_target_pairs={{0,3},{1,2},{2,1},{3,0},{4,7},{5,6},{6,5},{7,4},{8,11},{9,10},{10,... | collective-permute-start | bytes 393224 | tf_op jit(solution)/shard_map/ppermute | solution.py:695
  163.7 9.6 %collective-permute-start.30 = (bf16[1,16,4096]{2,1,0:T(8,128)(2,1)S(1)}, bf16[1,16,4096]{2,1,0:T(8,128)(2,1)S(1)}, u32[]{:S(2)}, u32[]{:S(2)}) collective-permute-start(bf16[1,16,4096]{2,1,0:T(8,128)(2,1)S(1)} %shard_map.274.refs_0_), channel_id=1, source_target_pairs={{0,2},{1,3},{2,0},{3,1},{4,6},{5,7},{6,4},{7,5},{8,10},{9,11},{10,... | collective-permute-start | bytes 393224 | tf_op jit(solution)/shard_map/ppermute | solution.py:695
  164.8 8.6 %collective-permute-start.29 = (bf16[1,16,4096]{2,1,0:T(8,128)(2,1)S(1)}, bf16[1,16,4096]{2,1,0:T(8,128)(2,1)S(1)}, u32[]{:S(2)}, u32[]{:S(2)}) collective-permute-start(bf16[1,16,4096]{2,1,0:T(8,128)(2,1)S(1)} %shard_map.274.refs_0_), channel_id=1, source_target_pairs={{0,1},{1,0},{2,3},{3,2},{4,5},{5,4},{6,7},{7,6},{8,9},{9,8},{10,11... | collective-permute-start | bytes 393224 | tf_op jit(solution)/shard_map/ppermute | solution.py:695
  173.4 15.8 %collective-permute-start.32 = (bf16[4,16,2048]{2,1,0:T(8,128)(2,1)S(1)}, bf16[4,16,2048]{2,1,0:T(8,128)(2,1)S(1)}, u32[]{:S(2)}, u32[]{:S(2)}) collective-permute-start(bf16[4,16,2048]{2,1,0:T(8,128)(2,1)S(1)} %get-tuple-element.192.refs_5_), channel_id=1, source_target_pairs={{0,16},{4,20},{8,24},{12,28},{16,0},{20,4},{24,8},{28,12},{1,17},{... | collective-permute-start | bytes 786440 | tf_op jit(solution)/shard_map/ppermute | solution.py:695
  174.9 14.2 %collective-permute-start.33 = (bf16[4,16,2048]{2,1,0:T(8,128)(2,1)S(1)}, bf16[4,16,2048]{2,1,0:T(8,128)(2,1)S(1)}, u32[]{:S(2)}, u32[]{:S(2)}) collective-permute-start(bf16[4,16,2048]{2,1,0:T(8,128)(2,1)S(1)} %get-tuple-element.193.refs_7_), channel_id=1, source_target_pairs={{0,8},{4,12},{8,0},{12,4},{16,24},{20,28},{24,16},{28,20},{1,9},{5... | collective-permute-start | bytes 786440 | tf_op jit(solution)/shard_map/ppermute | solution.py:695
  175.6 6.6 %collective-permute-start.26 = (bf16[1,16,4224]{2,1,0:T(8,128)(2,1)S(1)}, bf16[1,16,4224]{2,1,0:T(8,128)(2,1)S(1)}, u32[]{:S(2)}, u32[]{:S(2)}) collective-permute-start(bf16[1,16,4224]{2,1,0:T(8,128)(2,1)S(1)} %get-tuple-element.188), channel_id=1, source_target_pairs={{0,1},{1,0},{2,3},{3,2},{4,5},{5,4},{6,7},{7,6},{8,9},{9,8},{10,11... | collective-permute-start | bytes 405512 | tf_op jit(solution)/shard_map/ppermute | solution.py:695
  176.0 13.1 %collective-permute-start.27 = (bf16[1,16,4224]{2,1,0:T(8,128)(2,1)S(1)}, bf16[1,16,4224]{2,1,0:T(8,128)(2,1)S(1)}, u32[]{:S(2)}, u32[]{:S(2)}) collective-permute-start(bf16[1,16,4224]{2,1,0:T(8,128)(2,1)S(1)} %get-tuple-element.189), channel_id=1, source_target_pairs={{0,2},{1,3},{2,0},{3,1},{4,6},{5,7},{6,4},{7,5},{8,10},{9,11},{10,... | collective-permute-start | bytes 405512 | tf_op jit(solution)/shard_map/ppermute | solution.py:695
  179.4 9.7 %collective-permute-start.28 = (bf16[1,16,4224]{2,1,0:T(8,128)(2,1)S(1)}, bf16[1,16,4224]{2,1,0:T(8,128)(2,1)S(1)}, u32[]{:S(2)}, u32[]{:S(2)}) collective-permute-start(bf16[1,16,4224]{2,1,0:T(8,128)(2,1)S(1)} %get-tuple-element.190), channel_id=1, source_target_pairs={{0,3},{1,2},{2,1},{3,0},{4,7},{5,6},{6,5},{7,4},{8,11},{9,10},{10,... | collective-permute-start | bytes 405512 | tf_op jit(solution)/shard_map/ppermute | solution.py:695
  189.3 13.8 %collective-permute-start.37 = (bf16[8,16,2048]{2,1,0:T(8,128)(2,1)S(1)}, bf16[8,16,2048]{2,1,0:T(8,128)(2,1)S(1)}, u32[]{:S(2)}, u32[]{:S(2)}) collective-permute-start(bf16[8,16,2048]{2,1,0:T(8,128)(2,1)S(1)} %get-tuple-element.195.refs_4_), channel_id=1, source_target_pairs={{0,8},{4,12},{8,0},{12,4},{16,24},{20,28},{24,16},{28,20},{1,9},{5... | collective-permute-start | bytes 1572872 | tf_op jit(solution)/shard_map/ppermute | solution.py:695
  189.6 13.5 %collective-permute-start.38 = (bf16[8,16,2048]{2,1,0:T(8,128)(2,1)S(1)}, bf16[8,16,2048]{2,1,0:T(8,128)(2,1)S(1)}, u32[]{:S(2)}, u32[]{:S(2)}) collective-permute-start(bf16[8,16,2048]{2,1,0:T(8,128)(2,1)S(1)} %get-tuple-element.196.refs_6_), channel_id=1, source_target_pairs={{0,16},{4,20},{8,24},{12,28},{16,0},{20,4},{24,8},{28,12},{1,17},{... | collective-permute-start | bytes 1572872 | tf_op jit(solution)/shard_map/ppermute | solution.py:695
  191.2 8.3 %collective-permute-start.36 = (bf16[1,16,4224]{2,1,0:T(8,128)(2,1)S(1)}, bf16[1,16,4224]{2,1,0:T(8,128)(2,1)S(1)}, u32[]{:S(2)}, u32[]{:S(2)}) collective-permute-start(bf16[1,16,4224]{2,1,0:T(8,128)(2,1)S(1)} %get-tuple-element.194.refs_0_), channel_id=1, source_target_pairs={{0,3},{1,2},{2,1},{3,0},{4,7},{5,6},{6,5},{7,4},{8,11},{9,10},{10,... | collective-permute-start | bytes 405512 | tf_op jit(solution)/shard_map/ppermute | solution.py:695
  193.6 9.5 %collective-permute-start.35 = (bf16[1,16,4224]{2,1,0:T(8,128)(2,1)S(1)}, bf16[1,16,4224]{2,1,0:T(8,128)(2,1)S(1)}, u32[]{:S(2)}, u32[]{:S(2)}) collective-permute-start(bf16[1,16,4224]{2,1,0:T(8,128)(2,1)S(1)} %get-tuple-element.194.refs_0_), channel_id=1, source_target_pairs={{0,2},{1,3},{2,0},{3,1},{4,6},{5,7},{6,4},{7,5},{8,10},{9,11},{10,... | collective-permute-start | bytes 405512 | tf_op jit(solution)/shard_map/ppermute | solution.py:695
  195.6 7.6 %collective-permute-start.34 = (bf16[1,16,4224]{2,1,0:T(8,128)(2,1)S(1)}, bf16[1,16,4224]{2,1,0:T(8,128)(2,1)S(1)}, u32[]{:S(2)}, u32[]{:S(2)}) collective-permute-start(bf16[1,16,4224]{2,1,0:T(8,128)(2,1)S(1)} %get-tuple-element.194.refs_0_), channel_id=1, source_target_pairs={{0,1},{1,0},{2,3},{3,2},{4,5},{5,4},{6,7},{7,6},{8,9},{9,8},{10,11... | collective-permute-start | bytes 405512 | tf_op jit(solution)/shard_map/ppermute | solution.py:695
  203.3 13.7 %collective-permute-start.40 = (bf16[4,16,2176]{2,1,0:T(8,128)(2,1)S(1)}, bf16[4,16,2176]{2,1,0:T(8,128)(2,1)S(1)}, u32[]{:S(2)}, u32[]{:S(2)}) collective-permute-start(bf16[4,16,2176]{2,1,0:T(8,128)(2,1)S(1)} %get-tuple-element.198.refs_2_), channel_id=1, source_target_pairs={{0,8},{4,12},{8,0},{12,4},{16,24},{20,28},{24,16},{28,20},{1,9},{5... | collective-permute-start | bytes 835592 | tf_op jit(solution)/shard_map/ppermute | solution.py:695
  203.9 5.0 %collective-permute-start.41 = (bf16[256,512]{1,0:T(8,128)(2,1)S(1)}, bf16[256,512]{1,0:T(8,128)(2,1)S(1)}, u32[]{:S(2)}, u32[]{:S(2)}) collective-permute-start(bf16[256,512]{1,0:T(8,128)(2,1)S(1)} %get-tuple-element.202), channel_id=1, source_target_pairs={{2,1},{3,2},{6,5},{7,6},{10,9},{11,10},{14,13},{15,14},{18,17},{19... | collective-permute-start | bytes 786440 | tf_op jit(solution)/shard_map/ppermute | solution.py:653
  204.6 9.6 %collective-permute-start.42 = (bf16[256,512]{1,0:T(8,128)(2,1)S(1)}, bf16[256,512]{1,0:T(8,128)(2,1)S(1)}, u32[]{:S(2)}, u32[]{:S(2)}) collective-permute-start(bf16[256,512]{1,0:T(8,128)(2,1)S(1)} %get-tuple-element.203.refs_8_), channel_id=1, source_target_pairs={{1,0},{3,2},{5,4},{7,6},{9,8},{11,10},{13,12},{15,14},{17,16},{19,... | collective-permute-start | bytes 786440 | tf_op jit(solution)/shard_map/ppermute | solution.py:658
  205.9 11.1 %collective-permute-start.43 = (bf16[256,512]{1,0:T(8,128)(2,1)S(1)}, bf16[256,512]{1,0:T(8,128)(2,1)S(1)}, u32[]{:S(2)}, u32[]{:S(2)}) collective-permute-start(bf16[256,512]{1,0:T(8,128)(2,1)S(1)} %get-tuple-element.204.refs_11_), channel_id=1, source_target_pairs={{2,0},{6,4},{10,8},{14,12},{18,16},{22,20},{26,24},{30,28}} | collective-permute-start | bytes 786440 | tf_op jit(solution)/shard_map/ppermute | solution.py:658
  207.2 9.8 %collective-permute-start.39 = (bf16[4,16,2048]{2,1,0:T(8,128)(2,1)S(1)}, bf16[4,16,2048]{2,1,0:T(8,128)(2,1)S(1)}, u32[]{:S(2)}, u32[]{:S(2)}) collective-permute-start(bf16[4,16,2048]{2,1,0:T(8,128)(2,1)S(1)} %get-tuple-element.197.refs_0_), channel_id=1, source_target_pairs={{0,16},{4,20},{8,24},{12,28},{16,0},{20,4},{24,8},{28,12},{1,17},{... | collective-permute-start | bytes 786440 | tf_op jit(solution)/shard_map/ppermute | solution.py:695
  217.3 5.1 %collective-permute-start.47 = (bf16[16,16,4096]{2,1,0:T(8,128)(2,1)S(1)}, bf16[16,16,4096]{2,1,0:T(8,128)(2,1)S(1)}, u32[]{:S(2)}, u32[]{:S(2)}) collective-permute-start(bf16[16,16,4096]{2,1,0:T(8,128)(2,1)S(1)} %get-tuple-element.210.refs_0_), channel_id=1, source_target_pairs={{0,4},{4,0},{8,12},{12,8},{16,20},{20,16},{24,28},{28,24},{1,5},{5... | collective-permute-start | bytes 6291464 | tf_op jit(solution)/shard_map/ppermute | solution.py:695
  217.3 16.7 %collective-permute-start.45 = (bf16[8,16,2048]{2,1,0:T(8,128)(2,1)S(1)}, bf16[8,16,2048]{2,1,0:T(8,128)(2,1)S(1)}, u32[]{:S(2)}, u32[]{:S(2)}) collective-permute-start(bf16[8,16,2048]{2,1,0:T(8,128)(2,1)S(1)} %get-tuple-element.207.refs_0_), channel_id=1, source_target_pairs={{0,8},{4,12},{8,0},{12,4},{16,24},{20,28},{24,16},{28,20},{1,9},{5... | collective-permute-start | bytes 1572872 | tf_op jit(solution)/shard_map/ppermute | solution.py:695
  218.1 15.9 %collective-permute-start.44 = (bf16[256,512]{1,0:T(8,128)(2,1)S(1)}, bf16[256,512]{1,0:T(8,128)(2,1)S(1)}, u32[]{:S(2)}, u32[]{:S(2)}) collective-permute-start(bf16[256,512]{1,0:T(8,128)(2,1)S(1)} %get-tuple-element.205), channel_id=1, source_target_pairs={{1,0},{2,1},{3,2},{5,4},{6,5},{7,6},{9,8},{10,9},{11,10},{13,12},{... | collective-permute-start | bytes 786440 | tf_op jit(solution)/shard_map/ppermute | solution.py:653
  219.4 14.6 %collective-permute-start.48 = (bf16[256,512]{1,0:T(8,128)(2,1)S(1)}, bf16[256,512]{1,0:T(8,128)(2,1)S(1)}, u32[]{:S(2)}, u32[]{:S(2)}) collective-permute-start(bf16[256,512]{1,0:T(8,128)(2,1)S(1)} %get-tuple-element.212.refs_7_), channel_id=1, source_target_pairs={{2,0},{6,4},{10,8},{14,12},{18,16},{22,20},{26,24},{30,28}} | collective-permute-start | bytes 786440 | tf_op jit(solution)/shard_map/ppermute | solution.py:658
  220.7 14.8 %collective-permute-start.46 = (bf16[8,16,2176]{2,1,0:T(8,128)(2,1)S(1)}, bf16[8,16,2176]{2,1,0:T(8,128)(2,1)S(1)}, u32[]{:S(2)}, u32[]{:S(2)}) collective-permute-start(bf16[8,16,2176]{2,1,0:T(8,128)(2,1)S(1)} %get-tuple-element.208.refs_2_), channel_id=1, source_target_pairs={{0,16},{4,20},{8,24},{12,28},{16,0},{20,4},{24,8},{28,12},{1,17},{... | collective-permute-start | bytes 1671176 | tf_op jit(solution)/shard_map/ppermute | solution.py:695
  (21 other events, 419.5 us)
